TPU v7x, 128 devices: a whole 4x4x4 slice. The times are simulated.
128 devices in a mesh: replica: 16 (over x_hi, y, core), tensor: 8 (over z, x_lo).
Axes of the slice: x: 4 (x_hi: 2, x_lo: 2; x = x_hi * 2 + x_lo), y: 4, z: 4, core: 2. Of those that a mesh axis runs over, the one named last changes fastest.
Arguments:
- queries: bfloat16 [16, 128, 2, 8192], P('replica', None, None, 'tensor'), may hold values from -110 to 110
- step_key_value: bfloat16 [16, 128, 2, 2, 1024], P('replica', None, None, None, 'tensor'), may hold values from -4.1 to 4.1
- replica_page_store: bfloat16 [16, 2, 128, 64, 1024], P('replica', None, None, None, 'tensor'), may hold values from -4 to 4
- page_table: int32 [16, 128, 16], P('replica'), may hold values from 0 to 127
- lengths: int32 [16, 128], P('replica'), may hold values from 1 to 1024, 81920 in all within a row
- mig_offset: int32 [16, 14, 1], P('replica'), may hold values from 0 to 14; in each aligned block of 14 rows (0 to 13, 14 to 27, ..., all dimensions but the last counted through in order) at most 2 rows name the same one
- copy_order: int32 [16, 14, 16], P('replica'), may hold values from 0 to 15, each once within a row
- out_weight: bfloat16 [8192, 8192], P('tensor'), may hold values from -0.0625 to 0.0625
Outputs:
- attention: bfloat16 [16, 128, 2, 8192], P('replica', None, None, 'tensor')
- projected: bfloat16 [16, 128, 2, 8192], P('replica', 'tensor')
- arrived: bfloat16 [16, 14, 4, 2, 64, 1024], P('replica', None, None, None, None, 'tensor')
Inputs may be any that keep to these rules, and one draw needn't show every extreme that they name: Row 114 + j of replica r arrived from replica (r + 1 + mig_offset[r, j, 0]) mod 16; at most 2 of one replica's arriving rows come from one source. `page_table`: entries name pages of the pool of the row's home replica; pages may be shared. `lengths`: each replica has a row of exactly 1024 tokens. `copy_order`: each row is an ordering of its 16 pages.
All inputs are finite; a program needn't handle non-finite values.
Results may differ from a plain program's by a relative error of at most 0.019.
Values may be sent and summed in bfloat16 or wider, within the bound.
No kernel may reach another device: no remote copies, remote signals or barrier semaphores. Data moves between devices by JAX's collectives and lax.ppermute only.
A program may use at most 384 MiB of HBM per device.

v0:
```python
import math

import jax
import jax.numpy as jnp
from jax import lax
from jax.sharding import PartitionSpec as P

HEAD_SIZE = 128
MIGRANTS = 14
COPIED = 4


NEG_FILL = -1e30


def attend(query_head_vectors, keys_in, values_in, allowed):
    scores = jnp.einsum(
        "nsgjd,nkgd->nsgjk", query_head_vectors, keys_in, preferred_element_type=jnp.float32
    )
    scores = scores / math.sqrt(query_head_vectors.shape[-1])
    wide_mask = allowed[:, :, None, None, :]
    masked = jnp.where(wide_mask, scores, NEG_FILL)
    highest = jnp.max(masked, axis=-1)
    weights = jnp.where(wide_mask, jnp.exp(masked - highest[..., None]), 0.0).astype(jnp.bfloat16)
    total = jnp.sum(weights.astype(jnp.float32), axis=-1)
    weighted = jnp.einsum(
        "nsgjk,nkgd->nsgjd", weights, values_in, preferred_element_type=jnp.float32
    )
    return (highest, total, weighted)


def merge_parts(first, second):
    highest = jnp.maximum(first[0], second[0])
    scale_first = jnp.exp(first[0] - highest)
    scale_second = jnp.exp(second[0] - highest)
    total = first[1] * scale_first + second[1] * scale_second
    weighted = first[2] * scale_first[..., None] + second[2] * scale_second[..., None]
    return (highest, total, weighted)


def page_rows(pages_local, page_ids, kv_heads):
    selected_pages = jnp.take(pages_local, page_ids, axis=1)
    shape_out = page_ids.shape[:-1] + (
        page_ids.shape[-1] * pages_local.shape[2],
        kv_heads,
        HEAD_SIZE,
    )
    return (selected_pages[0].reshape(shape_out), selected_pages[1].reshape(shape_out))


def page_positions(logical, page_len):
    offsets = lax.broadcasted_iota(jnp.int32, logical.shape + (page_len,), logical.ndim)
    return (logical[..., None] * page_len + offsets).reshape(logical.shape[:-1] + (-1,))


def visible(position, limit):
    seen_once = position < limit[:, None]
    return jnp.broadcast_to(seen_once[:, None, :], (seen_once.shape[0], 2, seen_once.shape[1]))


def pick_slots(received, slot_of):
    count = received.shape[0] * received.shape[1]
    return received.reshape((count,) + received.shape[2:])[slot_of]


def outgoing_pages(pages_local, got_table, logical):
    page_ids = jnp.take_along_axis(got_table, logical, axis=2)
    return jnp.moveaxis(jnp.take(pages_local, page_ids, axis=1), 0, 3)


def body(
    queries,
    step_key_value,
    replica_page_store,
    page_table,
    lengths,
    mig_offset,
    copy_order,
    out_weight,
):
    replicas = lax.axis_size("replica")
    own_index = lax.axis_index("replica")
    capacity = max(2, (MIGRANTS + replicas - 2) // (replicas - 1))
    row_count = queries.shape[1]
    kv_heads = step_key_value.shape[-1] // HEAD_SIZE
    query_group_size = queries.shape[-1] // HEAD_SIZE // kv_heads
    staying = row_count - MIGRANTS
    page_len = replica_page_store.shape[3]
    pages_local = replica_page_store[0]
    row_table = page_table[0]
    row_length = lengths[0]
    query_head_vectors = queries[0].reshape(row_count, 2, kv_heads, query_group_size, HEAD_SIZE)
    fresh_token = step_key_value[0].reshape(row_count, 2, 2, kv_heads, HEAD_SIZE)
    causal = lax.broadcasted_iota(jnp.int32, (2, 2), 1) <= lax.broadcasted_iota(
        jnp.int32, (2, 2), 0
    )
    fresh_part = attend(
        query_head_vectors,
        fresh_token[:, :, 0],
        fresh_token[:, :, 1],
        jnp.broadcast_to(causal, (row_count, 2, 2)),
    )
    source_of = (own_index + 1 + mig_offset[0, :, 0]) % replicas
    earlier = lax.broadcasted_iota(jnp.int32, (MIGRANTS, MIGRANTS), 0) > lax.broadcasted_iota(
        jnp.int32, (MIGRANTS, MIGRANTS), 1
    )
    same_source = source_of[:, None] == source_of[None, :]
    slot_rank = jnp.sum(jnp.where(earlier & same_source, 1, 0), axis=1)
    slot_of = source_of * capacity + slot_rank
    placing = (
        lax.broadcasted_iota(jnp.int32, (replicas * capacity, MIGRANTS), 0) == slot_of[None, :]
    )
    mig_table = row_table[staying:]
    mig_order = copy_order[0]
    mig_length = row_length[staying:]
    send_table = jnp.sum(jnp.where(placing[:, :, None], mig_table[None], 0), axis=1).reshape(
        replicas, capacity, -1
    )
    send_order = jnp.sum(jnp.where(placing[:, :, None], mig_order[None], 0), axis=1).reshape(
        replicas, capacity, -1
    )
    send_length = jnp.sum(jnp.where(placing, mig_length[None], 0), axis=1).reshape(
        replicas, capacity, 1
    )
    got_table, got_order, got_length = (
        lax.all_to_all(send_table, "replica", split_axis=0, concat_axis=0, tiled=True),
        lax.all_to_all(send_order, "replica", split_axis=0, concat_axis=0, tiled=True),
        lax.all_to_all(send_length, "replica", split_axis=0, concat_axis=0, tiled=True),
    )
    cached_page_keys, cached_page_values = page_rows(pages_local, row_table[:staying], kv_heads)
    context_length = lax.broadcasted_iota(jnp.int32, (staying, cached_page_keys.shape[1]), 1)
    staying_part = attend(
        query_head_vectors[:staying],
        cached_page_keys,
        cached_page_values,
        visible(context_length, row_length[:staying]),
    )
    staying_part = merge_parts(staying_part, tuple((member[:staying] for member in fresh_part)))
    mig_queries = query_head_vectors[staying:]
    mig_fresh = tuple((member[staying:] for member in fresh_part))
    sending = outgoing_pages(pages_local, got_table, got_order)
    incoming = lax.all_to_all(sending, "replica", split_axis=0, concat_axis=0, tiled=True)
    own_pages = pick_slots(incoming, slot_of)
    arrived = own_pages[:, :COPIED]
    moved_keys = own_pages[:, :, 0].reshape(MIGRANTS, -1, kv_heads, HEAD_SIZE)
    moved_values = own_pages[:, :, 1].reshape(MIGRANTS, -1, kv_heads, HEAD_SIZE)
    moved_position = page_positions(mig_order, page_len)
    mig_part = attend(mig_queries, moved_keys, moved_values, visible(moved_position, mig_length))
    mig_part = merge_parts(mig_part, mig_fresh)
    total = jnp.concatenate([staying_part[1], mig_part[1]], axis=0)
    weighted = jnp.concatenate([staying_part[2], mig_part[2]], axis=0)
    attention = (weighted / total[..., None]).astype(jnp.bfloat16).reshape(row_count, 2, -1)
    product = jnp.dot(
        attention.reshape(row_count // lax.axis_size("tensor") * lax.axis_size("tensor") * 2, -1),
        out_weight,
        preferred_element_type=jnp.float32,
    )
    projected = lax.psum_scatter(
        product.reshape(
            row_count // lax.axis_size("tensor") * lax.axis_size("tensor"), 2, -1
        ).astype(jnp.bfloat16),
        "tensor",
        scatter_dimension=0,
        tiled=True,
    )
    return (attention[None], projected[None], arrived[None])


def solution(mesh):
    placed = (
        P("replica", None, None, "tensor"),
        P("replica", None, None, None, "tensor"),
        P("replica", None, None, None, "tensor"),
        P("replica", None, None),
        P("replica", None),
        P("replica", None, None),
        P("replica", None, None),
        P("tensor", None),
    )
    return jax.shard_map(
        body,
        mesh=mesh,
        in_specs=placed,
        out_specs=(
            P("replica", None, None, "tensor"),
            P("replica", "tensor", None, None),
            P("replica", None, None, None, None, "tensor"),
        ),
        check_vma=False,
    )
```

profile of v0, /device:TPU:10, one launch (start us, length us, event | category | flops | bytes accessed | tf_op | source)
XLA Modules:
  0.0 485.6 jit_solution(14092970569013270735)
XLA Ops:
  7.2 0.7 and_select_fusion.2
  8.0 0.7 multiply_add_fusion
  8.8 0.7 copy.104
  9.5 0.8 slice_bitcast_fusion.5
  10.5 0.7 copy.76
  11.1 6.5 %all-to-all-start = ((s32[16,2,16]{2,1,0:T(2,128)}), s32[16,2,16]{2,1,0:T(2,128)S(1)}, u32[]{:S(2)}, u32[]{:S(2)}) async-start(s32[16,2,16]{2,1,0:T(2,128)} %bitcast.31), calls=%async_computation | async-start | bytes 32768 | tf_op jit(solution)/shard_map/all_to_all | solution.py:127
  17.6 0.7 broadcast_multiply_fusion
  18.3 0.7 compare_select_fusion.2
  19.0 0.7 slice_bitcast_fusion.7
  19.8 1.0 copy.103
  20.8 1.4 reshape.380
  22.2 2.5 fusion.59
  24.6 0.6 convert_reduce_fusion.2
  25.3 0.7 compare_and_fusion.1
  26.0 0.9 slice.86
  26.8 1.3 slice.77
  28.2 0.7 iota.54
  29.0 0.7 copy.78
  29.9 0.7 reshape.389
  30.6 0.7 add.175
  31.7 7.2 %all-to-all-start.1 = ((s32[16,2,16]{2,1,0:T(2,128)}), s32[16,2,16]{2,1,0:T(2,128)S(1)}, u32[]{:S(2)}, u32[]{:S(2)}) async-start(s32[16,2,16]{2,1,0:T(2,128)} %bitcast.33), calls=%async_computation.1 | async-start | bytes 32768 | tf_op jit(solution)/shard_map/all_to_all | solution.py:126
  39.0 6.1 %all-to-all-done.1 = s32[16,2,16]{2,1,0:T(2,128)S(1)} async-done(((s32[16,2,16]{2,1,0:T(2,128)}), s32[16,2,16]{2,1,0:T(2,128)S(1)}, u32[]{:S(2)}, u32[]{:S(2)}) %all-to-all-start.1) | async-done | bytes 2080 | tf_op jit(solution)/shard_map/all_to_all | solution.py:126
  45.1 5.2 %gather_fusion.3 = s32[512]{0:T(512)S(1)} fusion(s32[16,2,16]{2,1,0:T(2,128)S(1)} %all-to-all-done.1, s32[512]{0:T(512)S(1)} %reshape.415), kind=kCustom, calls=%fused_computation.3 | custom fusion | bytes 10240 | tf_op jit(solution)/shard_map/jit(take_along_axis)/gather | solution.py:67
  50.5 15.5 %gather_fusion.1 = bf16[512,2,64,128]{3,2,1,0:T(8,128)(2,1)} fusion(bf16[2,128,64,128]{3,2,1,0:T(8,128)(2,1)} %bitcast.211, s32[1024]{0:T(1024)S(1)} %pad_clamp_fusion.2), kind=kCustom, calls=%fused_computation.1 | custom fusion | bytes 33556480 | tf_op jit(solution)/shard_map/jit(_take)/gather | solution.py:68
  66.1 14.2 %broadcast_select_fusion = bf16[16,2,16,2,64,128]{5,4,3,2,1,0:T(8,128)(2,1)} fusion(bf16[16,2,16,2,64,128]{5,4,3,2,1,0:T(8,128)(2,1)} %bitcast.215, pred[16,2,16]{2,1,0:T(4,128)(4,1)S(1)} %get-tuple-element.31), kind=kLoop, calls=%fused_computation.8 | loop fusion | flops 8388608 | bytes 33554944 | tf_op jit(solution)/shard_map/jit(_take)/select_n | solution.py:68
  80.2 6.4 %all-to-all-start.2 = ((bf16[16,2,16,2,64,128]{5,4,3,2,1,0:T(8,128)(2,1)}), bf16[16,2,16,2,64,128]{5,4,3,2,1,0:T(8,128)(2,1)}, u32[]{:S(2)}, u32[]{:S(2)}) async-start(bf16[16,2,16,2,64,128]{5,4,3,2,1,0:T(8,128)(2,1)} %broadcast_select_fusion), calls=%async_computation.2 | async-start | bytes 33554432 | tf_op jit(solution)/shard_map/all_to_all | solution.py:142
  86.9 44.2 %gather_fusion = bf16[1824,2,64,128]{3,2,1,0:T(8,128)(2,1)} fusion(bf16[2,128,64,128]{3,2,1,0:T(8,128)(2,1)} %bitcast.212, s32[2048]{0:T(1024)S(1)} %pad_clamp_fusion), kind=kCustom, calls=%fused_computation | custom fusion | bytes 119544960 | tf_op jit(solution)/shard_map/jit(_take)/gather | solution.py:42
  131.1 39.3 %fusion = bf16[2,114,16,64,128]{4,3,2,1,0:T(8,128)(2,1)} fusion(bf16[114,16,2,64,128]{4,3,2,1,0:T(8,128)(2,1)} %bitcast.213, pred[114,16]{1,0:T(8,128)(4,1)S(1)} %copy.72), kind=kLoop, calls=%fused_computation.5 | loop fusion | flops 29884416 | bytes 119539488 | tf_op jit(solution)/shard_map/jit(_take)/select_n | solution.py:42
  170.4 40.3 %fusion.57 = (bf16[1,114,16,64,128]{4,3,2,1,0:T(8,128)(2,1)}, bf16[1,114,16,64,128]{4,3,2,1,0:T(8,128)(2,1)}) fusion(bf16[2,114,16,64,128]{4,3,2,1,0:T(8,128)(2,1)} %fusion), kind=kLoop, calls=%fused_computation.106 | loop fusion | bytes 119537664 | tf_op jit(solution)/shard_map/slice | solution.py:48
  210.7 13.3 %bitcast_reduce_fusion = (f32[114,2,8]{2,1,0:T(2,128)S(1)}, f32[114,1024,2,8]{1,3,2,0:T(8,128)S(1)}) fusion(pred[114,1024]{1,0:T(8,128)(4,1)S(1)} %iota_compare_fusion, bf16[114,1024,128,1]{2,1,3,0:T(8,128)(2,1)} %bitcast.214, bf16[114,2,8,128]{3,2,1,0:T(8,128)(2,1)S(1)} %reshape.377), kind=kOutput, calls=%fused_computation.11 | convolution fusion | flops 483752160 | bytes 37946496 | tf_op jit(solution)/shard_map/nsgjd,nkgd->nsgjk/dot_general | solution.py:17
  224.1 3.0 copy-done
  227.1 3.1 convert_reduce_fusion
  230.8 13.9 %fusion.21 = f32[114,2,1,8,128]{4,3,1,0,2:T(8,128)S(1)} fusion(bf16[114,1024,128,1]{2,1,3,0:T(8,128)(2,1)} %bitcast.216, f32[128,2,1,8,128]{4,3,1,0,2:T(8,128)S(1)} %convolution_bitcast_fusion, f32[114,2,8]{2,1,0:T(2,128)S(1)} %get-tuple-element.25, f32[114,2,8]{2,1,0:T(2,128)S(1)} %get-tuple-element.24, f32[114,1024,2,8]{1,3,2,0:T(8,128)} %copy-done, ...), kind=kOutput, calls=%fused_computation.26 | convolution fusion | flops 488189952 | bytes 39819264 | tf_op jit(solution)/shard_map/nsgjk,nkgd->nsgjd/dot_general | solution.py:26
  244.8 0.5 concatenate.30
  245.3 1.2 copy.82
  246.7 97.1 %all-to-all-done.2 = bf16[16,2,16,2,64,128]{5,4,3,2,1,0:T(8,128)(2,1)} async-done(((bf16[16,2,16,2,64,128]{5,4,3,2,1,0:T(8,128)(2,1)}), bf16[16,2,16,2,64,128]{5,4,3,2,1,0:T(8,128)(2,1)}, u32[]{:S(2)}, u32[]{:S(2)}) %all-to-all-start.2) | async-done | bytes 16777248 | tf_op jit(solution)/shard_map/all_to_all | solution.py:142
  343.8 10.3 %gather_fusion.2 = bf16[14,16,2,64,128]{4,3,2,1,0:T(8,128)(2,1)} fusion(bf16[32,16,2,64,128]{4,3,2,1,0:T(8,128)(2,1)} %bitcast.36, s32[1024]{0:T(1024)S(1)} %pad_clamp_fusion.1), kind=kCustom, calls=%fused_computation.2 | custom fusion | bytes 14680120 | tf_op jit(solution)/shard_map/gather | solution.py:63
  354.1 7.1 %fusion.58 = (bf16[14,16,1,64,128]{4,3,2,1,0:T(8,128)(2,1)}, bf16[14,16,1,64,128]{4,3,2,1,0:T(8,128)(2,1)S(1)}) fusion(bf16[14,16,2,64,128]{4,3,2,1,0:T(8,128)(2,1)} %gather_fusion.2), kind=kLoop, calls=%fused_computation.107 | loop fusion | bytes 14680064 | tf_op jit(solution)/shard_map/slice | solution.py:146
  361.2 1.2 fusion.60
  362.9 2.7 fusion.29
  366.3 0.5 reshape.436
  366.8 12.9 %fusion.3 = bf16[128,2,8192]{2,0,1:T(8,128)(2,1)} fusion(bf16[1024,8192]{1,0:T(8,128)(2,1)} %param.15, f32[14,2,1024]{2,0,1:T(8,128)S(1)} %copy.83, f32[114,2,1024]{2,0,1:T(8,128)} %copy.82, f32[128,2,1024]{2,1,0:T(2,128)S(1)} %reshape.436), kind=kOutput, calls=%fused_computation.9 | convolution fusion | flops 4297850880 | bytes 23068672 | tf_op jit(solution)/shard_map/dot_general | solution.py:153
  379.7 0.5 concatenate.26
  380.3 0.5 div.65
  380.8 3.0 slice_bitcast_fusion
  383.8 1.4 fusion.31
  385.3 91.1 %reduce-scatter.2.cloned.1.call-done = bf16[16,2,8192]{2,0,1:T(8,128)(2,1)} async-done(((bf16[128,2,8192]{2,0,1:T(8,128)(2,1)}), bf16[16,2,8192]{2,0,1:T(8,128)(2,1)}) %reduce-scatter.2.cloned.1.call-update) | async-done | bytes 524304 | tf_op jit(solution)/shard_map/reduce_scatter | solution.py:158
  476.4 2.4 copy.85
  (53 shorter events, 3.9 us)
Async XLA Ops:
  8.0 1.4 copy-start.5
  11.1 20.5 %all-to-all-start = ((s32[16,2,16]{2,1,0:T(2,128)}), s32[16,2,16]{2,1,0:T(2,128)S(1)}, u32[]{:S(2)}, u32[]{:S(2)}) async-start(s32[16,2,16]{2,1,0:T(2,128)} %bitcast.31), calls=%async_computation | async-start | bytes 32768 | tf_op jit(solution)/shard_map/all_to_all | solution.py:127
  31.7 13.5 %all-to-all-start.1 = ((s32[16,2,16]{2,1,0:T(2,128)}), s32[16,2,16]{2,1,0:T(2,128)S(1)}, u32[]{:S(2)}, u32[]{:S(2)}) async-start(s32[16,2,16]{2,1,0:T(2,128)} %bitcast.33), calls=%async_computation.1 | async-start | bytes 32768 | tf_op jit(solution)/shard_map/all_to_all | solution.py:126
  80.2 263.6 %all-to-all-start.2 = ((bf16[16,2,16,2,64,128]{5,4,3,2,1,0:T(8,128)(2,1)}), bf16[16,2,16,2,64,128]{5,4,3,2,1,0:T(8,128)(2,1)}, u32[]{:S(2)}, u32[]{:S(2)}) async-start(bf16[16,2,16,2,64,128]{5,4,3,2,1,0:T(8,128)(2,1)} %broadcast_select_fusion), calls=%async_computation.2 | async-start | bytes 33554432 | tf_op jit(solution)/shard_map/all_to_all | solution.py:142
  86.6 389.8 %reduce-scatter.2.cloned.1.call-start = ((), (), s32[]{:S(2)}) async-start(), calls=%async_computation.4 | async-start | bytes 4718592 | tf_op jit(solution)/shard_map/reduce_scatter | solution.py:158
  224.1 3.0 copy-start
  230.8 15.7 %copy-start.4 = (s32[1,14,1]{1,2,0:T(1,128)S(1)}, s32[1,14,1]{1,2,0:T(1,128)}, u32[]{:S(2)}) copy-start(s32[1,14,1]{1,2,0:T(1,128)} %param.13) | copy-start | bytes 172
  230.8 15.7 %copy-start.6 = (s32[14]{0:T(128)S(1)}, s32[14]{0:T(128)}, u32[]{:S(2)}) copy-start(s32[14]{0:T(128)} %copy-done.5) | copy-start | bytes 172
  230.8 15.7 %copy-start.7 = (s32[1,128]{1,0:T(1,128)S(1)}, s32[1,128]{1,0:T(1,128)}, u32[]{:S(2)}) copy-start(s32[1,128]{1,0:T(1,128)} %param.12) | copy-start | bytes 1540
  230.8 15.8 %copy-start.1 = (s32[14,1024]{1,0:T(8,128)S(1)}, s32[14,1024]{1,0:T(8,128)}, u32[]{:S(2)}) copy-start(s32[14,1024]{1,0:T(8,128)} %add.175) | copy-start | bytes 172036
  230.8 15.8 %copy-start.3 = (s32[1024]{0:T(1024)S(1)}, s32[1024]{0:T(1024)}, u32[]{:S(2)}) copy-start(s32[1024]{0:T(1024)} %iota.54) | copy-start | bytes 12292
  354.1 7.1 %copy-start.2 = (bf16[14,2,8,128]{3,2,1,0:T(8,128)(2,1)S(1)}, bf16[14,2,8,128]{3,2,1,0:T(8,128)(2,1)}, u32[]{:S(2)}) copy-start(bf16[14,2,8,128]{3,2,1,0:T(8,128)(2,1)} %reshape.389) | copy-start | bytes 172036
Sparse Core Ops, SparseCore 0:
  379.8 96.5 reduce-scatter.1
where the time goes:
time: 489 us; the launch traced here: 486 us
  waiting for transfers between devices  194 us (40%)
  local copies, waits for them, and re-layouts  146 us (30%)
  other arithmetic  63.4 us (13%)
  matrix products  46.8 us (10%)
  starting transfers between devices  20.4 us (4%)
  between operations  14.3 us (3%)
    all_to_all x1, waiting for transfers between devices, body(): lax.all_to_all(sending, 'replica', split_axis=0, concat_axis=0, tiled=True)  97.1 us
    reduce_scatter x1, waiting for transfers between devices, body(): lax.psum_scatter(product.reshape(row_count // lax.axis_size('tensor') * l...  91.1 us
    gather x1, local copies, waits for them, and re-layouts, page_rows(): selected_pages = jnp.take(pages_local, page_ids, axis=1)  44.2 us
    slice x1, local copies, waits for them, and re-layouts, page_rows(): selected_pages[1].reshape(shape_out)  40.3 us
    select_n x2, other arithmetic, page_rows(): selected_pages = jnp.take(pages_local, page_ids, axis=1)  40 us
    dot_general x3, matrix products, attend(): jnp.einsum('nsgjk,nkgd->nsgjd', weights, values_in, preferred_element_typ...  17 us
    dot_general x3, matrix products, attend(): jnp.einsum('nsgjd,nkgd->nsgjk', query_head_vectors, keys_in, preferred_el...  16.9 us
    gather x1, local copies, waits for them, and re-layouts, outgoing_pages(): return jnp.moveaxis(jnp.take(pages_local, page_ids, axis=1), 0, 3)  15.5 us
  transfers between devices with their start and end apart: 4, of which 3 were waited for; matrix products, arithmetic and copies ran while one was open for 36% of the time, Pallas kernels for 0%

commit v1 on v0

v1 whole, which is shorter than its diff:
```python
import functools
import math

import jax
import jax.numpy as jnp
from jax import lax
from jax.experimental import pallas as pl
from jax.experimental.pallas import tpu as pltpu
from jax.sharding import PartitionSpec as P

HEAD = 128
ROWS = 128
MIGRANTS = 14
STAYING = ROWS - MIGRANTS
COPIED = 4
PAGES_ROW = 16
PAGE = 64
REPLICAS = 16
CAP = 2
SLOTS = REPLICAS * CAP
GROUP = 8
CONTEXT = PAGES_ROW * PAGE
NEG_FILL = -1e30
SCALE = math.log2(math.e) / math.sqrt(HEAD)
META_ROW = 4
PIECES = 2
VMEM = pl.BlockSpec(memory_space=pltpu.VMEM)
SMEM = pl.BlockSpec(memory_space=pltpu.SMEM)
HBM = pl.BlockSpec(memory_space=pltpu.HBM)


def attend_group(queries, fresh, pages, lengths, pool_ref, scores_ref):
    nt = (((1,), (1,)), ((), ()))
    for i in range(GROUP):
        keys = jnp.concatenate([pool_ref[0, page] for page in pages[i]], axis=0)
        scores_ref[i, :, 0:CONTEXT] = lax.dot_general(
            queries[i], keys, nt, preferred_element_type=jnp.float32
        )
        scores_ref[i, :, CONTEXT : CONTEXT + 16] = lax.dot_general(
            queries[i], fresh[i], nt, preferred_element_type=jnp.float32
        )
    outputs = []
    for i in range(GROUP):
        scores = scores_ref[i, :, 0:CONTEXT]
        position = lax.broadcasted_iota(jnp.int32, scores.shape, 1)
        scores = jnp.where(position < lengths[i], scores, NEG_FILL)
        fresh_scores = scores_ref[i, :, CONTEXT : CONTEXT + 16]
        token = lax.broadcasted_iota(jnp.int32, fresh_scores.shape, 1)
        step = lax.broadcasted_iota(jnp.int32, fresh_scores.shape, 0) // 8
        fresh_scores = jnp.where(token <= step, fresh_scores, NEG_FILL)
        highest = jnp.maximum(
            jnp.max(scores, axis=1, keepdims=True), jnp.max(fresh_scores, axis=1, keepdims=True)
        )
        weights = jnp.exp2((scores - highest) * SCALE).astype(jnp.bfloat16)
        fresh_weights = jnp.exp2((fresh_scores - highest) * SCALE).astype(jnp.bfloat16)
        total = jnp.sum(weights.astype(jnp.float32), axis=1, keepdims=True) + jnp.sum(
            fresh_weights.astype(jnp.float32), axis=1, keepdims=True
        )
        values = jnp.concatenate([pool_ref[1, page] for page in pages[i]], axis=0)
        fresh_values = pltpu.roll(fresh[i].astype(jnp.float32), 14, 0).astype(jnp.bfloat16)
        weighted = jnp.dot(weights, values, preferred_element_type=jnp.float32) + jnp.dot(
            fresh_weights, fresh_values, preferred_element_type=jnp.float32
        )
        outputs.append(weighted / total)
    return outputs


def store_rows(out_ref, start, outputs):
    block = jnp.stack(outputs).reshape(16, 8, HEAD).swapaxes(0, 1).astype(jnp.bfloat16)
    for h in range(8):
        out_ref[pl.ds(start, 16), h * HEAD : (h + 1) * HEAD] = block[h]


def fetch_pool(pool_hbm, pool_ref, sem):
    copies = [
        pltpu.make_async_copy(pool_hbm.at[k, p : p + 32], pool_ref.at[k, p : p + 32], sem.at[k, p // 32])
        for k in range(2)
        for p in range(0, 128, 32)
    ]
    for copy in copies:
        copy.start()
    return copies


def stay_kernel(
    table_ref, length_ref, query_ref, fresh_ref, pool_hbm, after_ref, out_ref, pool_ref, scores_ref, sem, *, first
):
    for copy in fetch_pool(pool_hbm, pool_ref, sem):
        copy.wait()

    def group(g, carry):
        rows = [first + g * GROUP + i for i in range(GROUP)]
        outputs = attend_group(
            [query_ref[row] for row in rows],
            [fresh_ref[row] for row in rows],
            [[table_ref[0, row, p] for p in range(PAGES_ROW)] for row in rows],
            [length_ref[0, row] for row in rows],
            pool_ref,
            scores_ref,
        )
        store_rows(out_ref, pl.multiple_of(g * 16, 16), outputs)
        return carry

    lax.fori_loop(0, out_ref.shape[0] // (2 * GROUP), group, 0)


def stay(table, lengths, query, fresh, pool, after, first, count):
    return pl.pallas_call(
        functools.partial(stay_kernel, first=first),
        out_shape=jax.ShapeDtypeStruct((count * 2, 8 * HEAD), jnp.bfloat16),
        in_specs=[SMEM, SMEM, VMEM, VMEM, HBM, SMEM],
        out_specs=VMEM,
        scratch_shapes=[
            pltpu.VMEM(pool.shape, pool.dtype),
            pltpu.VMEM((GROUP, 16, CONTEXT + 128), jnp.float32),
            pltpu.SemaphoreType.DMA((2, 4)),
        ],
        compiler_params=pltpu.CompilerParams(vmem_limit_bytes=24 * 2**20),
        cost_estimate=pl.CostEstimate(flops=count * 10**8, bytes_accessed=8 * 2**20, transcendentals=0),
        name="attend_staying",
    )(table, lengths, query, fresh, pool, after)


def request_kernel(
    offset_ref, order_ref, table_ref, length_ref, query_ref, fresh_ref, out_ref, slot_ref, used
):
    own = lax.axis_index("replica")
    out_ref[...] = jnp.zeros_like(out_ref)
    for s in range(REPLICAS):
        used[s] = 0
    lane = lax.broadcasted_iota(jnp.int32, (1, HEAD), 1)
    line = lax.broadcasted_iota(jnp.int32, (16, HEAD), 0)
    for j in range(MIGRANTS):
        row = STAYING + j
        source = lax.rem(own + 1 + offset_ref[0, j, 0], REPLICAS)
        rank = used[source]
        used[source] = rank + 1
        slot = source * CAP + rank
        slot_ref[j] = slot
        meta = jnp.zeros((1, HEAD), jnp.int32)
        for p in range(PAGES_ROW):
            meta = jnp.where(lane == p, table_ref[0, row, p], meta)
        for c in range(COPIED):
            wanted = table_ref[0, row, order_ref[0, j, c]]
            meta = jnp.where(lane == PAGES_ROW + c, wanted, meta)
        length = length_ref[0, row]
        meta = jnp.where(lane == 20, length // 32, meta)
        meta = jnp.where(lane == 21, lax.rem(length, 32), meta)
        meta = meta.astype(jnp.float32)
        out_ref[slot, 0:16] = query_ref[row]
        out_ref[slot, 16:32] = jnp.where(
            line == META_ROW, meta, fresh_ref[row].astype(jnp.float32)
        ).astype(jnp.bfloat16)


def request(offsets, order, table, lengths, query, fresh):
    return pl.pallas_call(
        request_kernel,
        out_shape=(
            jax.ShapeDtypeStruct((SLOTS, 32, HEAD), jnp.bfloat16),
            jax.ShapeDtypeStruct((MIGRANTS,), jnp.int32),
        ),
        in_specs=[SMEM] * 4 + [VMEM] * 2,
        out_specs=(VMEM, SMEM),
        scratch_shapes=[pltpu.SMEM((REPLICAS,), jnp.int32)],
        name="pack_requests",
    )(offsets, order, table, lengths, query, fresh)


def serve_kernel(
    got_ref, pool_hbm, ret_ref, send_ref, pool_ref, scores_ref, meta_vmem, meta_ref, active, pool_sem, meta_sem, page_sem
):
    fetch = fetch_pool(pool_hbm, pool_ref, pool_sem)
    for slot in range(SLOTS):
        meta_vmem[slot : slot + 1] = got_ref[slot, 16:32].astype(jnp.float32)[META_ROW : META_ROW + 1].astype(jnp.int32)
    meta_copy = pltpu.make_async_copy(meta_vmem, meta_ref, meta_sem)
    meta_copy.start()
    ret_ref[...] = jnp.zeros_like(ret_ref)
    meta_copy.wait()
    for copy in fetch:
        copy.wait()

    def copies(slot, carry):
        for c in range(COPIED):
            page = meta_ref[slot, PAGES_ROW + c]
            pltpu.make_async_copy(pool_ref.at[:, page], send_ref.at[slot, c], page_sem).start()
        return carry

    lax.fori_loop(0, SLOTS, copies, 0)
    for i in range(SLOTS + GROUP):
        active[i] = 0

    def collect(slot, count):
        used = meta_ref[slot, 20] + meta_ref[slot, 21] > 0

        @pl.when(used)
        def _():
            active[count] = slot

        return count + jnp.where(used, 1, 0)

    count = lax.fori_loop(0, SLOTS, collect, 0)

    def group(g, carry):
        slots = [active[g * GROUP + i] for i in range(GROUP)]
        outputs = attend_group(
            [got_ref[slot, 0:16] for slot in slots],
            [got_ref[slot, 16:32] for slot in slots],
            [[meta_ref[slot, p] for p in range(PAGES_ROW)] for slot in slots],
            [meta_ref[slot, 20] * 32 + meta_ref[slot, 21] for slot in slots],
            pool_ref,
            scores_ref,
        )
        for slot, output in zip(slots, outputs):
            ret_ref[slot] = output.astype(jnp.bfloat16)
        return carry

    lax.fori_loop(0, (count + GROUP - 1) // GROUP, group, 0)
    pltpu.make_async_copy(send_ref, send_ref, page_sem).wait()


def serve(got, pool):
    return pl.pallas_call(
        serve_kernel,
        out_shape=(
            jax.ShapeDtypeStruct((SLOTS, 16, HEAD), jnp.bfloat16),
            jax.ShapeDtypeStruct((SLOTS, COPIED, 2, PAGE, HEAD), jnp.bfloat16),
        ),
        in_specs=[VMEM, HBM],
        out_specs=(VMEM, HBM),
        scratch_shapes=[
            pltpu.VMEM(pool.shape, pool.dtype),
            pltpu.VMEM((GROUP, 16, CONTEXT + 128), jnp.float32),
            pltpu.VMEM((SLOTS, HEAD), jnp.int32),
            pltpu.SMEM((SLOTS, HEAD), jnp.int32),
            pltpu.SMEM((SLOTS + GROUP,), jnp.int32),
            pltpu.SemaphoreType.DMA((2, 4)),
            pltpu.SemaphoreType.DMA,
            pltpu.SemaphoreType.DMA,
        ],
        compiler_params=pltpu.CompilerParams(vmem_limit_bytes=24 * 2**20),
        cost_estimate=pl.CostEstimate(flops=4 * 10**9, bytes_accessed=8 * 2**20, transcendentals=0),
        name="serve_requests",
    )(got, pool)


def merge_kernel(slot_ref, first_ref, second_ref, ret_ref, out_ref):
    out_ref[0:128] = first_ref[...]
    out_ref[128:240] = second_ref[...]
    here = [ret_ref[slot_ref[j]].astype(jnp.float32) for j in range(MIGRANTS)]
    store_rows(out_ref, 240, here[6:])
    store_rows(out_ref, 224, here[:2] + here[:6])
    out_ref[224:228] = second_ref[96:100]


def merge(slots, first, second, returned):
    return pl.pallas_call(
        merge_kernel,
        out_shape=jax.ShapeDtypeStruct((ROWS * 2, 8 * HEAD), jnp.bfloat16),
        in_specs=[SMEM, VMEM, VMEM, VMEM],
        out_specs=VMEM,
        name="merge_rows",
    )(slots, first, second, returned)


def pick_kernel(slot_ref, got_ref, out_ref, held, in_sem, out_sem):
    loads = [
        pltpu.make_async_copy(got_ref.at[slot_ref[j]], held.at[j], in_sem.at[j]) for j in range(MIGRANTS)
    ]
    stores = [pltpu.make_async_copy(held.at[j], out_ref.at[j], out_sem.at[j]) for j in range(MIGRANTS)]
    for load in loads:
        load.start()
    for load, store in zip(loads, stores):
        load.wait()
        store.start()
    for store in stores:
        store.wait()


def pick(slots, got):
    shape = (MIGRANTS, COPIED, 2, PAGE, HEAD)
    return pl.pallas_call(
        pick_kernel,
        out_shape=jax.ShapeDtypeStruct(shape, jnp.bfloat16),
        in_specs=[SMEM, HBM],
        out_specs=HBM,
        scratch_shapes=[
            pltpu.VMEM(shape, jnp.bfloat16),
            pltpu.SemaphoreType.DMA((MIGRANTS,)),
            pltpu.SemaphoreType.DMA((MIGRANTS,)),
        ],
        name="pick_pages",
    )(slots, got)


def project_kernel(*refs, starts):
    row_refs, (weight_ref, own_ref, up_ref, far_ref, down_ref, rolled) = refs[:-6], refs[-6:]

    @pl.when(pl.program_id(0) == 0)
    def _():
        zi = lax.axis_index("tensor") // 2
        for z, (which, start) in enumerate(starts):
            place = lax.rem(z - zi + 4, 4) * 32
            rolled[pl.ds(pl.multiple_of(place, 32), 32)] = row_refs[which][start : start + 32]

    product = jnp.dot(rolled[...], weight_ref[...], preferred_element_type=jnp.float32)
    product = product.astype(jnp.bfloat16)
    for k, ref in enumerate((own_ref, up_ref, far_ref, down_ref)):
        ref[...] = product[32 * k : 32 * k + 32]


def project(rows, starts, weight, piece, width):
    tile = 512
    steps = width // tile
    depth = weight.shape[0]
    return pl.pallas_call(
        functools.partial(project_kernel, starts=starts),
        out_shape=[jax.ShapeDtypeStruct((32, width), jnp.bfloat16)] * 4,
        grid=(steps,),
        in_specs=[pl.BlockSpec(r.shape, lambda i: (0, 0)) for r in rows]
        + [pl.BlockSpec((depth, tile), lambda i: (0, piece * steps + i))],
        out_specs=[pl.BlockSpec((32, tile), lambda i: (0, i))] * 4,
        scratch_shapes=[pltpu.VMEM((128, depth), jnp.bfloat16)],
        compiler_params=pltpu.CompilerParams(vmem_limit_bytes=56 * 2**20),
        cost_estimate=pl.CostEstimate(
            flops=2 * 256 * depth * width, bytes_accessed=2 * depth * width, transcendentals=0
        ),
        name="project_piece",
    )(*rows, weight)


def shift_z(value, by):
    pairs = [(z * 2 + x, (z + by) % 4 * 2 + x) for z in range(4) for x in range(2)]
    return lax.ppermute(value, "tensor", pairs)


def send_x(value, to):
    return lax.ppermute(value, "tensor", [(2 * z + 1 - to, 2 * z + to) for z in range(4)])


def f32_sum(*terms):
    return functools.reduce(jnp.add, [term.astype(jnp.float32) for term in terms])


def reduce_z(rows, starts, weight, piece, width):
    here, up, far, down = project(rows, starts, weight, piece, width)
    if piece % 2 == 0:
        up = f32_sum(up, shift_z(far, 1)).astype(jnp.bfloat16)
    else:
        down = f32_sum(down, shift_z(far, -1)).astype(jnp.bfloat16)
    return f32_sum(here, shift_z(up, 1), shift_z(down, -1))


def body(
    queries,
    step_key_value,
    replica_page_store,
    page_table,
    lengths,
    mig_offset,
    copy_order,
    out_weight,
):
    xi = lax.axis_index("tensor") % 2
    pool = replica_page_store[0]
    query = queries[0].reshape(ROWS, 16, HEAD)
    fresh = step_key_value[0]
    fresh = jnp.concatenate(
        [fresh[:, :, 0], fresh[:, :, 1], jnp.zeros((ROWS, 12, HEAD), jnp.bfloat16)], axis=1
    )
    payload, slots = request(mig_offset, copy_order, page_table, lengths, query, fresh)
    got = lax.all_to_all(
        payload.reshape(REPLICAS, CAP, 32, HEAD), "replica", split_axis=0, concat_axis=0, tiled=True
    ).reshape(SLOTS, 32, HEAD)
    first = stay(page_table, lengths, query, fresh, pool, slots, 0, 64)
    answered, sending = serve(got, pool)
    returned = lax.all_to_all(
        answered.reshape(REPLICAS, CAP, 16, HEAD), "replica", split_axis=0, concat_axis=0, tiled=True
    ).reshape(SLOTS, 16, HEAD)
    incoming = lax.all_to_all(
        sending.reshape(REPLICAS, CAP, COPIED, 2, PAGE, HEAD),
        "replica",
        split_axis=0,
        concat_axis=0,
        tiled=True,
    ).reshape(SLOTS, COPIED, 2, PAGE, HEAD)
    second = stay(page_table, lengths, query, fresh, pool, slots, 64, 56)
    merged = merge(slots, first, second, returned)
    width = out_weight.shape[1] // PIECES
    groups = (
        ([first, second], ((0, 0), (0, 64), (1, 0), (1, 64))),
        ([merged], ((0, 32), (0, 96), (0, 160), (0, 224))),
    )
    finished = [[], []]
    for to, (rows, starts) in enumerate(groups):
        for piece in range(PIECES):
            total = reduce_z(rows, starts, out_weight, piece, width)
            finished[to].append(total + send_x(total.astype(jnp.bfloat16), to).astype(jnp.float32))
    projected = jnp.concatenate(
        [jnp.where(xi == 0, zero, one).astype(jnp.bfloat16) for zero, one in zip(*finished)], axis=1
    ).reshape(16, 2, -1)
    arrived = pick(slots, incoming)
    attention = merged.reshape(ROWS, 2, 8 * HEAD)
    return (attention[None], projected[None], arrived[None])


def solution(mesh):
    placed = (
        P("replica", None, None, "tensor"),
        P("replica", None, None, None, "tensor"),
        P("replica", None, None, None, "tensor"),
        P("replica", None, None),
        P("replica", None),
        P("replica", None, None),
        P("replica", None, None),
        P("tensor", None),
    )
    return jax.shard_map(
        body,
        mesh=mesh,
        in_specs=placed,
        out_specs=(
            P("replica", None, None, "tensor"),
            P("replica", "tensor", None, None),
            P("replica", None, None, None, None, "tensor"),
        ),
        check_vma=False,
    )
```

time: 489 us -> 178 us (0.36)
  waiting for transfers between devices: 194 us -> 37.6 us
  local copies, waits for them, and re-layouts: 146 us -> 22.1 us
  Pallas kernels: 0 us -> 66.5 us
  other arithmetic: 63.4 us -> 3.2 us
  matrix products: 46.8 us -> 0 us
  starting transfers between devices: 20.4 us -> 45.8 us
  between operations: 14.3 us -> 0.97 us
    all_to_all x3, waiting for transfers between devices: 103 us -> 2.86 us  [the longest x1 2.85 us: body(): lax.all_to_all(answered.reshape(REPLICAS, CAP, 16, HEAD), 'replica', spli...]
    reduce_scatter x1 -> x0, waiting for transfers between devices: 91.1 us -> none  [body(): lax.psum_scatter(product.reshape(row_count // lax.axis_size('tensor') * l...]
    gather x6 -> x0, local copies, waits for them, and re-layouts: 75.4 us -> none  [the longest x1 44.2 us: page_rows(): selected_pages = jnp.take(pages_local, page_ids, axis=1)]
    pallas_call x0 -> x10, Pallas kernels: none -> 66.5 us  [the longest x4 31.8 us: project(): pl.pallas_call(functools.partial(project_kernel, starts=starts), out_shap...]
    select_n x5 -> x0, other arithmetic: 54.8 us -> none  [the longest x2 40 us: page_rows(): selected_pages = jnp.take(pages_local, page_ids, axis=1)]
    slice x4 -> x0, local copies, waits for them, and re-layouts: 49.7 us -> none  [the longest x1 40.3 us: page_rows(): selected_pages[1].reshape(shape_out)]
    dot_general x7 -> x0, matrix products: 46.8 us -> none  [the longest x3 17 us: attend(): jnp.einsum('nsgjk,nkgd->nsgjd', weights, values_in, preferred_element_typ...]
    ppermute x0 -> x16, waiting for transfers between devices: none -> 34.7 us  [the longest x4 25.5 us: send_x(): lax.ppermute(value, 'tensor', [(2 * z + 1 - to, 2 * z + to) for z in rang...]
  transfers between devices with their start and end apart: 4 -> 19, of which waited for: 3 -> 6; matrix products, arithmetic and copies ran while one was open for 36% -> 2% of each run, Pallas kernels for 0% -> 34%
where the time goes in v1:
time: 178 us; the launch traced here: 176 us
  Pallas kernels  66.5 us (37%)
  starting transfers between devices  45.8 us (26%)
  waiting for transfers between devices  37.6 us (21%)
  local copies, waits for them, and re-layouts  22.1 us (12%)
  other arithmetic  3.2 us (2%)
    pallas_call x4, Pallas kernels, project(): pl.pallas_call(functools.partial(project_kernel, starts=starts), out_shap...  31.8 us
    ppermute x4, waiting for transfers between devices, send_x(): lax.ppermute(value, 'tensor', [(2 * z + 1 - to, 2 * z + to) for z in rang...  25.5 us
    pallas_call x2, Pallas kernels, stay(): pl.pallas_call(functools.partial(stay_kernel, first=first), out_shape=jax...  18.9 us
    ppermute x12, starting transfers between devices, shift_z(): return lax.ppermute(value, 'tensor', pairs)  18.7 us
    unnamed x46, local copies, waits for them, and re-layouts  17.7 us
    ppermute x12, waiting for transfers between devices, shift_z(): return lax.ppermute(value, 'tensor', pairs)  9.23 us
    pallas_call x1, Pallas kernels, serve(): pl.pallas_call(serve_kernel, out_shape=(jax.ShapeDtypeStruct((SLOTS, 16,...  7.67 us
    ppermute x4, starting transfers between devices, send_x(): lax.ppermute(value, 'tensor', [(2 * z + 1 - to, 2 * z + to) for z in rang...  7.25 us
  transfers between devices with their start and end apart: 19, of which 6 were waited for; matrix products, arithmetic and copies ran while one was open for 2% of the time, Pallas kernels for 34%

profile of v1, /device:TPU:10, one launch (start us, length us, event | category | flops | bytes accessed | tf_op | source)
XLA Modules:
  0.0 176.2 jit_solution(1378703411322198164)
XLA Ops:
  0.6 1.0 copy.18
  1.7 2.2 %reshape_squeeze.3.query_ref = bf16[128,16,128]{2,1,0:T(8,128)(2,1)} reshape(bf16[1,128,2,1024]{3,2,1,0:T(2,128)(2,1)} %param.8) | data formatting | bytes 1048576 | tf_op jit(solution)/shard_map/reshape;squeeze | solution.py:366
  3.9 1.4 copy.14.table_ref
  5.3 1.3 copy.12.offset_ref
  6.6 1.3 copy.13.order_ref
  8.0 1.0 maximum_maximum_fusion.fresh_ref
  9.0 3.1 %pack_requests.1 = (bf16[32,32,128]{2,1,0:T(8,128)(2,1)}, s32[14]{0:T(128)}) custom-call(s32[1,14,1]{2,1,0:T(8,128)} %copy.12.offset_ref, s32[1,14,16]{2,1,0:T(8,128)} %copy.13.order_ref, s32[1,128,16]{2,1,0:T(8,128)} %copy.14.table_ref, s32[1,128]{1,0:T(1,128)} %length_ref.5, bf16[128,16,128]{2,1,0:T(8,128)(2,1)} %reshape_squeeze.3.query_ref, ...), custom_call_target="tpu_custom_call" | custom-call | tf_op jit(solution)/shard_map/pack_requests/pallas_call | solution.py:157
  12.1 6.5 %all-to-all-start = ((bf16[16,2,32,128]{3,2,1,0:T(8,128)(2,1)}), bf16[16,2,32,128]{3,2,1,0:T(8,128)(2,1)S(1)}, u32[]{:S(2)}, u32[]{:S(2)}) async-start(bf16[16,2,32,128]{3,2,1,0:T(8,128)(2,1)} %bitcast.23), calls=%async_computation | async-start | bytes 524288 | tf_op jit(solution)/shard_map/all_to_all | solution.py:372
  18.6 1.0 copy-done.2
  19.7 1.0 copy-done.3
  20.7 0.8 copy-done.5
  22.9 2.2 %copy-done.9 = bf16[1,2,128,64,128]{4,3,2,1,0:T(8,128)(2,1)S(1)} copy-done((bf16[1,2,128,64,128]{4,3,2,1,0:T(8,128)(2,1)S(1)}, bf16[1,2,128,64,128]{4,3,2,1,0:T(8,128)(2,1)}, u32[]{:S(2)}) %copy-start.9) | copy-done | bytes 4194328
  25.1 9.0 %attend_staying.3.second_ref.refs_1_ = bf16[112,1024]{1,0:T(8,128)(2,1)S(1)} custom-call(s32[1,128,16]{2,1,0:T(8,128)S(1)} %copy-done.5, s32[1,128]{1,0:T(1,128)S(1)} %copy-done.8, bf16[128,16,128]{2,1,0:T(8,128)(2,1)S(1)} %copy-done.2, bf16[128,16,128]{2,1,0:T(8,128)(2,1)S(1)} %copy-done.3, bf16[2,128,64,128]{3,2,1,0:T(8,128)(2,1)S(1)} %bitcast.17, ...), custom_call_target="tpu_custom_call" | custom-call | flops 5600000000 | bytes 8388608 | tf_op jit(solution)/shard_map/attend_staying/pallas_call | solution.py:108
  34.1 0.7 copy-done.4
  34.8 10.0 %attend_staying.2.first_ref.refs_0_ = bf16[128,1024]{1,0:T(8,128)(2,1)S(1)} custom-call(s32[1,128,16]{2,1,0:T(8,128)S(1)} %copy-done.6, s32[1,128]{1,0:T(1,128)S(1)} %copy-done.8, bf16[128,16,128]{2,1,0:T(8,128)(2,1)S(1)} %copy-done.2, bf16[128,16,128]{2,1,0:T(8,128)(2,1)S(1)} %copy-done.3, bf16[2,128,64,128]{3,2,1,0:T(8,128)(2,1)S(1)} %bitcast.18, ...), custom_call_target="tpu_custom_call" | custom-call | flops 6400000000 | bytes 8388608 | tf_op jit(solution)/shard_map/attend_staying/pallas_call | solution.py:108
  44.8 0.7 copy-done.1
  45.5 7.9 %project_piece.4 = (bf16[32,4096]{1,0:T(8,128)(2,1)}, bf16[32,4096]{1,0:T(8,128)(2,1)}, bf16[32,4096]{1,0:T(8,128)(2,1)}, bf16[32,4096]{1,0:T(8,128)(2,1)}) custom-call(bf16[128,1024]{1,0:T(8,128)(2,1)} %copy-done.1, bf16[112,1024]{1,0:T(8,128)(2,1)} %copy-done.4, bf16[1024,8192]{1,0:T(8,128)(2,1)} %refs_1_.3), custom_call_target="tpu_custom_call" | custom-call | flops 2147483648 | bytes 8388608 | tf_op jit(solution)/shard_map/project_piece/pallas_call | solution.py:316
  53.4 1.9 %collective-permute-start = (bf16[32,4096]{1,0:T(8,128)(2,1)}, bf16[32,4096]{1,0:T(8,128)(2,1)S(1)}, u32[]{:S(2)}, u32[]{:S(2)}) collective-permute-start(bf16[32,4096]{1,0:T(8,128)(2,1)} %get-tuple-element.28), channel_id=1, source_target_pairs={{0,2},{1,3},{2,4},{3,5},{4,6},{5,7},{6,0},{7,1},{8,10},{9,11},{10,... | collective-permute-start | bytes 786440 | tf_op jit(solution)/shard_map/ppermute | solution.py:334
  55.3 2.2 %collective-permute-start.2 = (bf16[32,4096]{1,0:T(8,128)(2,1)}, bf16[32,4096]{1,0:T(8,128)(2,1)S(1)}, u32[]{:S(2)}, u32[]{:S(2)}) collective-permute-start(bf16[32,4096]{1,0:T(8,128)(2,1)} %get-tuple-element.29), channel_id=1, source_target_pairs={{0,6},{1,7},{2,0},{3,1},{4,2},{5,3},{6,4},{7,5},{8,14},{9,15},{10,... | collective-permute-start | bytes 786440 | tf_op jit(solution)/shard_map/ppermute | solution.py:334
  57.5 7.9 %project_piece.6 = (bf16[32,4096]{1,0:T(8,128)(2,1)}, bf16[32,4096]{1,0:T(8,128)(2,1)}, bf16[32,4096]{1,0:T(8,128)(2,1)}, bf16[32,4096]{1,0:T(8,128)(2,1)}) custom-call(bf16[128,1024]{1,0:T(8,128)(2,1)} %copy-done.1, bf16[112,1024]{1,0:T(8,128)(2,1)} %copy-done.4, bf16[1024,8192]{1,0:T(8,128)(2,1)} %refs_1_.3), custom_call_target="tpu_custom_call" | custom-call | flops 2147483648 | bytes 8388608 | tf_op jit(solution)/shard_map/project_piece/pallas_call | solution.py:316
  65.4 2.0 %collective-permute-start.9 = (bf16[32,4096]{1,0:T(8,128)(2,1)}, bf16[32,4096]{1,0:T(8,128)(2,1)S(1)}, u32[]{:S(2)}, u32[]{:S(2)}) collective-permute-start(bf16[32,4096]{1,0:T(8,128)(2,1)} %get-tuple-element.37), channel_id=1, source_target_pairs={{0,6},{1,7},{2,0},{3,1},{4,2},{5,3},{6,4},{7,5},{8,14},{9,15},{10,... | collective-permute-start | bytes 786440 | tf_op jit(solution)/shard_map/ppermute | solution.py:334
  67.4 2.2 %copy-done.10 = bf16[1,2,128,64,128]{4,3,2,1,0:T(8,128)(2,1)S(1)} copy-done((bf16[1,2,128,64,128]{4,3,2,1,0:T(8,128)(2,1)S(1)}, bf16[1,2,128,64,128]{4,3,2,1,0:T(8,128)(2,1)}, u32[]{:S(2)}) %copy-start.10) | copy-done | bytes 4194328
  69.6 7.7 %serve_requests.1 = (bf16[32,16,128]{2,1,0:T(8,128)(2,1)}, bf16[32,4,2,64,128]{4,3,2,1,0:T(8,128)(2,1)S(1)}) custom-call(bf16[32,32,128]{2,1,0:T(8,128)(2,1)S(1)} %bitcast.16, bf16[2,128,64,128]{3,2,1,0:T(8,128)(2,1)S(1)} %bitcast.19), custom_call_target="tpu_custom_call" | custom-call | flops 4000000000 | bytes 8388608 | tf_op jit(solution)/shard_map/serve_requests/pallas_call | solution.py:223
  77.3 1.9 %copy-done = bf16[32,4,2,64,128]{4,3,2,1,0:T(8,128)(2,1)} copy-done((bf16[32,4,2,64,128]{4,3,2,1,0:T(8,128)(2,1)}, bf16[32,4,2,64,128]{4,3,2,1,0:T(8,128)(2,1)S(1)}, u32[]{:S(2)}) %copy-start) | copy-done | bytes 4194328
  79.3 7.2 %all-to-all-start.1 = ((bf16[16,2,16,128]{3,2,1,0:T(8,128)(2,1)}), bf16[16,2,16,128]{3,2,1,0:T(8,128)(2,1)S(1)}, u32[]{:S(2)}, u32[]{:S(2)}) async-start(bf16[16,2,16,128]{3,2,1,0:T(8,128)(2,1)} %bitcast.6), calls=%async_computation.1 | async-start | bytes 262144 | tf_op jit(solution)/shard_map/all_to_all | solution.py:377
  86.8 3.3 %collective-permute-start.10 = (bf16[32,4096]{1,0:T(8,128)(2,1)S(1)}, bf16[32,4096]{1,0:T(8,128)(2,1)S(1)}, u32[]{:S(2)}, u32[]{:S(2)}) collective-permute-start(bf16[32,4096]{1,0:T(8,128)(2,1)S(1)} %add_convert_fusion.1), channel_id=1, source_target_pairs={{0,6},{1,7},{2,0},{3,1},{4,2},{5,3},{6,4},{7,5},{8,14},{9,15},{10,... | collective-permute-start | bytes 786440 | tf_op jit(solution)/shard_map/ppermute | solution.py:334
  90.0 2.9 %all-to-all-done.1 = bf16[16,2,16,128]{3,2,1,0:T(8,128)(2,1)S(1)} async-done(((bf16[16,2,16,128]{3,2,1,0:T(8,128)(2,1)}), bf16[16,2,16,128]{3,2,1,0:T(8,128)(2,1)S(1)}, u32[]{:S(2)}, u32[]{:S(2)}) %all-to-all-start.1) | async-done | bytes 131104 | tf_op jit(solution)/shard_map/all_to_all | solution.py:377
  93.5 6.2 %all-to-all-start.2 = ((bf16[16,2,4,2,64,128]{5,4,3,2,1,0:T(8,128)(2,1)}), bf16[16,2,4,2,64,128]{5,4,3,2,1,0:T(8,128)(2,1)}, u32[]{:S(2)}, u32[]{:S(2)}) async-start(bf16[16,2,4,2,64,128]{5,4,3,2,1,0:T(8,128)(2,1)} %bitcast.15), calls=%async_computation.2 | async-start | bytes 8388608 | tf_op jit(solution)/shard_map/all_to_all | solution.py:380
  99.7 2.0 %merge_rows.1.refs_0_ = bf16[256,1024]{1,0:T(8,128)(2,1)} custom-call(s32[14]{0:T(128)} %get-tuple-element.23.after_ref.slot_ref, bf16[128,1024]{1,0:T(8,128)(2,1)} %copy-done.1, bf16[112,1024]{1,0:T(8,128)(2,1)} %copy-done.4, bf16[32,16,128]{2,1,0:T(8,128)(2,1)} %bitcast.22), custom_call_target="tpu_custom_call" | custom-call | tf_op jit(solution)/shard_map/merge_rows/pallas_call | solution.py:257
  101.7 8.0 %project_piece.5 = (bf16[32,4096]{1,0:T(8,128)(2,1)}, bf16[32,4096]{1,0:T(8,128)(2,1)}, bf16[32,4096]{1,0:T(8,128)(2,1)}, bf16[32,4096]{1,0:T(8,128)(2,1)}) custom-call(bf16[256,1024]{1,0:T(8,128)(2,1)} %merge_rows.1.refs_0_, bf16[1024,8192]{1,0:T(8,128)(2,1)} %refs_1_.3), custom_call_target="tpu_custom_call" | custom-call | flops 2147483648 | bytes 8388608 | tf_op jit(solution)/shard_map/project_piece/pallas_call | solution.py:316
  109.7 1.0 broadcast_in_dim_reshape.6
  110.8 8.0 %project_piece.7 = (bf16[32,4096]{1,0:T(8,128)(2,1)}, bf16[32,4096]{1,0:T(8,128)(2,1)}, bf16[32,4096]{1,0:T(8,128)(2,1)}, bf16[32,4096]{1,0:T(8,128)(2,1)}) custom-call(bf16[256,1024]{1,0:T(8,128)(2,1)} %merge_rows.1.refs_0_, bf16[1024,8192]{1,0:T(8,128)(2,1)} %refs_1_.3), custom_call_target="tpu_custom_call" | custom-call | flops 2147483648 | bytes 8388608 | tf_op jit(solution)/shard_map/project_piece/pallas_call | solution.py:316
  118.8 3.3 %collective-permute-start.6 = (bf16[32,4096]{1,0:T(8,128)(2,1)S(1)}, bf16[32,4096]{1,0:T(8,128)(2,1)S(1)}, u32[]{:S(2)}, u32[]{:S(2)}) collective-permute-start(bf16[32,4096]{1,0:T(8,128)(2,1)S(1)} %copy-done.20), channel_id=1, source_target_pairs={{0,6},{1,7},{2,0},{3,1},{4,2},{5,3},{6,4},{7,5},{8,14},{9,15},{10,... | collective-permute-start | bytes 786440 | tf_op jit(solution)/shard_map/ppermute | solution.py:334
  122.1 1.9 %collective-permute-start.13 = (bf16[32,4096]{1,0:T(8,128)(2,1)}, bf16[32,4096]{1,0:T(8,128)(2,1)S(1)}, u32[]{:S(2)}, u32[]{:S(2)}) collective-permute-start(bf16[32,4096]{1,0:T(8,128)(2,1)} %get-tuple-element.41), channel_id=1, source_target_pairs={{0,6},{1,7},{2,0},{3,1},{4,2},{5,3},{6,4},{7,5},{8,14},{9,15},{10,... | collective-permute-start | bytes 786440 | tf_op jit(solution)/shard_map/ppermute | solution.py:334
  124.3 3.4 %collective-permute-start.3 = (bf16[32,4096]{1,0:T(8,128)(2,1)S(1)}, bf16[32,4096]{1,0:T(8,128)(2,1)S(1)}, u32[]{:S(2)}, u32[]{:S(2)}) collective-permute-start(bf16[32,4096]{1,0:T(8,128)(2,1)S(1)} %fusion), channel_id=1, source_target_pairs={{1,0},{3,2},{5,4},{7,6},{9,8},{11,10},{13,12},{15,14},{17,16},{19,... | collective-permute-start | bytes 786440 | tf_op jit(solution)/shard_map/ppermute | solution.py:338
  127.8 1.3 collective-permute-start.11
  129.2 4.5 %collective-permute-done.13 = bf16[32,4096]{1,0:T(8,128)(2,1)S(1)} collective-permute-done((bf16[32,4096]{1,0:T(8,128)(2,1)}, bf16[32,4096]{1,0:T(8,128)(2,1)S(1)}, u32[]{:S(2)}, u32[]{:S(2)}) %collective-permute-start.13) | collective-permute-done | bytes 262176 | tf_op jit(solution)/shard_map/ppermute | solution.py:334
  133.6 1.7 collective-permute-start.5
  135.3 1.0 add_convert_fusion
  136.3 2.0 %collective-permute-start.14 = (bf16[32,4096]{1,0:T(8,128)(2,1)S(1)}, bf16[32,4096]{1,0:T(8,128)(2,1)S(1)}, u32[]{:S(2)}, u32[]{:S(2)}) collective-permute-start(bf16[32,4096]{1,0:T(8,128)(2,1)S(1)} %add_convert_fusion), channel_id=1, source_target_pairs={{0,6},{1,7},{2,0},{3,1},{4,2},{5,3},{6,4},{7,5},{8,14},{9,15},{10,... | collective-permute-start | bytes 786440 | tf_op jit(solution)/shard_map/ppermute | solution.py:334
  138.3 4.7 %collective-permute-done.5 = bf16[32,4096]{1,0:T(8,128)(2,1)S(1)} collective-permute-done((bf16[32,4096]{1,0:T(8,128)(2,1)S(1)}, bf16[32,4096]{1,0:T(8,128)(2,1)S(1)}, u32[]{:S(2)}, u32[]{:S(2)}) %collective-permute-start.5) | collective-permute-done | bytes 262176 | tf_op jit(solution)/shard_map/ppermute | solution.py:334
  143.2 1.3 collective-permute-start.7
  144.6 1.3 collective-permute-start.15
  145.9 15.3 %collective-permute-done.3 = bf16[32,4096]{1,0:T(8,128)(2,1)S(1)} collective-permute-done((bf16[32,4096]{1,0:T(8,128)(2,1)S(1)}, bf16[32,4096]{1,0:T(8,128)(2,1)S(1)}, u32[]{:S(2)}, u32[]{:S(2)}) %collective-permute-start.3) | collective-permute-done | bytes 262176 | tf_op jit(solution)/shard_map/ppermute | solution.py:338
  161.2 5.3 %collective-permute-done.7 = bf16[32,4096]{1,0:T(8,128)(2,1)S(1)} collective-permute-done((bf16[32,4096]{1,0:T(8,128)(2,1)S(1)}, bf16[32,4096]{1,0:T(8,128)(2,1)S(1)}, u32[]{:S(2)}, u32[]{:S(2)}) %collective-permute-start.7) | collective-permute-done | bytes 262176 | tf_op jit(solution)/shard_map/ppermute | solution.py:338
  166.8 4.9 %collective-permute-done.15 = bf16[32,4096]{1,0:T(8,128)(2,1)S(1)} collective-permute-done((bf16[32,4096]{1,0:T(8,128)(2,1)S(1)}, bf16[32,4096]{1,0:T(8,128)(2,1)S(1)}, u32[]{:S(2)}, u32[]{:S(2)}) %collective-permute-start.15) | collective-permute-done | bytes 262176 | tf_op jit(solution)/shard_map/ppermute | solution.py:338
  172.0 1.1 broadcast_in_dim_reshape.7
  173.1 3.1 %pick_pages.1 = bf16[14,4,2,64,128]{4,3,2,1,0:T(8,128)(2,1)} custom-call(s32[14]{0:T(128)} %get-tuple-element.23.after_ref.slot_ref, bf16[32,4,2,64,128]{4,3,2,1,0:T(8,128)(2,1)} %bitcast.9.got_ref), custom_call_target="tpu_custom_call" | custom-call | tf_op jit(solution)/shard_map/pick_pages/pallas_call | solution.py:282
  (64 shorter events, 3.9 us)
Async XLA Ops:
  12.1 55.3 %all-to-all-start = ((bf16[16,2,32,128]{3,2,1,0:T(8,128)(2,1)}), bf16[16,2,32,128]{3,2,1,0:T(8,128)(2,1)S(1)}, u32[]{:S(2)}, u32[]{:S(2)}) async-start(bf16[16,2,32,128]{3,2,1,0:T(8,128)(2,1)} %bitcast.23), calls=%async_computation | async-start | bytes 524288 | tf_op jit(solution)/shard_map/all_to_all | solution.py:372
  18.6 1.0 copy-start.2
  19.7 1.0 copy-start.3
  20.7 0.8 copy-start.5
  21.6 0.7 copy-start.7
  22.2 0.7 copy-start.8
  22.9 2.2 %copy-start.9 = (bf16[1,2,128,64,128]{4,3,2,1,0:T(8,128)(2,1)S(1)}, bf16[1,2,128,64,128]{4,3,2,1,0:T(8,128)(2,1)}, u32[]{:S(2)}) copy-start(bf16[1,2,128,64,128]{4,3,2,1,0:T(8,128)(2,1)} %param.10) | copy-start | bytes 12582916
  25.1 9.7 %copy-start.6 = (s32[1,128,16]{2,1,0:T(8,128)S(1)}, s32[1,128,16]{2,1,0:T(8,128)}, u32[]{:S(2)}) copy-start(s32[1,128,16]{2,1,0:T(8,128)} %copy.14.table_ref) | copy-start | bytes 24580
  34.1 0.7 copy-start.4
  44.7 0.7 copy-start.1
  53.4 33.1 %collective-permute-start = (bf16[32,4096]{1,0:T(8,128)(2,1)}, bf16[32,4096]{1,0:T(8,128)(2,1)S(1)}, u32[]{:S(2)}, u32[]{:S(2)}) collective-permute-start(bf16[32,4096]{1,0:T(8,128)(2,1)} %get-tuple-element.28), channel_id=1, source_target_pairs={{0,2},{1,3},{2,4},{3,5},{4,6},{5,7},{6,0},{7,1},{8,10},{9,11},{10,... | collective-permute-start | bytes 786440 | tf_op jit(solution)/shard_map/ppermute | solution.py:334
  55.3 63.5 %collective-permute-start.2 = (bf16[32,4096]{1,0:T(8,128)(2,1)}, bf16[32,4096]{1,0:T(8,128)(2,1)S(1)}, u32[]{:S(2)}, u32[]{:S(2)}) collective-permute-start(bf16[32,4096]{1,0:T(8,128)(2,1)} %get-tuple-element.29), channel_id=1, source_target_pairs={{0,6},{1,7},{2,0},{3,1},{4,2},{5,3},{6,4},{7,5},{8,14},{9,15},{10,... | collective-permute-start | bytes 786440 | tf_op jit(solution)/shard_map/ppermute | solution.py:334
  65.4 21.3 %collective-permute-start.9 = (bf16[32,4096]{1,0:T(8,128)(2,1)}, bf16[32,4096]{1,0:T(8,128)(2,1)S(1)}, u32[]{:S(2)}, u32[]{:S(2)}) collective-permute-start(bf16[32,4096]{1,0:T(8,128)(2,1)} %get-tuple-element.37), channel_id=1, source_target_pairs={{0,6},{1,7},{2,0},{3,1},{4,2},{5,3},{6,4},{7,5},{8,14},{9,15},{10,... | collective-permute-start | bytes 786440 | tf_op jit(solution)/shard_map/ppermute | solution.py:334
  67.4 56.7 %collective-permute-start.8 = (bf16[32,4096]{1,0:T(8,128)(2,1)}, bf16[32,4096]{1,0:T(8,128)(2,1)S(1)}, u32[]{:S(2)}, u32[]{:S(2)}) collective-permute-start(bf16[32,4096]{1,0:T(8,128)(2,1)} %get-tuple-element.35), channel_id=1, source_target_pairs={{0,2},{1,3},{2,4},{3,5},{4,6},{5,7},{6,0},{7,1},{8,10},{9,11},{10,... | collective-permute-start | bytes 786440 | tf_op jit(solution)/shard_map/ppermute | solution.py:334
  67.4 2.2 %copy-start.10 = (bf16[1,2,128,64,128]{4,3,2,1,0:T(8,128)(2,1)S(1)}, bf16[1,2,128,64,128]{4,3,2,1,0:T(8,128)(2,1)}, u32[]{:S(2)}) copy-start(bf16[1,2,128,64,128]{4,3,2,1,0:T(8,128)(2,1)} %param.10) | copy-start | bytes 12582916
  69.6 16.9 %copy-start.17 = (bf16[32,4096]{1,0:T(8,128)(2,1)S(1)}, bf16[32,4096]{1,0:T(8,128)(2,1)}, u32[]{:S(2)}) copy-start(bf16[32,4096]{1,0:T(8,128)(2,1)} %get-tuple-element.27) | copy-start | bytes 786436
  69.6 17.1 %copy-start.18 = (bf16[32,4096]{1,0:T(8,128)(2,1)S(1)}, bf16[32,4096]{1,0:T(8,128)(2,1)}, u32[]{:S(2)}) copy-start(bf16[32,4096]{1,0:T(8,128)(2,1)} %get-tuple-element.36) | copy-start | bytes 786436
  77.3 2.0 %copy-start = (bf16[32,4,2,64,128]{4,3,2,1,0:T(8,128)(2,1)}, bf16[32,4,2,64,128]{4,3,2,1,0:T(8,128)(2,1)S(1)}, u32[]{:S(2)}) copy-start(bf16[32,4,2,64,128]{4,3,2,1,0:T(8,128)(2,1)S(1)} %get-tuple-element.42) | copy-start | bytes 12582916
  79.3 13.6 %all-to-all-start.1 = ((bf16[16,2,16,128]{3,2,1,0:T(8,128)(2,1)}), bf16[16,2,16,128]{3,2,1,0:T(8,128)(2,1)S(1)}, u32[]{:S(2)}, u32[]{:S(2)}) async-start(bf16[16,2,16,128]{3,2,1,0:T(8,128)(2,1)} %bitcast.6), calls=%async_computation.1 | async-start | bytes 262144 | tf_op jit(solution)/shard_map/all_to_all | solution.py:377
  86.6 35.5 %collective-permute-start.1 = (bf16[32,4096]{1,0:T(8,128)(2,1)S(1)}, bf16[32,4096]{1,0:T(8,128)(2,1)S(1)}, u32[]{:S(2)}, u32[]{:S(2)}) collective-permute-start(bf16[32,4096]{1,0:T(8,128)(2,1)S(1)} %add_convert_fusion.3), channel_id=1, source_target_pairs={{0,2},{1,3},{2,4},{3,5},{4,6},{5,7},{6,0},{7,1},{8,10},{9,11},{10,... | collective-permute-start | bytes 786440 | tf_op jit(solution)/shard_map/ppermute | solution.py:334
  86.8 37.5 %collective-permute-start.10 = (bf16[32,4096]{1,0:T(8,128)(2,1)S(1)}, bf16[32,4096]{1,0:T(8,128)(2,1)S(1)}, u32[]{:S(2)}, u32[]{:S(2)}) collective-permute-start(bf16[32,4096]{1,0:T(8,128)(2,1)S(1)} %add_convert_fusion.1), channel_id=1, source_target_pairs={{0,6},{1,7},{2,0},{3,1},{4,2},{5,3},{6,4},{7,5},{8,14},{9,15},{10,... | collective-permute-start | bytes 786440 | tf_op jit(solution)/shard_map/ppermute | solution.py:334
  92.9 0.7 copy-start.16
  93.5 79.6 %all-to-all-start.2 = ((bf16[16,2,4,2,64,128]{5,4,3,2,1,0:T(8,128)(2,1)}), bf16[16,2,4,2,64,128]{5,4,3,2,1,0:T(8,128)(2,1)}, u32[]{:S(2)}, u32[]{:S(2)}) async-start(bf16[16,2,4,2,64,128]{5,4,3,2,1,0:T(8,128)(2,1)} %bitcast.15), calls=%async_computation.2 | async-start | bytes 8388608 | tf_op jit(solution)/shard_map/all_to_all | solution.py:380
  101.7 8.0 %copy-start.11 = (bf16[256,1024]{1,0:T(8,128)(2,1)S(1)}, bf16[256,1024]{1,0:T(8,128)(2,1)}, u32[]{:S(2)}) copy-start(bf16[256,1024]{1,0:T(8,128)(2,1)} %merge_rows.1.refs_0_) | copy-start | bytes 1572868
  110.7 8.1 %copy-start.20 = (bf16[32,4096]{1,0:T(8,128)(2,1)S(1)}, bf16[32,4096]{1,0:T(8,128)(2,1)}, u32[]{:S(2)}) copy-start(bf16[32,4096]{1,0:T(8,128)(2,1)} %get-tuple-element.33) | copy-start | bytes 786436
  110.7 13.2 %copy-start.13 = (bf16[32,4096]{1,0:T(8,128)(2,1)S(1)}, bf16[32,4096]{1,0:T(8,128)(2,1)}, u32[]{:S(2)}) copy-start(bf16[32,4096]{1,0:T(8,128)(2,1)} %get-tuple-element.26) | copy-start | bytes 786436
  110.7 16.9 %copy-start.12 = (bf16[32,4096]{1,0:T(8,128)(2,1)S(1)}, bf16[32,4096]{1,0:T(8,128)(2,1)}, u32[]{:S(2)}) copy-start(bf16[32,4096]{1,0:T(8,128)(2,1)} %get-tuple-element.34) | copy-start | bytes 786436
  110.7 18.4 %copy-start.19 = (bf16[32,4096]{1,0:T(8,128)(2,1)S(1)}, bf16[32,4096]{1,0:T(8,128)(2,1)}, u32[]{:S(2)}) copy-start(bf16[32,4096]{1,0:T(8,128)(2,1)} %get-tuple-element.31) | copy-start | bytes 786436
  110.7 32.4 %copy-start.15 = (bf16[32,4096]{1,0:T(8,128)(2,1)S(1)}, bf16[32,4096]{1,0:T(8,128)(2,1)}, u32[]{:S(2)}) copy-start(bf16[32,4096]{1,0:T(8,128)(2,1)} %get-tuple-element.30) | copy-start | bytes 786436
  110.7 17.1 %collective-permute-start.4 = (bf16[32,4096]{1,0:T(8,128)(2,1)}, bf16[32,4096]{1,0:T(8,128)(2,1)S(1)}, u32[]{:S(2)}, u32[]{:S(2)}) collective-permute-start(bf16[32,4096]{1,0:T(8,128)(2,1)} %get-tuple-element.32), channel_id=1, source_target_pairs={{0,2},{1,3},{2,4},{3,5},{4,6},{5,7},{6,0},{7,1},{8,10},{9,11},{10,... | collective-permute-start | bytes 786440 | tf_op jit(solution)/shard_map/ppermute | solution.py:334
  118.8 25.7 %copy-start.14 = (bf16[32,4096]{1,0:T(8,128)(2,1)S(1)}, bf16[32,4096]{1,0:T(8,128)(2,1)}, u32[]{:S(2)}) copy-start(bf16[32,4096]{1,0:T(8,128)(2,1)} %get-tuple-element.38) | copy-start | bytes 786436
  118.8 17.5 %collective-permute-start.6 = (bf16[32,4096]{1,0:T(8,128)(2,1)S(1)}, bf16[32,4096]{1,0:T(8,128)(2,1)S(1)}, u32[]{:S(2)}, u32[]{:S(2)}) collective-permute-start(bf16[32,4096]{1,0:T(8,128)(2,1)S(1)} %copy-done.20), channel_id=1, source_target_pairs={{0,6},{1,7},{2,0},{3,1},{4,2},{5,3},{6,4},{7,5},{8,14},{9,15},{10,... | collective-permute-start | bytes 786440 | tf_op jit(solution)/shard_map/ppermute | solution.py:334
  122.1 11.6 %collective-permute-start.13 = (bf16[32,4096]{1,0:T(8,128)(2,1)}, bf16[32,4096]{1,0:T(8,128)(2,1)S(1)}, u32[]{:S(2)}, u32[]{:S(2)}) collective-permute-start(bf16[32,4096]{1,0:T(8,128)(2,1)} %get-tuple-element.41), channel_id=1, source_target_pairs={{0,6},{1,7},{2,0},{3,1},{4,2},{5,3},{6,4},{7,5},{8,14},{9,15},{10,... | collective-permute-start | bytes 786440 | tf_op jit(solution)/shard_map/ppermute | solution.py:334
  124.1 20.4 %collective-permute-start.12 = (bf16[32,4096]{1,0:T(8,128)(2,1)}, bf16[32,4096]{1,0:T(8,128)(2,1)S(1)}, u32[]{:S(2)}, u32[]{:S(2)}) collective-permute-start(bf16[32,4096]{1,0:T(8,128)(2,1)} %get-tuple-element.39), channel_id=1, source_target_pairs={{0,2},{1,3},{2,4},{3,5},{4,6},{5,7},{6,0},{7,1},{8,10},{9,11},{10,... | collective-permute-start | bytes 786440 | tf_op jit(solution)/shard_map/ppermute | solution.py:334
  124.3 36.9 %collective-permute-start.3 = (bf16[32,4096]{1,0:T(8,128)(2,1)S(1)}, bf16[32,4096]{1,0:T(8,128)(2,1)S(1)}, u32[]{:S(2)}, u32[]{:S(2)}) collective-permute-start(bf16[32,4096]{1,0:T(8,128)(2,1)S(1)} %fusion), channel_id=1, source_target_pairs={{1,0},{3,2},{5,4},{7,6},{9,8},{11,10},{13,12},{15,14},{17,16},{19,... | collective-permute-start | bytes 786440 | tf_op jit(solution)/shard_map/ppermute | solution.py:338
  127.8 39.0 %collective-permute-start.11 = (bf16[32,4096]{1,0:T(8,128)(2,1)S(1)}, bf16[32,4096]{1,0:T(8,128)(2,1)S(1)}, u32[]{:S(2)}, u32[]{:S(2)}) collective-permute-start(bf16[32,4096]{1,0:T(8,128)(2,1)S(1)} %fusion.2), channel_id=1, source_target_pairs={{1,0},{3,2},{5,4},{7,6},{9,8},{11,10},{13,12},{15,14},{17,16},{19,... | collective-permute-start | bytes 786440 | tf_op jit(solution)/shard_map/ppermute | solution.py:338
  133.6 9.4 %collective-permute-start.5 = (bf16[32,4096]{1,0:T(8,128)(2,1)S(1)}, bf16[32,4096]{1,0:T(8,128)(2,1)S(1)}, u32[]{:S(2)}, u32[]{:S(2)}) collective-permute-start(bf16[32,4096]{1,0:T(8,128)(2,1)S(1)} %add_convert_fusion.2), channel_id=1, source_target_pairs={{0,2},{1,3},{2,4},{3,5},{4,6},{5,7},{6,0},{7,1},{8,10},{9,11},{10,... | collective-permute-start | bytes 786440 | tf_op jit(solution)/shard_map/ppermute | solution.py:334
  136.3 8.2 %collective-permute-start.14 = (bf16[32,4096]{1,0:T(8,128)(2,1)S(1)}, bf16[32,4096]{1,0:T(8,128)(2,1)S(1)}, u32[]{:S(2)}, u32[]{:S(2)}) collective-permute-start(bf16[32,4096]{1,0:T(8,128)(2,1)S(1)} %add_convert_fusion), channel_id=1, source_target_pairs={{0,6},{1,7},{2,0},{3,1},{4,2},{5,3},{6,4},{7,5},{8,14},{9,15},{10,... | collective-permute-start | bytes 786440 | tf_op jit(solution)/shard_map/ppermute | solution.py:334
  143.2 23.4 %collective-permute-start.7 = (bf16[32,4096]{1,0:T(8,128)(2,1)S(1)}, bf16[32,4096]{1,0:T(8,128)(2,1)S(1)}, u32[]{:S(2)}, u32[]{:S(2)}) collective-permute-start(bf16[32,4096]{1,0:T(8,128)(2,1)S(1)} %fusion.1), channel_id=1, source_target_pairs={{0,1},{2,3},{4,5},{6,7},{8,9},{10,11},{12,13},{14,15},{16,17},{18,... | collective-permute-start | bytes 786440 | tf_op jit(solution)/shard_map/ppermute | solution.py:338
  144.6 27.1 %collective-permute-start.15 = (bf16[32,4096]{1,0:T(8,128)(2,1)S(1)}, bf16[32,4096]{1,0:T(8,128)(2,1)S(1)}, u32[]{:S(2)}, u32[]{:S(2)}) collective-permute-start(bf16[32,4096]{1,0:T(8,128)(2,1)S(1)} %fusion.3), channel_id=1, source_target_pairs={{0,1},{2,3},{4,5},{6,7},{8,9},{10,11},{12,13},{14,15},{16,17},{18,... | collective-permute-start | bytes 786440 | tf_op jit(solution)/shard_map/ppermute | solution.py:338

commit v2 on v1

v2 whole, which is shorter than its diff:
```python
import functools
import math

import jax
import jax.numpy as jnp
from jax import lax
from jax.experimental import pallas as pl
from jax.experimental.pallas import tpu as pltpu
from jax.sharding import PartitionSpec as P

HEAD = 128
ROWS = 128
MIGRANTS = 14
STAYING = ROWS - MIGRANTS
COPIED = 4
PAGES_ROW = 16
PAGE = 64
REPLICAS = 16
CAP = 2
SLOTS = REPLICAS * CAP
GROUP = 8
CONTEXT = PAGES_ROW * PAGE
NEG_FILL = -1e30
SCALE = math.log2(math.e) / math.sqrt(HEAD)
META_ROW = 4
FIRST = 64
WIDTH = 2048
WEIGHT_TILE = 1024
WEIGHT_PARTS = 4
VMEM = pl.BlockSpec(memory_space=pltpu.VMEM)
SMEM = pl.BlockSpec(memory_space=pltpu.SMEM)
HBM = pl.BlockSpec(memory_space=pltpu.HBM)
PARAMS = pltpu.CompilerParams(vmem_limit_bytes=60 * 2**20)


def attend_group(queries, fresh, pages, lengths, pool_ref, scores_ref):
    nt = (((1,), (1,)), ((), ()))
    for i in range(GROUP):
        keys = jnp.concatenate([pool_ref[0, page] for page in pages[i]], axis=0)
        scores_ref[i, :, 0:CONTEXT] = lax.dot_general(
            queries[i], keys, nt, preferred_element_type=jnp.float32
        )
        scores_ref[i, :, CONTEXT : CONTEXT + 8] = lax.dot_general(
            queries[i], fresh[i].astype(jnp.bfloat16), nt, preferred_element_type=jnp.float32
        )
    outputs = []
    for i in range(GROUP):
        scores = scores_ref[i, :, 0:CONTEXT]
        position = lax.broadcasted_iota(jnp.int32, scores.shape, 1)
        scores = jnp.where(position < lengths[i], scores, NEG_FILL)
        fresh_scores = scores_ref[i, :, CONTEXT : CONTEXT + 8]
        line = lax.broadcasted_iota(jnp.int32, fresh_scores.shape, 1)
        step = lax.rem(lax.broadcasted_iota(jnp.int32, fresh_scores.shape, 0), 2)
        fresh_scores = jnp.where((line == 0) | (line == 2 * step), fresh_scores, NEG_FILL)
        highest = jnp.maximum(
            jnp.max(scores, axis=1, keepdims=True), jnp.max(fresh_scores, axis=1, keepdims=True)
        )
        weights = jnp.exp2((scores - highest) * SCALE).astype(jnp.bfloat16)
        fresh_weights = jnp.exp2((fresh_scores - highest) * SCALE).astype(jnp.bfloat16)
        total = jnp.sum(weights.astype(jnp.float32), axis=1, keepdims=True) + jnp.sum(
            fresh_weights.astype(jnp.float32), axis=1, keepdims=True
        )
        values = jnp.concatenate([pool_ref[1, page] for page in pages[i]], axis=0)
        fresh_values = pltpu.roll(fresh[i], 7, 0).astype(jnp.bfloat16)
        weighted = jnp.dot(weights, values, preferred_element_type=jnp.float32) + jnp.dot(
            fresh_weights, fresh_values, preferred_element_type=jnp.float32
        )
        outputs.append((weighted / total).astype(jnp.bfloat16))
    return outputs


def fresh_rows(tokens):
    tokens = tokens.astype(jnp.float32).reshape(4, HEAD)
    return jnp.concatenate([tokens, jnp.zeros((4, HEAD), jnp.float32)], axis=0)


def fetch_pool(pool_hbm, pool_ref, sem):
    copies = [
        pltpu.make_async_copy(pool_hbm.at[k, p : p + 32], pool_ref.at[k, p : p + 32], sem.at[k, p // 32])
        for k in range(2)
        for p in range(0, 128, 32)
    ]
    for copy in copies:
        copy.start()
    return copies


def attend_staying(table_ref, length_ref, query_ref, fresh_ref, out_ref, pool_ref, scores_ref, first):
    def group(g, carry):
        rows = [first + g * GROUP + i for i in range(GROUP)]
        outputs = attend_group(
            [query_ref[row].reshape(16, HEAD) for row in rows],
            [fresh_rows(fresh_ref[row]) for row in rows],
            [[table_ref[p, row] for p in range(PAGES_ROW)] for row in rows],
            [length_ref[0, row] for row in rows],
            pool_ref,
            scores_ref,
        )
        for i, output in enumerate(outputs):
            out_ref[g * GROUP + i] = output.reshape(8, 2, HEAD)
        return carry

    lax.fori_loop(0, out_ref.shape[0] // GROUP, group, 0)


def stay_kernel(table_ref, length_ref, query_ref, fresh_ref, pool_hbm, out_ref, pool_ref, scores_ref, sem):
    for copy in fetch_pool(pool_hbm, pool_ref, sem):
        copy.wait()
    attend_staying(table_ref, length_ref, query_ref, fresh_ref, out_ref, pool_ref, scores_ref, 0)


def attention_scratch(pool):
    return [
        pltpu.VMEM(pool.shape, pool.dtype),
        pltpu.VMEM((GROUP, 16, CONTEXT + 128), jnp.float32),
        pltpu.SemaphoreType.DMA((2, 4)),
    ]


def stay(table, lengths, query, fresh, pool, count):
    return pl.pallas_call(
        stay_kernel,
        out_shape=jax.ShapeDtypeStruct((count, 8, 2, HEAD), jnp.bfloat16),
        in_specs=[SMEM, SMEM, VMEM, VMEM, HBM],
        out_specs=VMEM,
        scratch_shapes=attention_scratch(pool),
        compiler_params=PARAMS,
        cost_estimate=pl.CostEstimate(flops=8 * 10**9, bytes_accessed=8 * 2**20, transcendentals=0),
        name="attend_first",
    )(table, lengths, query, fresh, pool)


def fetch_weight(weight_hbm, weight_ref, sem, start):
    copies = []
    for c in range(WEIGHT_PARTS):
        place = c * WEIGHT_TILE
        copies.append(
            pltpu.make_async_copy(
                weight_hbm.at[:, start + place : start + place + WEIGHT_TILE],
                weight_ref.at[:, place : place + WEIGHT_TILE],
                sem.at[c],
            )
        )
    for copy in copies:
        copy.start()
    return copies


def second_kernel(
    meta_ref, table_ref, length_ref, query_ref, fresh_ref, pool_hbm, out_ref, send_ref, pool_ref, scores_ref, sem, page_sem
):
    for copy in fetch_pool(pool_hbm, pool_ref, sem):
        copy.wait()

    def copies(slot, carry):
        for c in range(COPIED):
            page = meta_ref[slot, PAGES_ROW + c]
            pltpu.make_async_copy(pool_ref.at[:, page], send_ref.at[slot, c], page_sem).start()
        return carry

    lax.fori_loop(0, SLOTS, copies, 0)
    attend_staying(table_ref, length_ref, query_ref, fresh_ref, out_ref, pool_ref, scores_ref, FIRST)
    pltpu.make_async_copy(send_ref, send_ref, page_sem).wait()


def attend_second(meta, table, lengths, query, fresh, pool):
    return pl.pallas_call(
        second_kernel,
        out_shape=(
            jax.ShapeDtypeStruct((120 - FIRST, 8, 2, HEAD), jnp.bfloat16),
            jax.ShapeDtypeStruct((SLOTS, COPIED, 2, PAGE, HEAD), jnp.bfloat16),
        ),
        in_specs=[SMEM, SMEM, SMEM, VMEM, VMEM, HBM],
        out_specs=(VMEM, HBM),
        scratch_shapes=attention_scratch(pool) + [pltpu.SemaphoreType.DMA],
        compiler_params=PARAMS,
        cost_estimate=pl.CostEstimate(flops=8 * 10**9, bytes_accessed=8 * 2**20, transcendentals=0),
        name="attend_second",
    )(meta, table, lengths, query, fresh, pool)


def project_rolled(rolled_ref, weight_ref, fetch, part_refs):
    for c, copy in enumerate(fetch):
        copy.wait()
        product = jnp.dot(
            rolled_ref[...],
            weight_ref[:, c * WEIGHT_TILE : (c + 1) * WEIGHT_TILE],
            preferred_element_type=jnp.float32,
        ).astype(jnp.bfloat16)
        piece, place = divmod(c * WEIGHT_TILE, WIDTH)
        for k in range(4):
            part_refs[piece * 4 + k][:, place : place + WEIGHT_TILE] = product[64 * k : 64 * k + 64]


PARTS = [jax.ShapeDtypeStruct((64, WIDTH), jnp.bfloat16)] * 8


def weight_scratch(weight):
    return [pltpu.VMEM((weight.shape[0], 2 * WIDTH), weight.dtype), pltpu.SemaphoreType.DMA((WEIGHT_PARTS,))]


def merge_kernel(place_ref, first_ref, second_ref, ret_ref, weight_hbm, out_ref, rolled_ref, *refs):
    part_refs, (weight_ref, weight_sem) = refs[:8], refs[8:]
    fetch = fetch_weight(weight_hbm, weight_ref, weight_sem, 0)
    out_ref[0:FIRST] = first_ref[...]
    out_ref[FIRST:STAYING] = second_ref[0 : STAYING - FIRST]
    for j in range(MIGRANTS):
        out_ref[STAYING + j] = ret_ref[place_ref[j]].reshape(8, 2, HEAD)
    zi = lax.axis_index("tensor") // 2
    for z in range(4):
        place = pl.multiple_of(lax.rem(z - zi + 4, 4) * 64, 64)
        for h in range(8):
            rolled_ref[pl.ds(place, 64), h * HEAD : (h + 1) * HEAD] = out_ref[32 * z : 32 * z + 32, h].reshape(64, HEAD)
    project_rolled(rolled_ref, weight_ref, fetch, part_refs)


def merge_project(places, first, second, returned, weight):
    out = pl.pallas_call(
        merge_kernel,
        out_shape=[
            jax.ShapeDtypeStruct((ROWS, 8, 2, HEAD), jnp.bfloat16),
            jax.ShapeDtypeStruct((2 * ROWS, 8 * HEAD), jnp.bfloat16),
        ]
        + PARTS,
        in_specs=[SMEM, VMEM, VMEM, VMEM, HBM],
        out_specs=[VMEM] * 10,
        scratch_shapes=weight_scratch(weight),
        compiler_params=PARAMS,
        cost_estimate=pl.CostEstimate(flops=5 * 10**9, bytes_accessed=8 * 2**20, transcendentals=0),
        name="merge_project",
    )(places, first, second, returned, weight)
    return out[0], out[1], out[2:]


def project_kernel(rolled_ref, weight_hbm, *refs):
    part_refs, (weight_ref, weight_sem) = refs[:8], refs[8:]
    project_rolled(rolled_ref, weight_ref, fetch_weight(weight_hbm, weight_ref, weight_sem, 2 * WIDTH), part_refs)


def project(rolled, weight):
    return pl.pallas_call(
        project_kernel,
        out_shape=PARTS,
        in_specs=[VMEM, HBM],
        out_specs=[VMEM] * 8,
        scratch_shapes=weight_scratch(weight),
        compiler_params=PARAMS,
        cost_estimate=pl.CostEstimate(flops=5 * 10**9, bytes_accessed=8 * 2**20, transcendentals=0),
        name="project_rest",
    )(rolled, weight)


def request_kernel(
    offset_ref, order_ref, table_ref, length_ref, query_ref, fresh_ref, out_ref, slot_ref, used
):
    own = lax.axis_index("replica")
    out_ref[...] = jnp.zeros_like(out_ref)
    for s in range(REPLICAS):
        used[s] = 0
    lane = lax.broadcasted_iota(jnp.int32, (1, HEAD), 1)
    for j in range(MIGRANTS):
        row = STAYING + j
        source = lax.rem(own + 1 + offset_ref[0, j], REPLICAS)
        rank = used[source]
        used[source] = rank + 1
        slot = source * CAP + rank
        slot_ref[j] = slot
        meta = jnp.zeros((1, HEAD), jnp.int32)
        for p in range(PAGES_ROW):
            meta = jnp.where(lane == p, table_ref[p, row], meta)
        for c in range(COPIED):
            wanted = table_ref[order_ref[j, 0, c], row]
            meta = jnp.where(lane == PAGES_ROW + c, wanted, meta)
        length = length_ref[0, row]
        meta = jnp.where(lane == 20, length // 32, meta)
        meta = jnp.where(lane == 21, lax.rem(length, 32), meta)
        out_ref[slot, 0:16] = query_ref[row].reshape(16, HEAD)
        out_ref[slot, 16:32] = jnp.concatenate(
            [
                fresh_ref[row].astype(jnp.float32).reshape(4, HEAD),
                meta.astype(jnp.float32),
                jnp.zeros((11, HEAD), jnp.float32),
            ],
            axis=0,
        ).astype(jnp.bfloat16)


def request(offsets, order, table, lengths, query, fresh):
    return pl.pallas_call(
        request_kernel,
        out_shape=(
            jax.ShapeDtypeStruct((SLOTS, 32, HEAD), jnp.bfloat16),
            jax.ShapeDtypeStruct((MIGRANTS,), jnp.int32),
        ),
        in_specs=[SMEM] * 4 + [VMEM] * 2,
        out_specs=(VMEM, SMEM),
        scratch_shapes=[pltpu.SMEM((REPLICAS,), jnp.int32)],
        compiler_params=PARAMS,
        name="pack_requests",
    )(offsets, order, table, lengths, query, fresh)


def serve_kernel(
    got_ref, after_ref, pool_hbm, ret_ref, meta_ref, pool_ref, scores_ref, pool_sem, meta_vmem, active, meta_sem
):
    fetch = fetch_pool(pool_hbm, pool_ref, pool_sem)
    for slot in range(SLOTS):
        meta_vmem[slot : slot + 1] = got_ref[slot, 16:32].astype(jnp.float32)[META_ROW : META_ROW + 1].astype(jnp.int32)
    meta_copy = pltpu.make_async_copy(meta_vmem, meta_ref, meta_sem)
    meta_copy.start()
    ret_ref[...] = jnp.zeros_like(ret_ref)
    for i in range(SLOTS + GROUP):
        active[i] = 0
    meta_copy.wait()

    def collect(slot, count):
        used = meta_ref[slot, 20] + meta_ref[slot, 21] > 0

        @pl.when(used)
        def _():
            active[count] = slot

        return count + jnp.where(used, 1, 0)

    count = lax.fori_loop(0, SLOTS, collect, 0)
    for copy in fetch:
        copy.wait()

    def group(g, carry):
        slots = [active[g * GROUP + i] for i in range(GROUP)]
        outputs = attend_group(
            [got_ref[slot, 0:16] for slot in slots],
            [got_ref[slot, 16:32].astype(jnp.float32)[0:8] for slot in slots],
            [[meta_ref[slot, p] for p in range(PAGES_ROW)] for slot in slots],
            [meta_ref[slot, 20] * 32 + meta_ref[slot, 21] for slot in slots],
            pool_ref,
            scores_ref,
        )
        for slot, output in zip(slots, outputs):
            ret_ref[slot] = output
        return carry

    lax.fori_loop(0, (count + GROUP - 1) // GROUP, group, 0)


def serve(got, after, pool):
    return pl.pallas_call(
        serve_kernel,
        out_shape=(
            jax.ShapeDtypeStruct((SLOTS, 16, HEAD), jnp.bfloat16),
            jax.ShapeDtypeStruct((SLOTS, HEAD), jnp.int32),
        ),
        in_specs=[VMEM, HBM, HBM],
        out_specs=(VMEM, SMEM),
        scratch_shapes=attention_scratch(pool)
        + [
            pltpu.VMEM((SLOTS, HEAD), jnp.int32),
            pltpu.SMEM((SLOTS + GROUP,), jnp.int32),
            pltpu.SemaphoreType.DMA,
        ],
        compiler_params=PARAMS,
        cost_estimate=pl.CostEstimate(flops=6 * 10**9, bytes_accessed=8 * 2**20, transcendentals=0),
        name="serve_requests",
    )(got, after, pool)


def pick_kernel(slot_ref, got_ref, out_ref, held, in_sem, out_sem):
    loads = [
        pltpu.make_async_copy(got_ref.at[slot_ref[j]], held.at[j], in_sem.at[j]) for j in range(MIGRANTS)
    ]
    stores = [pltpu.make_async_copy(held.at[j], out_ref.at[j], out_sem.at[j]) for j in range(MIGRANTS)]
    for load in loads:
        load.start()
    for load, store in zip(loads, stores):
        load.wait()
        store.start()
    for store in stores:
        store.wait()


def pick(slots, got):
    shape = (MIGRANTS, COPIED, 2, PAGE, HEAD)
    return pl.pallas_call(
        pick_kernel,
        out_shape=jax.ShapeDtypeStruct(shape, jnp.bfloat16),
        in_specs=[SMEM, HBM],
        out_specs=HBM,
        scratch_shapes=[
            pltpu.VMEM(shape, jnp.bfloat16),
            pltpu.SemaphoreType.DMA((MIGRANTS,)),
            pltpu.SemaphoreType.DMA((MIGRANTS,)),
        ],
        compiler_params=PARAMS,
        name="pick_pages",
    )(slots, got)


def shift_z(value, by):
    pairs = [(z * 2 + x, (z + by) % 4 * 2 + x) for z in range(4) for x in range(2)]
    return lax.ppermute(value, "tensor", pairs)


def swap_x(value):
    return lax.ppermute(value, "tensor", [(t, t ^ 1) for t in range(8)])


def f32_sum(*terms):
    return functools.reduce(jnp.add, [term.astype(jnp.float32) for term in terms])


def reduce_z(here, up, far, down, piece):
    if piece == 0:
        up = f32_sum(up, shift_z(far, 1)).astype(jnp.bfloat16)
    else:
        down = f32_sum(down, shift_z(far, -1)).astype(jnp.bfloat16)
    return f32_sum(here, shift_z(up, 1), shift_z(down, -1))


def body(
    queries,
    step_key_value,
    replica_page_store,
    page_table,
    lengths,
    mig_offset,
    copy_order,
    out_weight,
):
    xi = lax.axis_index("tensor") % 2
    pool = replica_page_store[0]
    query = queries[0].reshape(ROWS, 2, 8, HEAD).transpose(0, 2, 1, 3)
    fresh = step_key_value[0]
    table = page_table[0].T
    payload, slots = request(
        mig_offset[:, :, 0], copy_order.transpose(1, 0, 2), table, lengths, query, fresh
    )
    got = lax.all_to_all(
        payload.reshape(REPLICAS, CAP, 32, HEAD), "replica", split_axis=0, concat_axis=0, tiled=True
    ).reshape(SLOTS, 32, HEAD)
    first = stay(table, lengths, query, fresh, pool, FIRST)
    answered, meta = serve(got, first, pool)
    returned = lax.all_to_all(
        answered.reshape(REPLICAS, CAP, 16, HEAD), "replica", split_axis=0, concat_axis=0, tiled=True
    ).reshape(SLOTS, 16, HEAD)
    second, sending = attend_second(meta, table, lengths, query, fresh, pool)
    incoming = lax.all_to_all(
        sending.reshape(REPLICAS, CAP, COPIED, 2, PAGE, HEAD),
        "replica",
        split_axis=0,
        concat_axis=0,
        tiled=True,
    ).reshape(SLOTS, COPIED, 2, PAGE, HEAD)
    merged, rolled, parts = merge_project(slots, first, second, returned, out_weight)
    parts = list(parts) + list(project(rolled, out_weight))
    finished = []
    for piece in range(4):
        total = reduce_z(*parts[piece * 4 : piece * 4 + 4], piece % 2).reshape(2, 32, WIDTH)
        mine = lax.dynamic_index_in_dim(total, xi, 0, keepdims=False)
        other = lax.dynamic_index_in_dim(total, 1 - xi, 0, keepdims=False)
        finished.append((mine + swap_x(other.astype(jnp.bfloat16)).astype(jnp.float32)).astype(jnp.bfloat16))
    projected = jnp.concatenate(finished, axis=1).reshape(16, 2, -1)
    arrived = pick(slots, incoming)
    attention = merged.transpose(0, 2, 1, 3).reshape(ROWS, 2, 8 * HEAD)
    return (attention[None], projected[None], arrived[None])


def solution(mesh):
    placed = (
        P("replica", None, None, "tensor"),
        P("replica", None, None, None, "tensor"),
        P("replica", None, None, None, "tensor"),
        P("replica", None, None),
        P("replica", None),
        P("replica", None, None),
        P("replica", None, None),
        P("tensor", None),
    )
    return jax.shard_map(
        body,
        mesh=mesh,
        in_specs=placed,
        out_specs=(
            P("replica", None, None, "tensor"),
            P("replica", "tensor", None, None),
            P("replica", None, None, None, None, "tensor"),
        ),
        check_vma=False,
    )
```

time: 178 us -> 132 us (0.74)
  local copies, waits for them, and re-layouts: 22.1 us -> 2.59 us
  Pallas kernels: 66.5 us -> 47.7 us
  waiting for transfers between devices: 37.6 us -> 33.4 us
    unnamed x46 -> x16, local copies, waits for them, and re-layouts: 17.7 us -> 1.36 us
    pallas_call x7 -> x4, Pallas kernels: 52.6 us -> 36.5 us  [the longest x1 12 us: stay(): pl.pallas_call(stay_kernel, out_shape=jax.ShapeDtypeStruct((count, 8, 2,...]
    ppermute x4, waiting for transfers between devices: 25.5 us -> 16.8 us  [swap_x(): return lax.ppermute(value, 'tensor', [(t, t ^ 1) for t in range(8)])]
    ppermute x12, waiting for transfers between devices: 9.23 us -> 16.6 us  [shift_z(): return lax.ppermute(value, 'tensor', pairs)]
    ppermute x4, starting transfers between devices: 7.25 us -> 4.29 us  [swap_x(): return lax.ppermute(value, 'tensor', [(t, t ^ 1) for t in range(8)])]
    all_to_all x1, waiting for transfers between devices: 2.85 us -> 0.01 us  [body(): lax.all_to_all(answered.reshape(REPLICAS, CAP, 16, HEAD), 'replica', spli...]
    another operation x1 -> x0, local copies, waits for them, and re-layouts: 2.17 us -> none  [body(): query = queries[0].reshape(ROWS, 16, HEAD)]
  transfers between devices with their start and end apart: 19 -> 19, of which waited for: 6 -> 8; matrix products, arithmetic and copies ran while one was open for 2% -> 3% of each run, Pallas kernels for 34% -> 28%
where the time goes in v2:
time: 132 us
  Pallas kernels  47.7 us (36%)
  starting transfers between devices  44.3 us (34%)
  waiting for transfers between devices  33.4 us (25%)
  other arithmetic  2.67 us (2%)
  local copies, waits for them, and re-layouts  2.59 us (2%)
    ppermute x12, starting transfers between devices, shift_z(): return lax.ppermute(value, 'tensor', pairs)  19.1 us
    ppermute x4, waiting for transfers between devices, swap_x(): return lax.ppermute(value, 'tensor', [(t, t ^ 1) for t in range(8)])  16.8 us
    ppermute x12, waiting for transfers between devices, shift_z(): return lax.ppermute(value, 'tensor', pairs)  16.6 us
    pallas_call x1, Pallas kernels, stay(): pl.pallas_call(stay_kernel, out_shape=jax.ShapeDtypeStruct((count, 8, 2,...  12 us
    pallas_call x1, Pallas kernels, attend_second(): pl.pallas_call(second_kernel, out_shape=(jax.ShapeDtypeStruct((120 - FIRS...  11.4 us
    all_to_all x1, starting transfers between devices, body(): lax.all_to_all(answered.reshape(REPLICAS, CAP, 16, HEAD), 'replica', spli...  7.24 us
    all_to_all x1, starting transfers between devices, body(): lax.all_to_all(sending.reshape(REPLICAS, CAP, COPIED, 2, PAGE, HEAD), 're...  7.23 us
    pallas_call x1, Pallas kernels, merge_project(): pl.pallas_call(merge_kernel, out_shape=[jax.ShapeDtypeStruct((ROWS, 8, 2,...  6.53 us
  transfers between devices with their start and end apart: 19, of which 8 were waited for; matrix products, arithmetic and copies ran while one was open for 3% of the time, Pallas kernels for 28%

profile of v2, /device:TPU:10, one launch (start us, length us, event | category | flops | bytes accessed | tf_op | source)
XLA Modules:
  0.0 131.7 jit_solution(10938661261719950257)
XLA Ops:
  0.6 2.1 %pack_requests.1 = (bf16[32,32,128]{2,1,0:T(8,128)(2,1)}, s32[14]{0:T(128)}) custom-call(s32[1,14]{1,0:T(1,128)} %bitcast.72, s32[14,1,16]{2,1,0:T(1,128)} %bitcast.71, s32[16,128]{1,0:T(8,128)} %bitcast.68, s32[1,128]{1,0:T(1,128)} %length_ref.5, bf16[128,8,2,128]{3,2,1,0:T(2,128)(2,1)} %bitcast.58, bf16[128,2,2,128]{3,2,1,0:T(2,128)(2,1)} %bitcast.65), custom_call_target="tpu_custom_call" | custom-call | tf_op jit(solution)/shard_map/pack_requests/pallas_call | solution.py:289
  2.8 6.5 %all-to-all-start = ((bf16[16,2,32,128]{3,2,1,0:T(8,128)(2,1)}), bf16[16,2,32,128]{3,2,1,0:T(8,128)(2,1)S(1)}, u32[]{:S(2)}, u32[]{:S(2)}) async-start(bf16[16,2,32,128]{3,2,1,0:T(8,128)(2,1)} %bitcast.62), calls=%async_computation | async-start | bytes 524288 | tf_op jit(solution)/shard_map/all_to_all | solution.py:437
  9.3 12.0 %attend_first.1.after_ref.first_ref = bf16[64,8,2,128]{3,2,1,0:T(2,128)(2,1)} custom-call(s32[16,128]{1,0:T(8,128)} %bitcast.69, s32[1,128]{1,0:T(1,128)} %length_ref.5, bf16[128,8,2,128]{3,2,1,0:T(2,128)(2,1)} %bitcast.59, bf16[128,2,2,128]{3,2,1,0:T(2,128)(2,1)} %bitcast.66, bf16[2,128,64,128]{3,2,1,0:T(8,128)(2,1)} %bitcast.73), custom_call_target="tpu_custom_call" | custom-call | flops 8000000000 | bytes 8388608 | tf_op jit(solution)/shard_map/attend_first/pallas_call | solution.py:121
  21.3 0.0 all-to-all-done
  21.3 0.0 copy-start.6
  21.3 0.7 copy-done.6
  22.0 6.0 %serve_requests.1 = (bf16[32,16,128]{2,1,0:T(8,128)(2,1)}, s32[32,128]{1,0:T(8,128)}) custom-call(bf16[32,32,128]{2,1,0:T(8,128)(2,1)} %bitcast.61, bf16[64,8,2,128]{3,2,1,0:T(2,128)(2,1)} %attend_first.1.after_ref.first_ref, bf16[2,128,64,128]{3,2,1,0:T(8,128)(2,1)} %bitcast.74), custom_call_target="tpu_custom_call" | custom-call | flops 6000000000 | bytes 8388608 | tf_op jit(solution)/shard_map/serve_requests/pallas_call | solution.py:347
  28.0 7.2 %all-to-all-start.1 = ((bf16[16,2,16,128]{3,2,1,0:T(8,128)(2,1)}), bf16[16,2,16,128]{3,2,1,0:T(8,128)(2,1)S(1)}, u32[]{:S(2)}, u32[]{:S(2)}) async-start(bf16[16,2,16,128]{3,2,1,0:T(8,128)(2,1)} %bitcast.64), calls=%async_computation.1 | async-start | bytes 262144 | tf_op jit(solution)/shard_map/all_to_all | solution.py:442
  35.2 11.4 %attend_second.1 = (bf16[56,8,2,128]{3,2,1,0:T(2,128)(2,1)}, bf16[32,4,2,64,128]{4,3,2,1,0:T(8,128)(2,1)}) custom-call(s32[32,128]{1,0:T(8,128)} %get-tuple-element.29.meta_ref, s32[16,128]{1,0:T(8,128)} %bitcast.70, s32[1,128]{1,0:T(1,128)} %length_ref.5, bf16[128,8,2,128]{3,2,1,0:T(2,128)(2,1)} %bitcast.60, bf16[128,2,2,128]{3,2,1,0:T(2,128)(2,1)} %bitcast.67, ...), custom_call_target="tpu_custom_call" | custom-call | flops 8000000000 | bytes 8388608 | tf_op jit(solution)/shard_map/attend_second/pallas_call | solution.py:167
  46.7 0.6 copy-done.7
  47.3 7.2 %all-to-all-start.2 = ((bf16[16,2,4,2,64,128]{5,4,3,2,1,0:T(8,128)(2,1)}), bf16[16,2,4,2,64,128]{5,4,3,2,1,0:T(8,128)(2,1)}, u32[]{:S(2)}, u32[]{:S(2)}) async-start(bf16[16,2,4,2,64,128]{5,4,3,2,1,0:T(8,128)(2,1)} %bitcast.48), calls=%async_computation.2 | async-start | bytes 8388608 | tf_op jit(solution)/shard_map/all_to_all | solution.py:446
  54.5 6.5 %merge_project.1 = (bf16[128,8,2,128]{3,2,1,0:T(2,128)(2,1)}, bf16[256,1024]{1,0:T(8,128)(2,1)}, bf16[64,2048]{1,0:T(8,128)(2,1)}, bf16[64,2048]{1,0:T(8,128)(2,...) custom-call(s32[14]{0:T(128)} %get-tuple-element.27.place_ref.slot_r, ...), custom_call_target="tpu_custom_call" | custom-call | flops 5000000000 | bytes 8388608 | tf_op jit(solution)/shard_map/merge_project/pallas_call | solution.py:218
  61.1 2.0 %collective-permute-start = (bf16[64,2048]{1,0:T(8,128)(2,1)}, bf16[64,2048]{1,0:T(8,128)(2,1)S(1)}, u32[]{:S(2)}, u32[]{:S(2)}) collective-permute-start(bf16[64,2048]{1,0:T(8,128)(2,1)} %get-tuple-element.35), channel_id=1, source_target_pairs={{0,2},{1,3},{2,4},{3,5},{4,6},{5,7},{6,0},{7,1},{8,10},{9,11},{10,... | collective-permute-start | bytes 786440 | tf_op jit(solution)/shard_map/ppermute | solution.py:400
  63.1 2.2 %collective-permute-start.2 = (bf16[64,2048]{1,0:T(8,128)(2,1)}, bf16[64,2048]{1,0:T(8,128)(2,1)S(1)}, u32[]{:S(2)}, u32[]{:S(2)}) collective-permute-start(bf16[64,2048]{1,0:T(8,128)(2,1)} %get-tuple-element.36), channel_id=1, source_target_pairs={{0,6},{1,7},{2,0},{3,1},{4,2},{5,3},{6,4},{7,5},{8,14},{9,15},{10,... | collective-permute-start | bytes 786440 | tf_op jit(solution)/shard_map/ppermute | solution.py:400
  65.3 3.2 %collective-permute-start.5 = (bf16[64,2048]{1,0:T(8,128)(2,1)}, bf16[64,2048]{1,0:T(8,128)(2,1)S(1)}, u32[]{:S(2)}, u32[]{:S(2)}) collective-permute-start(bf16[64,2048]{1,0:T(8,128)(2,1)} %get-tuple-element.40), channel_id=1, source_target_pairs={{0,6},{1,7},{2,0},{3,1},{4,2},{5,3},{6,4},{7,5},{8,14},{9,15},{10,... | collective-permute-start | bytes 786440 | tf_op jit(solution)/shard_map/ppermute | solution.py:400
  68.5 6.5 %project_rest.1 = (bf16[64,2048]{1,0:T(8,128)(2,1)}, bf16[64,2048]{1,0:T(8,128)(2,1)}, bf16[64,2048]{1,0:T(8,128)(2,1)}, bf16[64,2048]{1,0:T(8,128)(2,1)}, bf16[...) custom-call(bf16[256,1024]{1,0:T(8,128)(2,1)} %get-tuple-element.41.rolled_, ...), custom_call_target="tpu_custom_call" | custom-call | flops 5000000000 | bytes 8388608 | tf_op jit(solution)/shard_map/project_rest/pallas_call | solution.py:241
  75.0 0.0 copy-start.2
  75.1 0.1 collective-permute-start.8
  75.1 0.0 collective-permute-done
  75.1 3.2 %collective-permute-start.10 = (bf16[64,2048]{1,0:T(8,128)(2,1)}, bf16[64,2048]{1,0:T(8,128)(2,1)S(1)}, u32[]{:S(2)}, u32[]{:S(2)}) collective-permute-start(bf16[64,2048]{1,0:T(8,128)(2,1)} %get-tuple-element.45), channel_id=1, source_target_pairs={{0,6},{1,7},{2,0},{3,1},{4,2},{5,3},{6,4},{7,5},{8,14},{9,15},{10,... | collective-permute-start | bytes 786440 | tf_op jit(solution)/shard_map/ppermute | solution.py:400
  78.4 0.1 add_convert_fusion.3
  78.4 0.0 collective-permute-done.5
  78.4 1.6 %collective-permute-start.12 = (bf16[64,2048]{1,0:T(8,128)(2,1)}, bf16[64,2048]{1,0:T(8,128)(2,1)S(1)}, u32[]{:S(2)}, u32[]{:S(2)}) collective-permute-start(bf16[64,2048]{1,0:T(8,128)(2,1)} %get-tuple-element.47), channel_id=1, source_target_pairs={{0,2},{1,3},{2,4},{3,5},{4,6},{5,7},{6,0},{7,1},{8,10},{9,11},{10,... | collective-permute-start | bytes 786440 | tf_op jit(solution)/shard_map/ppermute | solution.py:400
  80.0 0.1 add_convert_fusion.2
  80.1 5.7 %collective-permute-done.8 = bf16[64,2048]{1,0:T(8,128)(2,1)S(1)} collective-permute-done((bf16[64,2048]{1,0:T(8,128)(2,1)}, bf16[64,2048]{1,0:T(8,128)(2,1)S(1)}, u32[]{:S(2)}, u32[]{:S(2)}) %collective-permute-start.8) | collective-permute-done | bytes 262176 | tf_op jit(solution)/shard_map/ppermute | solution.py:400
  85.8 0.0 collective-permute-start.13
  85.8 1.0 add_convert_fusion.1
  86.8 5.6 %collective-permute-done.13 = bf16[64,2048]{1,0:T(8,128)(2,1)S(1)} collective-permute-done((bf16[64,2048]{1,0:T(8,128)(2,1)}, bf16[64,2048]{1,0:T(8,128)(2,1)S(1)}, u32[]{:S(2)}, u32[]{:S(2)}) %collective-permute-start.13) | collective-permute-done | bytes 262176 | tf_op jit(solution)/shard_map/ppermute | solution.py:400
  92.4 0.0 collective-permute-start.1
  92.4 1.0 add_convert_fusion
  93.4 3.5 %collective-permute-start.6 = (bf16[64,2048]{1,0:T(8,128)(2,1)S(1)}, bf16[64,2048]{1,0:T(8,128)(2,1)S(1)}, u32[]{:S(2)}, u32[]{:S(2)}) collective-permute-start(bf16[64,2048]{1,0:T(8,128)(2,1)S(1)} %add_convert_fusion.2), channel_id=1, source_target_pairs={{0,6},{1,7},{2,0},{3,1},{4,2},{5,3},{6,4},{7,5},{8,14},{9,15},{10,... | collective-permute-start | bytes 786440 | tf_op jit(solution)/shard_map/ppermute | solution.py:400
  96.9 3.4 %collective-permute-done.1 = bf16[64,2048]{1,0:T(8,128)(2,1)S(1)} collective-permute-done((bf16[64,2048]{1,0:T(8,128)(2,1)S(1)}, bf16[64,2048]{1,0:T(8,128)(2,1)S(1)}, u32[]{:S(2)}, u32[]{:S(2)}) %collective-permute-start.1) | collective-permute-done | bytes 262176 | tf_op jit(solution)/shard_map/ppermute | solution.py:400
  100.3 0.1 convert_add_fusion.3
  100.4 3.3 %collective-permute-start.14 = (bf16[64,2048]{1,0:T(8,128)(2,1)S(1)}, bf16[64,2048]{1,0:T(8,128)(2,1)S(1)}, u32[]{:S(2)}, u32[]{:S(2)}) collective-permute-start(bf16[64,2048]{1,0:T(8,128)(2,1)S(1)} %add_convert_fusion), channel_id=1, source_target_pairs={{0,6},{1,7},{2,0},{3,1},{4,2},{5,3},{6,4},{7,5},{8,14},{9,15},{10,... | collective-permute-start | bytes 786440 | tf_op jit(solution)/shard_map/ppermute | solution.py:400
  103.7 1.4 %collective-permute-start.3 = (bf16[32,2048]{1,0:T(8,128)(2,1)S(1)}, bf16[32,2048]{1,0:T(8,128)(2,1)S(1)}, u32[]{:S(2)}, u32[]{:S(2)}) collective-permute-start(bf16[32,2048]{1,0:T(8,128)(2,1)S(1)} %fusion.4), channel_id=1, source_target_pairs={{0,1},{1,0},{2,3},{3,2},{4,5},{5,4},{6,7},{7,6},{8,9},{9,8},{10,11... | collective-permute-start | bytes 393224 | tf_op jit(solution)/shard_map/ppermute | solution.py:404
  105.2 0.1 convert_add_fusion.2
  105.3 0.7 collective-permute-start.7
  106.0 1.9 %collective-permute-done.9 = bf16[64,2048]{1,0:T(8,128)(2,1)S(1)} collective-permute-done((bf16[64,2048]{1,0:T(8,128)(2,1)S(1)}, bf16[64,2048]{1,0:T(8,128)(2,1)S(1)}, u32[]{:S(2)}, u32[]{:S(2)}) %collective-permute-start.9) | collective-permute-done | bytes 262176 | tf_op jit(solution)/shard_map/ppermute | solution.py:400
  107.9 0.1 convert_add_fusion.1
  108.0 1.5 %collective-permute-start.11 = (bf16[32,2048]{1,0:T(8,128)(2,1)S(1)}, bf16[32,2048]{1,0:T(8,128)(2,1)S(1)}, u32[]{:S(2)}, u32[]{:S(2)}) collective-permute-start(bf16[32,2048]{1,0:T(8,128)(2,1)S(1)} %fusion.6), channel_id=1, source_target_pairs={{0,1},{1,0},{2,3},{3,2},{4,5},{5,4},{6,7},{7,6},{8,9},{9,8},{10,11... | collective-permute-start | bytes 393224 | tf_op jit(solution)/shard_map/ppermute | solution.py:404
  109.5 0.1 convert_add_fusion
  109.7 0.7 collective-permute-start.15
  110.3 9.0 %collective-permute-done.3 = bf16[32,2048]{1,0:T(8,128)(2,1)S(1)} collective-permute-done((bf16[32,2048]{1,0:T(8,128)(2,1)S(1)}, bf16[32,2048]{1,0:T(8,128)(2,1)S(1)}, u32[]{:S(2)}, u32[]{:S(2)}) %collective-permute-start.3) | collective-permute-done | bytes 131104 | tf_op jit(solution)/shard_map/ppermute | solution.py:404
  119.3 2.8 %collective-permute-done.7 = bf16[32,2048]{1,0:T(8,128)(2,1)S(1)} collective-permute-done((bf16[32,2048]{1,0:T(8,128)(2,1)S(1)}, bf16[32,2048]{1,0:T(8,128)(2,1)S(1)}, u32[]{:S(2)}, u32[]{:S(2)}) %collective-permute-start.7) | collective-permute-done | bytes 131104 | tf_op jit(solution)/shard_map/ppermute | solution.py:404
  122.1 2.8 %collective-permute-done.11 = bf16[32,2048]{1,0:T(8,128)(2,1)S(1)} collective-permute-done((bf16[32,2048]{1,0:T(8,128)(2,1)S(1)}, bf16[32,2048]{1,0:T(8,128)(2,1)S(1)}, u32[]{:S(2)}, u32[]{:S(2)}) %collective-permute-start.11) | collective-permute-done | bytes 131104 | tf_op jit(solution)/shard_map/ppermute | solution.py:404
  125.0 2.3 %collective-permute-done.15 = bf16[32,2048]{1,0:T(8,128)(2,1)S(1)} collective-permute-done((bf16[32,2048]{1,0:T(8,128)(2,1)S(1)}, bf16[32,2048]{1,0:T(8,128)(2,1)S(1)}, u32[]{:S(2)}, u32[]{:S(2)}) %collective-permute-start.15) | collective-permute-done | bytes 131104 | tf_op jit(solution)/shard_map/ppermute | solution.py:404
  127.3 1.1 broadcast_in_dim_reshape.7
  128.5 3.1 %pick_pages.1 = bf16[14,4,2,64,128]{4,3,2,1,0:T(8,128)(2,1)} custom-call(s32[14]{0:T(128)} %get-tuple-element.27.place_ref.slot_ref, bf16[32,4,2,64,128]{4,3,2,1,0:T(8,128)(2,1)} %bitcast.29.got_ref), custom_call_target="tpu_custom_call" | custom-call | tf_op jit(solution)/shard_map/pick_pages/pallas_call | solution.py:383
  (31 shorter events, 0.3 us)
Async XLA Ops:
  2.8 18.5 %all-to-all-start = ((bf16[16,2,32,128]{3,2,1,0:T(8,128)(2,1)}), bf16[16,2,32,128]{3,2,1,0:T(8,128)(2,1)S(1)}, u32[]{:S(2)}, u32[]{:S(2)}) async-start(bf16[16,2,32,128]{3,2,1,0:T(8,128)(2,1)} %bitcast.62), calls=%async_computation | async-start | bytes 524288 | tf_op jit(solution)/shard_map/all_to_all | solution.py:437
  21.3 0.7 copy-start.6
  28.0 18.7 %all-to-all-start.1 = ((bf16[16,2,16,128]{3,2,1,0:T(8,128)(2,1)}), bf16[16,2,16,128]{3,2,1,0:T(8,128)(2,1)S(1)}, u32[]{:S(2)}, u32[]{:S(2)}) async-start(bf16[16,2,16,128]{3,2,1,0:T(8,128)(2,1)} %bitcast.64), calls=%async_computation.1 | async-start | bytes 262144 | tf_op jit(solution)/shard_map/all_to_all | solution.py:442
  46.7 0.6 copy-start.7
  47.3 81.2 %all-to-all-start.2 = ((bf16[16,2,4,2,64,128]{5,4,3,2,1,0:T(8,128)(2,1)}), bf16[16,2,4,2,64,128]{5,4,3,2,1,0:T(8,128)(2,1)}, u32[]{:S(2)}, u32[]{:S(2)}) async-start(bf16[16,2,4,2,64,128]{5,4,3,2,1,0:T(8,128)(2,1)} %bitcast.48), calls=%async_computation.2 | async-start | bytes 8388608 | tf_op jit(solution)/shard_map/all_to_all | solution.py:446
  61.1 14.1 %collective-permute-start = (bf16[64,2048]{1,0:T(8,128)(2,1)}, bf16[64,2048]{1,0:T(8,128)(2,1)S(1)}, u32[]{:S(2)}, u32[]{:S(2)}) collective-permute-start(bf16[64,2048]{1,0:T(8,128)(2,1)} %get-tuple-element.35), channel_id=1, source_target_pairs={{0,2},{1,3},{2,4},{3,5},{4,6},{5,7},{6,0},{7,1},{8,10},{9,11},{10,... | collective-permute-start | bytes 786440 | tf_op jit(solution)/shard_map/ppermute | solution.py:400
  63.1 30.3 %collective-permute-start.2 = (bf16[64,2048]{1,0:T(8,128)(2,1)}, bf16[64,2048]{1,0:T(8,128)(2,1)S(1)}, u32[]{:S(2)}, u32[]{:S(2)}) collective-permute-start(bf16[64,2048]{1,0:T(8,128)(2,1)} %get-tuple-element.36), channel_id=1, source_target_pairs={{0,6},{1,7},{2,0},{3,1},{4,2},{5,3},{6,4},{7,5},{8,14},{9,15},{10,... | collective-permute-start | bytes 786440 | tf_op jit(solution)/shard_map/ppermute | solution.py:400
  65.3 35.2 %collective-permute-start.4 = (bf16[64,2048]{1,0:T(8,128)(2,1)}, bf16[64,2048]{1,0:T(8,128)(2,1)S(1)}, u32[]{:S(2)}, u32[]{:S(2)}) collective-permute-start(bf16[64,2048]{1,0:T(8,128)(2,1)} %get-tuple-element.38), channel_id=1, source_target_pairs={{0,2},{1,3},{2,4},{3,5},{4,6},{5,7},{6,0},{7,1},{8,10},{9,11},{10,... | collective-permute-start | bytes 786440 | tf_op jit(solution)/shard_map/ppermute | solution.py:400
  65.3 13.2 %collective-permute-start.5 = (bf16[64,2048]{1,0:T(8,128)(2,1)}, bf16[64,2048]{1,0:T(8,128)(2,1)S(1)}, u32[]{:S(2)}, u32[]{:S(2)}) collective-permute-start(bf16[64,2048]{1,0:T(8,128)(2,1)} %get-tuple-element.40), channel_id=1, source_target_pairs={{0,6},{1,7},{2,0},{3,1},{4,2},{5,3},{6,4},{7,5},{8,14},{9,15},{10,... | collective-permute-start | bytes 786440 | tf_op jit(solution)/shard_map/ppermute | solution.py:400
  68.5 9.9 %copy-start.5 = (bf16[64,2048]{1,0:T(8,128)(2,1)S(1)}, bf16[64,2048]{1,0:T(8,128)(2,1)}, u32[]{:S(2)}) copy-start(bf16[64,2048]{1,0:T(8,128)(2,1)} %get-tuple-element.34) | copy-start | bytes 786436
  68.5 11.5 %copy-start.4 = (bf16[64,2048]{1,0:T(8,128)(2,1)S(1)}, bf16[64,2048]{1,0:T(8,128)(2,1)}, u32[]{:S(2)}) copy-start(bf16[64,2048]{1,0:T(8,128)(2,1)} %get-tuple-element.39) | copy-start | bytes 786436
  68.5 31.8 %copy-start.3 = (bf16[64,2048]{1,0:T(8,128)(2,1)S(1)}, bf16[64,2048]{1,0:T(8,128)(2,1)}, u32[]{:S(2)}) copy-start(bf16[64,2048]{1,0:T(8,128)(2,1)} %get-tuple-element.33) | copy-start | bytes 786436
  75.0 30.2 %copy-start.1 = (bf16[64,2048]{1,0:T(8,128)(2,1)S(1)}, bf16[64,2048]{1,0:T(8,128)(2,1)}, u32[]{:S(2)}) copy-start(bf16[64,2048]{1,0:T(8,128)(2,1)} %get-tuple-element.37) | copy-start | bytes 786436
  75.0 32.9 %copy-start.2 = (bf16[64,2048]{1,0:T(8,128)(2,1)S(1)}, bf16[64,2048]{1,0:T(8,128)(2,1)}, u32[]{:S(2)}) copy-start(bf16[64,2048]{1,0:T(8,128)(2,1)} %get-tuple-element.42) | copy-start | bytes 786436
  75.0 34.5 %copy-start = (bf16[64,2048]{1,0:T(8,128)(2,1)S(1)}, bf16[64,2048]{1,0:T(8,128)(2,1)}, u32[]{:S(2)}) copy-start(bf16[64,2048]{1,0:T(8,128)(2,1)} %get-tuple-element.46) | copy-start | bytes 786436
  75.1 10.7 %collective-permute-start.8 = (bf16[64,2048]{1,0:T(8,128)(2,1)}, bf16[64,2048]{1,0:T(8,128)(2,1)S(1)}, u32[]{:S(2)}, u32[]{:S(2)}) collective-permute-start(bf16[64,2048]{1,0:T(8,128)(2,1)} %get-tuple-element.44), channel_id=1, source_target_pairs={{0,2},{1,3},{2,4},{3,5},{4,6},{5,7},{6,0},{7,1},{8,10},{9,11},{10,... | collective-permute-start | bytes 786440 | tf_op jit(solution)/shard_map/ppermute | solution.py:400
  75.1 30.2 %collective-permute-start.10 = (bf16[64,2048]{1,0:T(8,128)(2,1)}, bf16[64,2048]{1,0:T(8,128)(2,1)S(1)}, u32[]{:S(2)}, u32[]{:S(2)}) collective-permute-start(bf16[64,2048]{1,0:T(8,128)(2,1)} %get-tuple-element.45), channel_id=1, source_target_pairs={{0,6},{1,7},{2,0},{3,1},{4,2},{5,3},{6,4},{7,5},{8,14},{9,15},{10,... | collective-permute-start | bytes 786440 | tf_op jit(solution)/shard_map/ppermute | solution.py:400
  78.4 31.1 %collective-permute-start.12 = (bf16[64,2048]{1,0:T(8,128)(2,1)}, bf16[64,2048]{1,0:T(8,128)(2,1)S(1)}, u32[]{:S(2)}, u32[]{:S(2)}) collective-permute-start(bf16[64,2048]{1,0:T(8,128)(2,1)} %get-tuple-element.47), channel_id=1, source_target_pairs={{0,2},{1,3},{2,4},{3,5},{4,6},{5,7},{6,0},{7,1},{8,10},{9,11},{10,... | collective-permute-start | bytes 786440 | tf_op jit(solution)/shard_map/ppermute | solution.py:400
  85.8 6.6 %collective-permute-start.13 = (bf16[64,2048]{1,0:T(8,128)(2,1)}, bf16[64,2048]{1,0:T(8,128)(2,1)S(1)}, u32[]{:S(2)}, u32[]{:S(2)}) collective-permute-start(bf16[64,2048]{1,0:T(8,128)(2,1)} %get-tuple-element.49), channel_id=1, source_target_pairs={{0,6},{1,7},{2,0},{3,1},{4,2},{5,3},{6,4},{7,5},{8,14},{9,15},{10,... | collective-permute-start | bytes 786440 | tf_op jit(solution)/shard_map/ppermute | solution.py:400
  92.4 7.9 %collective-permute-start.1 = (bf16[64,2048]{1,0:T(8,128)(2,1)S(1)}, bf16[64,2048]{1,0:T(8,128)(2,1)S(1)}, u32[]{:S(2)}, u32[]{:S(2)}) collective-permute-start(bf16[64,2048]{1,0:T(8,128)(2,1)S(1)} %add_convert_fusion.3), channel_id=1, source_target_pairs={{0,2},{1,3},{2,4},{3,5},{4,6},{5,7},{6,0},{7,1},{8,10},{9,11},{10,... | collective-permute-start | bytes 786440 | tf_op jit(solution)/shard_map/ppermute | solution.py:400
  93.4 10.3 %collective-permute-start.6 = (bf16[64,2048]{1,0:T(8,128)(2,1)S(1)}, bf16[64,2048]{1,0:T(8,128)(2,1)S(1)}, u32[]{:S(2)}, u32[]{:S(2)}) collective-permute-start(bf16[64,2048]{1,0:T(8,128)(2,1)S(1)} %add_convert_fusion.2), channel_id=1, source_target_pairs={{0,6},{1,7},{2,0},{3,1},{4,2},{5,3},{6,4},{7,5},{8,14},{9,15},{10,... | collective-permute-start | bytes 786440 | tf_op jit(solution)/shard_map/ppermute | solution.py:400
  100.3 7.6 %collective-permute-start.9 = (bf16[64,2048]{1,0:T(8,128)(2,1)S(1)}, bf16[64,2048]{1,0:T(8,128)(2,1)S(1)}, u32[]{:S(2)}, u32[]{:S(2)}) collective-permute-start(bf16[64,2048]{1,0:T(8,128)(2,1)S(1)} %add_convert_fusion.1), channel_id=1, source_target_pairs={{0,2},{1,3},{2,4},{3,5},{4,6},{5,7},{6,0},{7,1},{8,10},{9,11},{10,... | collective-permute-start | bytes 786440 | tf_op jit(solution)/shard_map/ppermute | solution.py:400
  100.4 9.1 %collective-permute-start.14 = (bf16[64,2048]{1,0:T(8,128)(2,1)S(1)}, bf16[64,2048]{1,0:T(8,128)(2,1)S(1)}, u32[]{:S(2)}, u32[]{:S(2)}) collective-permute-start(bf16[64,2048]{1,0:T(8,128)(2,1)S(1)} %add_convert_fusion), channel_id=1, source_target_pairs={{0,6},{1,7},{2,0},{3,1},{4,2},{5,3},{6,4},{7,5},{8,14},{9,15},{10,... | collective-permute-start | bytes 786440 | tf_op jit(solution)/shard_map/ppermute | solution.py:400
  103.7 15.6 %collective-permute-start.3 = (bf16[32,2048]{1,0:T(8,128)(2,1)S(1)}, bf16[32,2048]{1,0:T(8,128)(2,1)S(1)}, u32[]{:S(2)}, u32[]{:S(2)}) collective-permute-start(bf16[32,2048]{1,0:T(8,128)(2,1)S(1)} %fusion.4), channel_id=1, source_target_pairs={{0,1},{1,0},{2,3},{3,2},{4,5},{5,4},{6,7},{7,6},{8,9},{9,8},{10,11... | collective-permute-start | bytes 393224 | tf_op jit(solution)/shard_map/ppermute | solution.py:404
  105.3 16.8 %collective-permute-start.7 = (bf16[32,2048]{1,0:T(8,128)(2,1)S(1)}, bf16[32,2048]{1,0:T(8,128)(2,1)S(1)}, u32[]{:S(2)}, u32[]{:S(2)}) collective-permute-start(bf16[32,2048]{1,0:T(8,128)(2,1)S(1)} %fusion.5), channel_id=1, source_target_pairs={{0,1},{1,0},{2,3},{3,2},{4,5},{5,4},{6,7},{7,6},{8,9},{9,8},{10,11... | collective-permute-start | bytes 393224 | tf_op jit(solution)/shard_map/ppermute | solution.py:404
  108.0 16.9 %collective-permute-start.11 = (bf16[32,2048]{1,0:T(8,128)(2,1)S(1)}, bf16[32,2048]{1,0:T(8,128)(2,1)S(1)}, u32[]{:S(2)}, u32[]{:S(2)}) collective-permute-start(bf16[32,2048]{1,0:T(8,128)(2,1)S(1)} %fusion.6), channel_id=1, source_target_pairs={{0,1},{1,0},{2,3},{3,2},{4,5},{5,4},{6,7},{7,6},{8,9},{9,8},{10,11... | collective-permute-start | bytes 393224 | tf_op jit(solution)/shard_map/ppermute | solution.py:404
  109.7 17.6 %collective-permute-start.15 = (bf16[32,2048]{1,0:T(8,128)(2,1)S(1)}, bf16[32,2048]{1,0:T(8,128)(2,1)S(1)}, u32[]{:S(2)}, u32[]{:S(2)}) collective-permute-start(bf16[32,2048]{1,0:T(8,128)(2,1)S(1)} %fusion.7), channel_id=1, source_target_pairs={{0,1},{1,0},{2,3},{3,2},{4,5},{5,4},{6,7},{7,6},{8,9},{9,8},{10,11... | collective-permute-start | bytes 393224 | tf_op jit(solution)/shard_map/ppermute | solution.py:404

commit v3 on v2

v3 whole, which is shorter than its diff:
```python
import functools
import math

import jax
import jax.numpy as jnp
from jax import lax
from jax.experimental import pallas as pl
from jax.experimental.pallas import tpu as pltpu
from jax.sharding import PartitionSpec as P

HEAD = 128
ROWS = 128
MIGRANTS = 14
STAYING = ROWS - MIGRANTS
COPIED = 4
PAGES_ROW = 16
PAGE = 64
REPLICAS = 16
CAP = 2
SLOTS = REPLICAS * CAP
GROUP = 8
CONTEXT = PAGES_ROW * PAGE
NEG_FILL = -1e30
SCALE = math.log2(math.e) / math.sqrt(HEAD)
META_ROW = 4
CHUNK = 256
FIRST = 48
SECOND = 32
THIRD = 40
WIDTH = 2048
WEIGHT_TILE = 1024
WEIGHT_PARTS = 8
VMEM = pl.BlockSpec(memory_space=pltpu.VMEM)
SMEM = pl.BlockSpec(memory_space=pltpu.SMEM)
HBM = pl.BlockSpec(memory_space=pltpu.HBM)
PARAMS = pltpu.CompilerParams(vmem_limit_bytes=60 * 2**20)


def attend_group(tokens, queries, fresh, pages, lengths, pool_ref, scores_ref):
    nt = (((1,), (1,)), ((), ()))
    for i in range(GROUP):
        keys = jnp.concatenate([pool_ref[0, page] for page in pages[i][: tokens // PAGE]], axis=0)
        scores_ref[i, :, 0:tokens] = lax.dot_general(
            queries[i], keys, nt, preferred_element_type=jnp.float32
        )
        scores_ref[i, :, CONTEXT : CONTEXT + 8] = lax.dot_general(
            queries[i], fresh[i].astype(jnp.bfloat16), nt, preferred_element_type=jnp.float32
        )
    outputs = []
    for i in range(GROUP):
        scores = scores_ref[i, :, 0:tokens]
        position = lax.broadcasted_iota(jnp.int32, scores.shape, 1)
        scores = jnp.where(position < lengths[i], scores, NEG_FILL)
        fresh_scores = scores_ref[i, :, CONTEXT : CONTEXT + 8]
        line = lax.broadcasted_iota(jnp.int32, fresh_scores.shape, 1)
        step = lax.rem(lax.broadcasted_iota(jnp.int32, fresh_scores.shape, 0), 2)
        fresh_scores = jnp.where((line == 0) | (line == 2 * step), fresh_scores, NEG_FILL)
        highest = jnp.maximum(
            jnp.max(scores, axis=1, keepdims=True), jnp.max(fresh_scores, axis=1, keepdims=True)
        )
        weights = jnp.exp2((scores - highest) * SCALE).astype(jnp.bfloat16)
        fresh_weights = jnp.exp2((fresh_scores - highest) * SCALE).astype(jnp.bfloat16)
        total = jnp.sum(weights.astype(jnp.float32), axis=1, keepdims=True) + jnp.sum(
            fresh_weights.astype(jnp.float32), axis=1, keepdims=True
        )
        values = jnp.concatenate([pool_ref[1, page] for page in pages[i][: tokens // PAGE]], axis=0)
        fresh_values = pltpu.roll(fresh[i], 7, 0).astype(jnp.bfloat16)
        weighted = jnp.dot(weights, values, preferred_element_type=jnp.float32) + jnp.dot(
            fresh_weights, fresh_values, preferred_element_type=jnp.float32
        )
        outputs.append((weighted / total).astype(jnp.bfloat16))
    return outputs


def fresh_rows(tokens):
    tokens = tokens.astype(jnp.float32).reshape(4, HEAD)
    return jnp.concatenate([tokens, jnp.zeros((4, HEAD), jnp.float32)], axis=0)


def fetch_pool(pool_hbm, pool_ref, sem):
    copies = [
        pltpu.make_async_copy(pool_hbm.at[k, p : p + 32], pool_ref.at[k, p : p + 32], sem.at[k, p // 32])
        for k in range(2)
        for p in range(0, 128, 32)
    ]
    for copy in copies:
        copy.start()
    return copies


def chunks_of(length):
    return (length + CHUNK - 1) // CHUNK


def sort_rows(length_of, count, order_ref):
    def tally(i, counts):
        chunks = chunks_of(length_of(i))
        return tuple(c + jnp.where(chunks == k, 1, 0) for k, c in enumerate(counts))

    zero = jnp.int32(0)
    counts = lax.fori_loop(0, count, tally, (zero,) * 5)
    starts = [zero]
    for c in counts[:4]:
        starts.append(starts[-1] + c)

    def put(i, starts):
        chunks = chunks_of(length_of(i))
        place = zero
        for k in range(5):
            place = jnp.where(chunks == k, starts[k], place)
        order_ref[place] = i
        return tuple(s + jnp.where(chunks == k, 1, 0) for k, s in enumerate(starts))

    lax.fori_loop(0, count, put, tuple(starts))
    return counts[0]


def each_group(groups, order_ref, length_of, attend):
    def group(g, carry):
        rows = [order_ref[g * GROUP + i] for i in range(GROUP)]
        chunks = jnp.maximum(chunks_of(length_of(rows[-1])), 1)
        for k in range(1, CONTEXT // CHUNK + 1):

            @pl.when(chunks == k)
            def _():
                attend(k * CHUNK, rows)

        return carry

    lax.fori_loop(groups[0], groups[1], group, 0)


def stay_copies(first, count, query_hbm, fresh_hbm, query_ref, fresh_ref, sem):
    copies = [
        pltpu.make_async_copy(query_hbm.at[first : first + count], query_ref, sem.at[0]),
        pltpu.make_async_copy(fresh_hbm.at[first : first + count], fresh_ref, sem.at[1]),
    ]
    for copy in copies:
        copy.start()
    return copies


def attend_staying(
    first, count, table_ref, length_ref, query_hbm, fresh_hbm, pool_hbm, out_ref, out_first, refs, meanwhile=None
):
    pool_ref, scores_ref, pool_sem, query_ref, fresh_ref, order_ref, row_sem = refs
    copies = fetch_pool(pool_hbm, pool_ref, pool_sem)
    copies += stay_copies(first, count, query_hbm, fresh_hbm, query_ref, fresh_ref, row_sem)
    length_of = lambda i: jnp.where(first + i < STAYING, length_ref[0, first + i], 1)
    sort_rows(length_of, count, order_ref)
    for copy in copies:
        copy.wait()
    started = meanwhile() if meanwhile is not None else None

    def attend(tokens, rows):
        outputs = attend_group(
            tokens,
            [query_ref[row].reshape(16, HEAD) for row in rows],
            [fresh_rows(fresh_ref[row]) for row in rows],
            [[table_ref[p, first + row] for p in range(PAGES_ROW)] for row in rows],
            [length_of(row) for row in rows],
            pool_ref,
            scores_ref,
        )
        for row, output in zip(rows, outputs):
            out_ref[out_first + row] = output.reshape(8, 2, HEAD)

    each_group((0, count // GROUP), order_ref, length_of, attend)
    return started


def stay_kernel(table_ref, length_ref, query_hbm, fresh_hbm, pool_hbm, out_ref, *refs):
    attend_staying(0, FIRST, table_ref, length_ref, query_hbm, fresh_hbm, pool_hbm, out_ref, 0, refs)


def attention_scratch(pool):
    return [
        pltpu.VMEM(pool.shape, pool.dtype),
        pltpu.VMEM((GROUP, 16, CONTEXT + 128), jnp.float32),
        pltpu.SemaphoreType.DMA((2, 4)),
    ]


def stay_scratch(pool, count):
    return attention_scratch(pool) + [
        pltpu.VMEM((count, 8, 2, HEAD), jnp.bfloat16),
        pltpu.VMEM((count, 2, 2, HEAD), jnp.bfloat16),
        pltpu.SMEM((count,), jnp.int32),
        pltpu.SemaphoreType.DMA((2,)),
    ]


def stay(table, lengths, query, fresh, pool, count):
    return pl.pallas_call(
        stay_kernel,
        out_shape=jax.ShapeDtypeStruct((count, 8, 2, HEAD), jnp.bfloat16),
        in_specs=[SMEM, SMEM, HBM, HBM, HBM],
        out_specs=VMEM,
        scratch_shapes=stay_scratch(pool, count),
        compiler_params=PARAMS,
        cost_estimate=pl.CostEstimate(flops=8 * 10**9, bytes_accessed=8 * 2**20, transcendentals=0),
        name="attend_first",
    )(table, lengths, query, fresh, pool)


def fetch_weight(weight_hbm, weight_ref, sem):
    copies = []
    for c in range(WEIGHT_PARTS):
        columns = slice(c * WEIGHT_TILE, (c + 1) * WEIGHT_TILE)
        copies.append(pltpu.make_async_copy(weight_hbm.at[:, columns], weight_ref.at[:, columns], sem.at[c]))
    for copy in copies:
        copy.start()
    return copies


def second_kernel(after_ref, table_ref, length_ref, query_hbm, fresh_hbm, pool_hbm, out_ref, *refs):
    attend_staying(FIRST, SECOND, table_ref, length_ref, query_hbm, fresh_hbm, pool_hbm, out_ref, 0, refs)


def attend_second(after, table, lengths, query, fresh, pool):
    return pl.pallas_call(
        second_kernel,
        out_shape=jax.ShapeDtypeStruct((SECOND, 8, 2, HEAD), jnp.bfloat16),
        in_specs=[SMEM, SMEM, SMEM, HBM, HBM, HBM],
        out_specs=VMEM,
        scratch_shapes=stay_scratch(pool, SECOND),
        compiler_params=PARAMS,
        cost_estimate=pl.CostEstimate(flops=8 * 10**9, bytes_accessed=8 * 2**20, transcendentals=0),
        name="attend_second",
    )(after, table, lengths, query, fresh, pool)


def project_rolled(rolled_ref, weight_ref, fetch, held_refs, part_refs, sem):
    copies = []
    for c, copy in enumerate(fetch):
        copy.wait()
        start = c * WEIGHT_TILE
        product = jnp.dot(
            rolled_ref[...], weight_ref[:, start : start + WEIGHT_TILE], preferred_element_type=jnp.float32
        ).astype(jnp.bfloat16)
        half, start = divmod(start, 2 * WIDTH)
        own, above, far, below = (product[64 * k : 64 * k + 64] for k in range(4))
        place = slice(start % WIDTH, start % WIDTH + WEIGHT_TILE)
        first, second = slice(0, 64), slice(64, 128)
        if start < WIDTH:
            puts = [(1, first, far), (2, second, below), (3, first, above)]
        else:
            puts = [(2, first, far), (1, second, above), (4, first, below)]
        puts = [(part, lines, place, value) for part, lines, value in puts]
        puts.append((0, first, slice(start, start + WEIGHT_TILE), own))
        for k, (part, lines, columns, value) in enumerate(puts):
            held, target = held_refs[half * 5 + part], part_refs[half * 5 + part]
            held[lines, columns] = value
            copies.append(pltpu.make_async_copy(held.at[lines, columns], target.at[lines, columns], sem.at[c, k]))
            copies[-1].start()
    return copies


PART_SHAPES = ((64, 2 * WIDTH), (128, WIDTH), (128, WIDTH), (64, WIDTH), (64, WIDTH)) * 2


def project_kernel(
    slot_ref, table_ref, length_ref, query_hbm, fresh_hbm, pool_hbm, first_ref, second_ref, ret_ref, weight_hbm,
    out_ref, *refs
):
    part_refs, refs = refs[:10], refs[10:]
    stay_refs, held_refs, (weight_ref, rolled_ref, weight_sem, part_sem) = refs[:-14], refs[-14:-4], refs[-4:]
    done = FIRST + SECOND

    def start_weight():
        return fetch_weight(weight_hbm, weight_ref, weight_sem)

    fetch = attend_staying(
        done, THIRD, table_ref, length_ref, query_hbm, fresh_hbm, pool_hbm, out_ref, done, stay_refs, start_weight
    )
    out_ref[0:FIRST] = first_ref[...]
    out_ref[FIRST:done] = second_ref[...]
    for j in range(MIGRANTS):
        out_ref[STAYING + j] = ret_ref[slot_ref[j]].reshape(8, 2, HEAD)
    zi = lax.axis_index("tensor") // 2
    for z in range(4):
        place = pl.multiple_of(lax.rem(z - zi + 4, 4) * 64, 64)
        for h in range(8):
            rolled_ref[pl.ds(place, 64), h * HEAD : (h + 1) * HEAD] = out_ref[32 * z : 32 * z + 32, h].reshape(64, HEAD)
    for copy in project_rolled(rolled_ref, weight_ref, fetch, held_refs, part_refs, part_sem):
        copy.wait()


def project(slots, table, lengths, query, fresh, pool, first, second, returned, weight):
    out = pl.pallas_call(
        project_kernel,
        out_shape=[jax.ShapeDtypeStruct((ROWS, 8, 2, HEAD), jnp.bfloat16)]
        + [jax.ShapeDtypeStruct(shape, jnp.bfloat16) for shape in PART_SHAPES],
        in_specs=[SMEM, SMEM, SMEM, HBM, HBM, HBM, VMEM, VMEM, VMEM, HBM],
        out_specs=[VMEM] + [HBM] * 10,
        scratch_shapes=stay_scratch(pool, THIRD)
        + [pltpu.VMEM(shape, jnp.bfloat16) for shape in PART_SHAPES]
        + [
            pltpu.VMEM(weight.shape, weight.dtype),
            pltpu.VMEM((2 * ROWS, weight.shape[0]), jnp.bfloat16),
            pltpu.SemaphoreType.DMA((WEIGHT_PARTS,)),
            pltpu.SemaphoreType.DMA((WEIGHT_PARTS, 4)),
        ],
        compiler_params=PARAMS,
        cost_estimate=pl.CostEstimate(flops=10**9, bytes_accessed=2**20, transcendentals=0),
        name="attend_third_project",
    )(slots, table, lengths, query, fresh, pool, first, second, returned, weight)
    return out[0], list(out[1:6]), list(out[6:])


def same_kernel(*refs):
    pass


def second_turn(up, down):
    return pl.pallas_call(
        same_kernel,
        out_shape=[jax.ShapeDtypeStruct(x.shape, x.dtype) for x in (up, down)],
        in_specs=[HBM, HBM],
        out_specs=[HBM, HBM],
        input_output_aliases={0: 0, 1: 1},
        compiler_params=PARAMS,
        cost_estimate=pl.CostEstimate(flops=3 * 10**10, bytes_accessed=2**20, transcendentals=0),
        name="second_turn",
    )(up, down)


def request_kernel(
    offset_ref, order_ref, table_ref, length_ref, query_ref, fresh_ref, out_ref, slot_ref, used
):
    own = lax.axis_index("replica")
    out_ref[...] = jnp.zeros_like(out_ref)
    for s in range(REPLICAS):
        used[s] = 0
    lane = lax.broadcasted_iota(jnp.int32, (1, HEAD), 1)
    for j in range(MIGRANTS):
        row = STAYING + j
        source = lax.rem(own + 1 + offset_ref[0, j], REPLICAS)
        rank = used[source]
        used[source] = rank + 1
        slot = source * CAP + rank
        slot_ref[j] = slot
        meta = jnp.zeros((1, HEAD), jnp.int32)
        for p in range(PAGES_ROW):
            meta = jnp.where(lane == p, table_ref[p, row], meta)
        for c in range(COPIED):
            wanted = table_ref[order_ref[j, 0, c], row]
            meta = jnp.where(lane == PAGES_ROW + c, wanted, meta)
        length = length_ref[0, row]
        meta = jnp.where(lane == 20, length // 32, meta)
        meta = jnp.where(lane == 21, lax.rem(length, 32), meta)
        out_ref[slot, 0:16] = query_ref[row].reshape(16, HEAD)
        out_ref[slot, 16:32] = jnp.concatenate(
            [
                fresh_ref[row].astype(jnp.float32).reshape(4, HEAD),
                meta.astype(jnp.float32),
                jnp.zeros((11, HEAD), jnp.float32),
            ],
            axis=0,
        ).astype(jnp.bfloat16)


def request(offsets, order, table, lengths, query, fresh):
    return pl.pallas_call(
        request_kernel,
        out_shape=(
            jax.ShapeDtypeStruct((SLOTS, 32, HEAD), jnp.bfloat16),
            jax.ShapeDtypeStruct((MIGRANTS,), jnp.int32),
        ),
        in_specs=[SMEM] * 4 + [VMEM] * 2,
        out_specs=(VMEM, SMEM),
        scratch_shapes=[pltpu.SMEM((REPLICAS,), jnp.int32)],
        compiler_params=PARAMS,
        name="pack_requests",
    )(offsets, order, table, lengths, query, fresh)


def serve_kernel(
    got_ref, after_ref, pool_hbm, ret_ref, send_ref, unused_ref, pool_ref, scores_ref, pool_sem, meta_vmem, meta_ref, order_ref,
    meta_sem, page_sem
):
    fetch = fetch_pool(pool_hbm, pool_ref, pool_sem)
    for slot in range(SLOTS):
        meta_vmem[slot : slot + 1] = got_ref[slot, 16:32].astype(jnp.float32)[META_ROW : META_ROW + 1].astype(jnp.int32)
    meta_copy = pltpu.make_async_copy(meta_vmem, meta_ref, meta_sem)
    meta_copy.start()
    ret_ref[...] = jnp.zeros_like(ret_ref)
    meta_copy.wait()
    length_of = lambda slot: meta_ref[slot, 20] * 32 + meta_ref[slot, 21]
    unused = sort_rows(length_of, SLOTS, order_ref)
    unused_ref[0] = unused
    for copy in fetch:
        copy.wait()

    def copies(slot, carry):
        for c in range(COPIED):
            page = meta_ref[slot, PAGES_ROW + c]
            pltpu.make_async_copy(pool_ref.at[:, page], send_ref.at[slot, c], page_sem).start()
        return carry

    lax.fori_loop(0, SLOTS, copies, 0)

    def attend(tokens, slots):
        outputs = attend_group(
            tokens,
            [got_ref[slot, 0:16] for slot in slots],
            [got_ref[slot, 16:32].astype(jnp.float32)[0:8] for slot in slots],
            [[meta_ref[slot, p] for p in range(PAGES_ROW)] for slot in slots],
            [length_of(slot) for slot in slots],
            pool_ref,
            scores_ref,
        )
        for slot, output in zip(slots, outputs):
            ret_ref[slot] = output

    each_group((unused // GROUP, SLOTS // GROUP), order_ref, length_of, attend)
    pltpu.make_async_copy(send_ref, send_ref, page_sem).wait()


def serve(got, after, pool):
    return pl.pallas_call(
        serve_kernel,
        out_shape=(
            jax.ShapeDtypeStruct((SLOTS, 16, HEAD), jnp.bfloat16),
            jax.ShapeDtypeStruct((SLOTS, COPIED, 2, PAGE, HEAD), jnp.bfloat16),
            jax.ShapeDtypeStruct((1,), jnp.int32),
        ),
        in_specs=[VMEM, HBM, HBM],
        out_specs=(VMEM, HBM, SMEM),
        scratch_shapes=attention_scratch(pool)
        + [
            pltpu.VMEM((SLOTS, HEAD), jnp.int32),
            pltpu.SMEM((SLOTS, HEAD), jnp.int32),
            pltpu.SMEM((SLOTS,), jnp.int32),
            pltpu.SemaphoreType.DMA,
            pltpu.SemaphoreType.DMA,
        ],
        compiler_params=PARAMS,
        cost_estimate=pl.CostEstimate(flops=6 * 10**9, bytes_accessed=8 * 2**20, transcendentals=0),
        name="serve_requests",
    )(got, after, pool)


def pick_kernel(slot_ref, got_ref, out_ref, done_ref, held, in_sem, out_sem):
    done_ref[0] = 0.0
    loads = [
        pltpu.make_async_copy(got_ref.at[slot_ref[j]], held.at[j], in_sem.at[j]) for j in range(MIGRANTS)
    ]
    stores = [pltpu.make_async_copy(held.at[j], out_ref.at[j], out_sem.at[j]) for j in range(MIGRANTS)]
    for load in loads:
        load.start()
    for load, store in zip(loads, stores):
        load.wait()
        store.start()
    for store in stores:
        store.wait()


def pick(slots, got):
    shape = (MIGRANTS, COPIED, 2, PAGE, HEAD)
    return pl.pallas_call(
        pick_kernel,
        out_shape=(jax.ShapeDtypeStruct(shape, jnp.bfloat16), jax.ShapeDtypeStruct((1,), jnp.float32)),
        in_specs=[SMEM, HBM],
        out_specs=(HBM, SMEM),
        scratch_shapes=[
            pltpu.VMEM(shape, jnp.bfloat16),
            pltpu.SemaphoreType.DMA((MIGRANTS,)),
            pltpu.SemaphoreType.DMA((MIGRANTS,)),
        ],
        compiler_params=PARAMS,
        name="pick_pages",
    )(slots, got)


def shift_z(value, by):
    pairs = [(z * 2 + x, (z + by) % 4 * 2 + x) for z in range(4) for x in range(2)]
    return lax.ppermute(value, "tensor", pairs)


def swap_x(value):
    return lax.ppermute(value, "tensor", [(t, t ^ 1) for t in range(8)])


def f32_sum(*terms):
    return functools.reduce(jnp.add, [term.astype(jnp.float32) for term in terms])


def reduce_z(own, up, down, up_later, down_later):
    from_below, from_above = shift_z(up, 1), shift_z(down, -1)
    up_later = f32_sum(up_later, from_below[:64]).astype(jnp.bfloat16)
    down_later = f32_sum(down_later, from_above[:64]).astype(jnp.bfloat16)
    first = f32_sum(own[:, :WIDTH], from_above[64:], shift_z(up_later, 1))
    second = f32_sum(own[:, WIDTH:], from_below[64:], shift_z(down_later, -1))
    return jnp.concatenate([first, second], axis=1)


def body(
    queries,
    step_key_value,
    replica_page_store,
    page_table,
    lengths,
    mig_offset,
    copy_order,
    out_weight,
):
    xi = lax.axis_index("tensor") % 2
    pool = replica_page_store[0]
    query = queries[0].reshape(ROWS, 2, 8, HEAD).transpose(0, 2, 1, 3)
    fresh = step_key_value[0]
    table = page_table[0].T
    payload, slots = request(
        mig_offset[:, :, 0], copy_order.transpose(1, 0, 2), table, lengths, query, fresh
    )
    got = lax.all_to_all(
        payload.reshape(REPLICAS, CAP, 32, HEAD), "replica", split_axis=0, concat_axis=0, tiled=True
    ).reshape(SLOTS, 32, HEAD)
    first = stay(table, lengths, query, fresh, pool, FIRST)
    answered, sending, unused = serve(got, first, pool)
    second = attend_second(unused, table, lengths, query, fresh, pool)
    returned = lax.all_to_all(
        answered.reshape(REPLICAS, CAP, 16, HEAD), "replica", split_axis=0, concat_axis=0, tiled=True
    ).reshape(SLOTS, 16, HEAD)
    incoming = lax.all_to_all(
        sending.reshape(REPLICAS, CAP, COPIED, 2, PAGE, HEAD),
        "replica",
        split_axis=0,
        concat_axis=0,
        tiled=True,
    ).reshape(SLOTS, COPIED, 2, PAGE, HEAD)
    merged, zero_parts, one_parts = project(
        slots, table, lengths, query, fresh, pool, first, second, returned, out_weight
    )
    one_parts[1:3] = second_turn(*one_parts[1:3])
    arrived, nothing = pick(slots, incoming)
    finished = []
    for parts in (zero_parts, one_parts):
        total = reduce_z(*parts).reshape(2, 32, 2 * WIDTH)
        mine = lax.dynamic_index_in_dim(total, xi, 0, keepdims=False)
        other = lax.dynamic_index_in_dim(total, 1 - xi, 0, keepdims=False)
        finished.append(mine + swap_x(other.astype(jnp.bfloat16)).astype(jnp.float32))
    finished[1] += nothing[0]
    projected = jnp.concatenate([half.astype(jnp.bfloat16) for half in finished], axis=1).reshape(16, 2, -1)
    attention = merged.transpose(0, 2, 1, 3).reshape(ROWS, 2, 8 * HEAD)
    return (attention[None], projected[None], arrived[None])


def solution(mesh):
    placed = (
        P("replica", None, None, "tensor"),
        P("replica", None, None, None, "tensor"),
        P("replica", None, None, None, "tensor"),
        P("replica", None, None),
        P("replica", None),
        P("replica", None, None),
        P("replica", None, None),
        P("tensor", None),
    )
    return jax.shard_map(
        body,
        mesh=mesh,
        in_specs=placed,
        out_specs=(
            P("replica", None, None, "tensor"),
            P("replica", "tensor", None, None),
            P("replica", None, None, None, None, "tensor"),
        ),
        check_vma=False,
    )
```

time: 132 us -> 124 us (0.939)
  starting transfers between devices: 44.3 us -> 39 us
  Pallas kernels: 47.7 us -> 44.7 us
    ppermute x12 -> x8, waiting for transfers between devices: 16.6 us -> 24.6 us  [shift_z(): return lax.ppermute(value, 'tensor', pairs)]
    ppermute x4 -> x2, waiting for transfers between devices: 16.8 us -> 9.92 us  [swap_x(): return lax.ppermute(value, 'tensor', [(t, t ^ 1) for t in range(8)])]
    ppermute x12 -> x8, starting transfers between devices: 19.1 us -> 14.9 us  [shift_z(): return lax.ppermute(value, 'tensor', pairs)]
    pallas_call x1, Pallas kernels: 12 us -> 9.12 us  [stay(): pl.pallas_call(stay_kernel, out_shape=jax.ShapeDtypeStruct((count, 8, 2,...]
    ppermute x4 -> x2, starting transfers between devices: 4.29 us -> 3.03 us  [swap_x(): return lax.ppermute(value, 'tensor', [(t, t ^ 1) for t in range(8)])]
  transfers between devices with their start and end apart: 19 -> 13, of which waited for: 8 -> 7; matrix products, arithmetic and copies ran while one was open for 3% -> 1% of each run, Pallas kernels for 28% -> 29%
where the time goes in v3:
time: 124 us; the launch traced here: 123 us
  Pallas kernels  44.7 us (36%)
  starting transfers between devices  39 us (31%)
  waiting for transfers between devices  34.6 us (28%)
  local copies, waits for them, and re-layouts  2.58 us (2%)
  other arithmetic  1.6 us (1%)
    ppermute x8, waiting for transfers between devices, shift_z(): return lax.ppermute(value, 'tensor', pairs)  24.6 us
    pallas_call x1, Pallas kernels, project(): pl.pallas_call(project_kernel, out_shape=[jax.ShapeDtypeStruct((ROWS, 8,...  15.5 us
    ppermute x8, starting transfers between devices, shift_z(): return lax.ppermute(value, 'tensor', pairs)  14.9 us
    ppermute x2, waiting for transfers between devices, swap_x(): return lax.ppermute(value, 'tensor', [(t, t ^ 1) for t in range(8)])  9.92 us
    pallas_call x1, Pallas kernels, stay(): pl.pallas_call(stay_kernel, out_shape=jax.ShapeDtypeStruct((count, 8, 2,...  9.12 us
    pallas_call x1, Pallas kernels, attend_second(): pl.pallas_call(second_kernel, out_shape=jax.ShapeDtypeStruct((SECOND, 8,...  7.99 us
    all_to_all x1, starting transfers between devices, body(): lax.all_to_all(answered.reshape(REPLICAS, CAP, 16, HEAD), 'replica', spli...  7.43 us
    all_to_all x1, starting transfers between devices, body(): lax.all_to_all(sending.reshape(REPLICAS, CAP, COPIED, 2, PAGE, HEAD), 're...  7.13 us
  transfers between devices with their start and end apart: 13, of which 7 were waited for; matrix products, arithmetic and copies ran while one was open for 1% of the time, Pallas kernels for 29%

profile of v3, /device:TPU:10, one launch (start us, length us, event | category | flops | bytes accessed | tf_op | source)
XLA Modules:
  0.0 123.3 jit_solution(16233442868680578375)
XLA Ops:
  0.6 2.1 %pack_requests.1 = (bf16[32,32,128]{2,1,0:T(8,128)(2,1)}, s32[14]{0:T(128)}) custom-call(s32[1,14]{1,0:T(1,128)} %bitcast.63, s32[14,1,16]{2,1,0:T(1,128)} %bitcast.62, s32[16,128]{1,0:T(8,128)} %bitcast.58, s32[1,128]{1,0:T(1,128)} %length_ref.7, bf16[128,8,2,128]{3,2,1,0:T(2,128)(2,1)} %bitcast.46, bf16[128,2,2,128]{3,2,1,0:T(2,128)(2,1)} %bitcast.51), custom_call_target="tpu_custom_call" | custom-call | tf_op jit(solution)/shard_map/pack_requests/pallas_call | solution.py:364
  2.8 6.5 %all-to-all-start = ((bf16[16,2,32,128]{3,2,1,0:T(8,128)(2,1)}), bf16[16,2,32,128]{3,2,1,0:T(8,128)(2,1)S(1)}, u32[]{:S(2)}, u32[]{:S(2)}) async-start(bf16[16,2,32,128]{3,2,1,0:T(8,128)(2,1)} %bitcast.56), calls=%async_computation | async-start | bytes 524288 | tf_op jit(solution)/shard_map/all_to_all | solution.py:516
  9.3 9.1 %attend_first.1.after_ref.first_ref = bf16[48,8,2,128]{3,2,1,0:T(2,128)(2,1)} custom-call(s32[16,128]{1,0:T(8,128)} %bitcast.59, s32[1,128]{1,0:T(1,128)} %length_ref.7, bf16[128,8,2,128]{3,2,1,0:T(2,128)(2,1)} %bitcast.47, bf16[128,2,2,128]{3,2,1,0:T(2,128)(2,1)} %bitcast.52, bf16[2,128,64,128]{3,2,1,0:T(8,128)(2,1)} %bitcast.37), custom_call_target="tpu_custom_call" | custom-call | flops 8000000000 | bytes 8388608 | tf_op jit(solution)/shard_map/attend_first/pallas_call | solution.py:194
  18.4 0.0 all-to-all-done
  18.4 0.0 copy-start.7
  18.4 0.7 copy-done.7
  19.1 6.3 %serve_requests.1 = (bf16[32,16,128]{2,1,0:T(8,128)(2,1)}, bf16[32,4,2,64,128]{4,3,2,1,0:T(8,128)(2,1)}, s32[1]{0:T(128)}) custom-call(bf16[32,32,128]{2,1,0:T(8,128)(2,1)} %bitcast.55, bf16[48,8,2,128]{3,2,1,0:T(2,128)(2,1)} %attend_first.1.after_ref.first_ref, bf16[2,128,64,128]{3,2,1,0:T(8,128)(2,1)} %bitcast.38), custom_call_target="tpu_custom_call" | custom-call | flops 6000000000 | bytes 8388608 | tf_op jit(solution)/shard_map/serve_requests/pallas_call | solution.py:421
  25.4 7.4 %all-to-all-start.1 = ((bf16[16,2,16,128]{3,2,1,0:T(8,128)(2,1)}), bf16[16,2,16,128]{3,2,1,0:T(8,128)(2,1)S(1)}, u32[]{:S(2)}, u32[]{:S(2)}) async-start(bf16[16,2,16,128]{3,2,1,0:T(8,128)(2,1)} %bitcast.57), calls=%async_computation.1 | async-start | bytes 262144 | tf_op jit(solution)/shard_map/all_to_all | solution.py:522
  32.9 8.0 %attend_second.1.second_ref = bf16[32,8,2,128]{3,2,1,0:T(2,128)(2,1)} custom-call(s32[1]{0:T(128)} %get-tuple-element.25.after_ref, s32[16,128]{1,0:T(8,128)} %bitcast.60, s32[1,128]{1,0:T(1,128)} %length_ref.7, bf16[128,8,2,128]{3,2,1,0:T(2,128)(2,1)} %bitcast.48, bf16[128,2,2,128]{3,2,1,0:T(2,128)(2,1)} %bitcast.53, bf16[2,128,64,128]{3,2,1,0:T(8,128)(2,1)} %bitcast.39), custom_call_target="tpu_custom_call" | custom-call | flops 8000000000 | bytes 8388608 | tf_op jit(solution)/shard_map/attend_second/pallas_call | solution.py:221
  40.9 0.0 all-to-all-done.1
  40.9 0.0 copy-start
  40.9 0.6 copy-done
  41.5 7.1 %all-to-all-start.2 = ((bf16[16,2,4,2,64,128]{5,4,3,2,1,0:T(8,128)(2,1)}), bf16[16,2,4,2,64,128]{5,4,3,2,1,0:T(8,128)(2,1)}, u32[]{:S(2)}, u32[]{:S(2)}) async-start(bf16[16,2,4,2,64,128]{5,4,3,2,1,0:T(8,128)(2,1)} %bitcast.41), calls=%async_computation.2 | async-start | bytes 8388608 | tf_op jit(solution)/shard_map/all_to_all | solution.py:525
  48.7 15.5 %attend_third_project.1 = (bf16[128,8,2,128]{3,2,1,0:T(2,128)(2,1)}, bf16[64,4096]{1,0:T(8,128)(2,1)}, bf16[128,2048]{1,0:T(8,128)(2,1)}, bf16[128,2048]{1,0:T(8...) custom-call(s32[14]{0:T(128)} %get-tuple-element.23.slot_ref, ...), custom_call_target="tpu_custom_call" | custom-call | flops 1000000000 | bytes 1048576 | tf_op jit(solution)/shard_map/attend_third_project/pallas_call | solution.py:290
  64.2 4.1 %collective-permute-start = (bf16[128,2048]{1,0:T(8,128)(2,1)}, bf16[128,2048]{1,0:T(8,128)(2,1)S(1)}, u32[]{:S(2)}, u32[]{:S(2)}) collective-permute-start(bf16[128,2048]{1,0:T(8,128)(2,1)} %get-tuple-element.29), channel_id=1, source_target_pairs={{0,6},{1,7},{2,0},{3,1},{4,2},{5,3},{6,4},{7,5},{8,14},{9,15},{10,... | collective-permute-start | bytes 1572872 | tf_op jit(solution)/shard_map/ppermute | solution.py:478
  68.3 0.0 collective-permute-start.1
  68.3 0.0 copy-start.3
  68.3 0.0 copy-start.2
  68.3 3.3 %collective-permute-start.5 = (bf16[128,2048]{1,0:T(8,128)(2,1)}, bf16[128,2048]{1,0:T(8,128)(2,1)S(1)}, u32[]{:S(2)}, u32[]{:S(2)}) collective-permute-start(bf16[128,2048]{1,0:T(8,128)(2,1)} %get-tuple-element.36), channel_id=1, source_target_pairs={{0,6},{1,7},{2,0},{3,1},{4,2},{5,3},{6,4},{7,5},{8,14},{9,15},{10,... | collective-permute-start | bytes 1572872 | tf_op jit(solution)/shard_map/ppermute | solution.py:478
  71.6 0.0 collective-permute-start.6
  71.6 9.3 %collective-permute-done = bf16[128,2048]{1,0:T(8,128)(2,1)S(1)} collective-permute-done((bf16[128,2048]{1,0:T(8,128)(2,1)}, bf16[128,2048]{1,0:T(8,128)(2,1)S(1)}, u32[]{:S(2)}, u32[]{:S(2)}) %collective-permute-start) | collective-permute-done | bytes 524320 | tf_op jit(solution)/shard_map/ppermute | solution.py:478
  80.9 0.1 add_convert_fusion.2
  81.0 3.7 %collective-permute-start.3 = (bf16[64,2048]{1,0:T(8,128)(2,1)S(1)}, bf16[64,2048]{1,0:T(8,128)(2,1)S(1)}, u32[]{:S(2)}, u32[]{:S(2)}) collective-permute-start(bf16[64,2048]{1,0:T(8,128)(2,1)S(1)} %add_convert_fusion.2), channel_id=1, source_target_pairs={{0,6},{1,7},{2,0},{3,1},{4,2},{5,3},{6,4},{7,5},{8,14},{9,15},{10,... | collective-permute-start | bytes 786440 | tf_op jit(solution)/shard_map/ppermute | solution.py:478
  84.6 0.0 collective-permute-done.1
  84.6 0.1 add_convert_fusion.3
  84.7 0.1 collective-permute-start.2
  84.8 7.3 %collective-permute-done.5 = bf16[128,2048]{1,0:T(8,128)(2,1)S(1)} collective-permute-done((bf16[128,2048]{1,0:T(8,128)(2,1)}, bf16[128,2048]{1,0:T(8,128)(2,1)S(1)}, u32[]{:S(2)}, u32[]{:S(2)}) %collective-permute-start.5) | collective-permute-done | bytes 524320 | tf_op jit(solution)/shard_map/ppermute | solution.py:478
  92.1 0.1 add_convert_fusion
  92.2 3.7 %collective-permute-start.8 = (bf16[64,2048]{1,0:T(8,128)(2,1)S(1)}, bf16[64,2048]{1,0:T(8,128)(2,1)S(1)}, u32[]{:S(2)}, u32[]{:S(2)}) collective-permute-start(bf16[64,2048]{1,0:T(8,128)(2,1)S(1)} %add_convert_fusion), channel_id=1, source_target_pairs={{0,6},{1,7},{2,0},{3,1},{4,2},{5,3},{6,4},{7,5},{8,14},{9,15},{10,... | collective-permute-start | bytes 786440 | tf_op jit(solution)/shard_map/ppermute | solution.py:478
  95.9 0.0 collective-permute-done.6
  95.9 0.1 add_convert_fusion.1
  95.9 0.1 collective-permute-start.7
  96.0 1.6 %collective-permute-done.3 = bf16[64,2048]{1,0:T(8,128)(2,1)S(1)} collective-permute-done((bf16[64,2048]{1,0:T(8,128)(2,1)S(1)}, bf16[64,2048]{1,0:T(8,128)(2,1)S(1)}, u32[]{:S(2)}, u32[]{:S(2)}) %collective-permute-start.3) | collective-permute-done | bytes 262176 | tf_op jit(solution)/shard_map/ppermute | solution.py:478
  97.6 3.7 %collective-permute-done.2 = bf16[64,2048]{1,0:T(8,128)(2,1)S(1)} collective-permute-done((bf16[64,2048]{1,0:T(8,128)(2,1)S(1)}, bf16[64,2048]{1,0:T(8,128)(2,1)S(1)}, u32[]{:S(2)}, u32[]{:S(2)}) %collective-permute-start.2) | collective-permute-done | bytes 262176 | tf_op jit(solution)/shard_map/ppermute | solution.py:478
  101.4 0.2 convert_add_fusion.3
  101.6 0.1 pad_maximum_fusion
  101.7 1.5 %collective-permute-start.4 = (bf16[32,4096]{1,0:T(8,128)(2,1)S(1)}, bf16[32,4096]{1,0:T(8,128)(2,1)S(1)}, u32[]{:S(2)}, u32[]{:S(2)}) collective-permute-start(bf16[32,4096]{1,0:T(8,128)(2,1)S(1)} %fusion.3), channel_id=1, source_target_pairs={{0,1},{1,0},{2,3},{3,2},{4,5},{5,4},{6,7},{7,6},{8,9},{9,8},{10,11... | collective-permute-start | bytes 786440 | tf_op jit(solution)/shard_map/ppermute | solution.py:482
  103.2 0.0 collective-permute-done.8
  103.2 2.6 %collective-permute-done.7 = bf16[64,2048]{1,0:T(8,128)(2,1)S(1)} collective-permute-done((bf16[64,2048]{1,0:T(8,128)(2,1)S(1)}, bf16[64,2048]{1,0:T(8,128)(2,1)S(1)}, u32[]{:S(2)}, u32[]{:S(2)}) %collective-permute-start.7) | collective-permute-done | bytes 262176 | tf_op jit(solution)/shard_map/ppermute | solution.py:478
  105.9 0.2 convert_add_fusion.1
  106.1 0.1 pad_maximum_fusion.1
  106.2 1.5 %collective-permute-start.9 = (bf16[32,4096]{1,0:T(8,128)(2,1)S(1)}, bf16[32,4096]{1,0:T(8,128)(2,1)S(1)}, u32[]{:S(2)}, u32[]{:S(2)}) collective-permute-start(bf16[32,4096]{1,0:T(8,128)(2,1)S(1)} %fusion.4), channel_id=1, source_target_pairs={{0,1},{1,0},{2,3},{3,2},{4,5},{5,4},{6,7},{7,6},{8,9},{9,8},{10,11... | collective-permute-start | bytes 786440 | tf_op jit(solution)/shard_map/ppermute | solution.py:482
  107.7 8.5 %collective-permute-done.4 = bf16[32,4096]{1,0:T(8,128)(2,1)S(1)} collective-permute-done((bf16[32,4096]{1,0:T(8,128)(2,1)S(1)}, bf16[32,4096]{1,0:T(8,128)(2,1)S(1)}, u32[]{:S(2)}, u32[]{:S(2)}) %collective-permute-start.4) | collective-permute-done | bytes 262176 | tf_op jit(solution)/shard_map/ppermute | solution.py:482
  116.3 0.0 all-to-all-done.2
  116.3 3.6 %pick_pages.1 = (bf16[14,4,2,64,128]{4,3,2,1,0:T(8,128)(2,1)}, f32[1]{0:T(128)}) custom-call(s32[14]{0:T(128)} %get-tuple-element.23.slot_ref, bf16[32,4,2,64,128]{4,3,2,1,0:T(8,128)(2,1)} %bitcast.23.got_ref), custom_call_target="tpu_custom_call" | custom-call | tf_op jit(solution)/shard_map/pick_pages/pallas_call | solution.py:461
  119.9 1.4 %collective-permute-done.9 = bf16[32,4096]{1,0:T(8,128)(2,1)S(1)} collective-permute-done((bf16[32,4096]{1,0:T(8,128)(2,1)S(1)}, bf16[32,4096]{1,0:T(8,128)(2,1)S(1)}, u32[]{:S(2)}, u32[]{:S(2)}) %collective-permute-start.9) | collective-permute-done | bytes 262176 | tf_op jit(solution)/shard_map/ppermute | solution.py:482
  121.4 0.7 fusion.1
  122.1 1.1 broadcast_in_dim_reshape.7
  (15 shorter events, 0.2 us)
Async XLA Ops:
  2.8 15.7 %all-to-all-start = ((bf16[16,2,32,128]{3,2,1,0:T(8,128)(2,1)}), bf16[16,2,32,128]{3,2,1,0:T(8,128)(2,1)S(1)}, u32[]{:S(2)}, u32[]{:S(2)}) async-start(bf16[16,2,32,128]{3,2,1,0:T(8,128)(2,1)} %bitcast.56), calls=%async_computation | async-start | bytes 524288 | tf_op jit(solution)/shard_map/all_to_all | solution.py:516
  18.4 0.7 copy-start.7
  25.4 15.4 %all-to-all-start.1 = ((bf16[16,2,16,128]{3,2,1,0:T(8,128)(2,1)}), bf16[16,2,16,128]{3,2,1,0:T(8,128)(2,1)S(1)}, u32[]{:S(2)}, u32[]{:S(2)}) async-start(bf16[16,2,16,128]{3,2,1,0:T(8,128)(2,1)} %bitcast.57), calls=%async_computation.1 | async-start | bytes 262144 | tf_op jit(solution)/shard_map/all_to_all | solution.py:522
  40.9 0.7 copy-start
  41.5 74.7 %all-to-all-start.2 = ((bf16[16,2,4,2,64,128]{5,4,3,2,1,0:T(8,128)(2,1)}), bf16[16,2,4,2,64,128]{5,4,3,2,1,0:T(8,128)(2,1)}, u32[]{:S(2)}, u32[]{:S(2)}) async-start(bf16[16,2,4,2,64,128]{5,4,3,2,1,0:T(8,128)(2,1)} %bitcast.41), calls=%async_computation.2 | async-start | bytes 8388608 | tf_op jit(solution)/shard_map/all_to_all | solution.py:525
  64.2 16.7 %collective-permute-start = (bf16[128,2048]{1,0:T(8,128)(2,1)}, bf16[128,2048]{1,0:T(8,128)(2,1)S(1)}, u32[]{:S(2)}, u32[]{:S(2)}) collective-permute-start(bf16[128,2048]{1,0:T(8,128)(2,1)} %get-tuple-element.29), channel_id=1, source_target_pairs={{0,6},{1,7},{2,0},{3,1},{4,2},{5,3},{6,4},{7,5},{8,14},{9,15},{10,... | collective-permute-start | bytes 1572872 | tf_op jit(solution)/shard_map/ppermute | solution.py:478
  68.3 16.3 %collective-permute-start.1 = (bf16[128,2048]{1,0:T(8,128)(2,1)}, bf16[128,2048]{1,0:T(8,128)(2,1)S(1)}, u32[]{:S(2)}, u32[]{:S(2)}) collective-permute-start(bf16[128,2048]{1,0:T(8,128)(2,1)} %get-tuple-element.31), channel_id=1, source_target_pairs={{0,2},{1,3},{2,4},{3,5},{4,6},{5,7},{6,0},{7,1},{8,10},{9,11},{10,... | collective-permute-start | bytes 1572872 | tf_op jit(solution)/shard_map/ppermute | solution.py:478
  68.3 12.6 %copy-start.6 = (bf16[64,2048]{1,0:T(8,128)(2,1)S(1)}, bf16[64,2048]{1,0:T(8,128)(2,1)}, u32[]{:S(2)}) copy-start(bf16[64,2048]{1,0:T(8,128)(2,1)} %get-tuple-element.32) | copy-start | bytes 786436
  68.3 16.3 %copy-start.5 = (bf16[64,2048]{1,0:T(8,128)(2,1)S(1)}, bf16[64,2048]{1,0:T(8,128)(2,1)}, u32[]{:S(2)}) copy-start(bf16[64,2048]{1,0:T(8,128)(2,1)} %get-tuple-element.30) | copy-start | bytes 786436
  68.3 23.8 %copy-start.4 = (bf16[64,2048]{1,0:T(8,128)(2,1)S(1)}, bf16[64,2048]{1,0:T(8,128)(2,1)}, u32[]{:S(2)}) copy-start(bf16[64,2048]{1,0:T(8,128)(2,1)} %get-tuple-element.39) | copy-start | bytes 786436
  68.3 27.6 %copy-start.3 = (bf16[64,2048]{1,0:T(8,128)(2,1)S(1)}, bf16[64,2048]{1,0:T(8,128)(2,1)}, u32[]{:S(2)}) copy-start(bf16[64,2048]{1,0:T(8,128)(2,1)} %get-tuple-element.37) | copy-start | bytes 786436
  68.3 33.1 %copy-start.2 = (bf16[64,4096]{1,0:T(8,128)(2,1)S(1)}, bf16[64,4096]{1,0:T(8,128)(2,1)}, u32[]{:S(2)}) copy-start(bf16[64,4096]{1,0:T(8,128)(2,1)} %get-tuple-element.28) | copy-start | bytes 1572868
  68.3 23.8 %collective-permute-start.5 = (bf16[128,2048]{1,0:T(8,128)(2,1)}, bf16[128,2048]{1,0:T(8,128)(2,1)S(1)}, u32[]{:S(2)}, u32[]{:S(2)}) collective-permute-start(bf16[128,2048]{1,0:T(8,128)(2,1)} %get-tuple-element.36), channel_id=1, source_target_pairs={{0,6},{1,7},{2,0},{3,1},{4,2},{5,3},{6,4},{7,5},{8,14},{9,15},{10,... | collective-permute-start | bytes 1572872 | tf_op jit(solution)/shard_map/ppermute | solution.py:478
  71.6 24.2 %collective-permute-start.6 = (bf16[128,2048]{1,0:T(8,128)(2,1)}, bf16[128,2048]{1,0:T(8,128)(2,1)S(1)}, u32[]{:S(2)}, u32[]{:S(2)}) collective-permute-start(bf16[128,2048]{1,0:T(8,128)(2,1)} %get-tuple-element.38), channel_id=1, source_target_pairs={{0,2},{1,3},{2,4},{3,5},{4,6},{5,7},{6,0},{7,1},{8,10},{9,11},{10,... | collective-permute-start | bytes 1572872 | tf_op jit(solution)/shard_map/ppermute | solution.py:478
  80.9 25.0 %copy-start.1 = (bf16[64,4096]{1,0:T(8,128)(2,1)S(1)}, bf16[64,4096]{1,0:T(8,128)(2,1)}, u32[]{:S(2)}) copy-start(bf16[64,4096]{1,0:T(8,128)(2,1)} %get-tuple-element.33) | copy-start | bytes 1572868
  81.0 16.7 %collective-permute-start.3 = (bf16[64,2048]{1,0:T(8,128)(2,1)S(1)}, bf16[64,2048]{1,0:T(8,128)(2,1)S(1)}, u32[]{:S(2)}, u32[]{:S(2)}) collective-permute-start(bf16[64,2048]{1,0:T(8,128)(2,1)S(1)} %add_convert_fusion.2), channel_id=1, source_target_pairs={{0,6},{1,7},{2,0},{3,1},{4,2},{5,3},{6,4},{7,5},{8,14},{9,15},{10,... | collective-permute-start | bytes 786440 | tf_op jit(solution)/shard_map/ppermute | solution.py:478
  84.7 16.7 %collective-permute-start.2 = (bf16[64,2048]{1,0:T(8,128)(2,1)S(1)}, bf16[64,2048]{1,0:T(8,128)(2,1)S(1)}, u32[]{:S(2)}, u32[]{:S(2)}) collective-permute-start(bf16[64,2048]{1,0:T(8,128)(2,1)S(1)} %add_convert_fusion.3), channel_id=1, source_target_pairs={{0,2},{1,3},{2,4},{3,5},{4,6},{5,7},{6,0},{7,1},{8,10},{9,11},{10,... | collective-permute-start | bytes 786440 | tf_op jit(solution)/shard_map/ppermute | solution.py:478
  92.2 11.0 %collective-permute-start.8 = (bf16[64,2048]{1,0:T(8,128)(2,1)S(1)}, bf16[64,2048]{1,0:T(8,128)(2,1)S(1)}, u32[]{:S(2)}, u32[]{:S(2)}) collective-permute-start(bf16[64,2048]{1,0:T(8,128)(2,1)S(1)} %add_convert_fusion), channel_id=1, source_target_pairs={{0,6},{1,7},{2,0},{3,1},{4,2},{5,3},{6,4},{7,5},{8,14},{9,15},{10,... | collective-permute-start | bytes 786440 | tf_op jit(solution)/shard_map/ppermute | solution.py:478
  95.9 9.9 %collective-permute-start.7 = (bf16[64,2048]{1,0:T(8,128)(2,1)S(1)}, bf16[64,2048]{1,0:T(8,128)(2,1)S(1)}, u32[]{:S(2)}, u32[]{:S(2)}) collective-permute-start(bf16[64,2048]{1,0:T(8,128)(2,1)S(1)} %add_convert_fusion.1), channel_id=1, source_target_pairs={{0,2},{1,3},{2,4},{3,5},{4,6},{5,7},{6,0},{7,1},{8,10},{9,11},{10,... | collective-permute-start | bytes 786440 | tf_op jit(solution)/shard_map/ppermute | solution.py:478
  101.7 14.5 %collective-permute-start.4 = (bf16[32,4096]{1,0:T(8,128)(2,1)S(1)}, bf16[32,4096]{1,0:T(8,128)(2,1)S(1)}, u32[]{:S(2)}, u32[]{:S(2)}) collective-permute-start(bf16[32,4096]{1,0:T(8,128)(2,1)S(1)} %fusion.3), channel_id=1, source_target_pairs={{0,1},{1,0},{2,3},{3,2},{4,5},{5,4},{6,7},{7,6},{8,9},{9,8},{10,11... | collective-permute-start | bytes 786440 | tf_op jit(solution)/shard_map/ppermute | solution.py:482
  106.2 15.1 %collective-permute-start.9 = (bf16[32,4096]{1,0:T(8,128)(2,1)S(1)}, bf16[32,4096]{1,0:T(8,128)(2,1)S(1)}, u32[]{:S(2)}, u32[]{:S(2)}) collective-permute-start(bf16[32,4096]{1,0:T(8,128)(2,1)S(1)} %fusion.4), channel_id=1, source_target_pairs={{0,1},{1,0},{2,3},{3,2},{4,5},{5,4},{6,7},{7,6},{8,9},{9,8},{10,11... | collective-permute-start | bytes 786440 | tf_op jit(solution)/shard_map/ppermute | solution.py:482

commit v4 on v3

--- a/solution.py
+++ b/solution.py
@@ -34,6 +34,7 @@
 SMEM = pl.BlockSpec(memory_space=pltpu.SMEM)
 HBM = pl.BlockSpec(memory_space=pltpu.HBM)
 PARAMS = pltpu.CompilerParams(vmem_limit_bytes=60 * 2**20)
+ROOMY = pltpu.CompilerParams(vmem_limit_bytes=52 * 2**20)
 
 
 def attend_group(tokens, queries, fresh, pages, lengths, pool_ref, scores_ref):
@@ -169,7 +170,8 @@
     return started
 
 
-def stay_kernel(table_ref, length_ref, query_hbm, fresh_hbm, pool_hbm, out_ref, *refs):
+def stay_kernel(table_ref, length_ref, query_hbm, fresh_hbm, pool_hbm, out_ref, turn_ref, *refs):
+    turn_ref[...] = jnp.zeros_like(turn_ref)
     attend_staying(0, FIRST, table_ref, length_ref, query_hbm, fresh_hbm, pool_hbm, out_ref, 0, refs)
 
 
@@ -193,9 +195,9 @@
 def stay(table, lengths, query, fresh, pool, count):
     return pl.pallas_call(
         stay_kernel,
-        out_shape=jax.ShapeDtypeStruct((count, 8, 2, HEAD), jnp.bfloat16),
+        out_shape=(jax.ShapeDtypeStruct((count, 8, 2, HEAD), jnp.bfloat16), pltpu.VMEM((8, HEAD), jnp.float32)),
         in_specs=[SMEM, SMEM, HBM, HBM, HBM],
-        out_specs=VMEM,
+        out_specs=(VMEM, VMEM),
         scratch_shapes=stay_scratch(pool, count),
         compiler_params=PARAMS,
         cost_estimate=pl.CostEstimate(flops=8 * 10**9, bytes_accessed=8 * 2**20, transcendentals=0),
@@ -301,7 +303,7 @@
             pltpu.SemaphoreType.DMA((WEIGHT_PARTS,)),
             pltpu.SemaphoreType.DMA((WEIGHT_PARTS, 4)),
         ],
-        compiler_params=PARAMS,
+        compiler_params=ROOMY,
         cost_estimate=pl.CostEstimate(flops=10**9, bytes_accessed=2**20, transcendentals=0),
         name="attend_third_project",
     )(slots, table, lengths, query, fresh, pool, first, second, returned, weight)
@@ -349,10 +351,10 @@
         length = length_ref[0, row]
         meta = jnp.where(lane == 20, length // 32, meta)
         meta = jnp.where(lane == 21, lax.rem(length, 32), meta)
-        out_ref[slot, 0:16] = query_ref[row].reshape(16, HEAD)
+        out_ref[slot, 0:16] = query_ref[row - (ROWS - 16)].reshape(16, HEAD)
         out_ref[slot, 16:32] = jnp.concatenate(
             [
-                fresh_ref[row].astype(jnp.float32).reshape(4, HEAD),
+                fresh_ref[row - (ROWS - 16)].astype(jnp.float32).reshape(4, HEAD),
                 meta.astype(jnp.float32),
                 jnp.zeros((11, HEAD), jnp.float32),
             ],
@@ -367,7 +369,9 @@
             jax.ShapeDtypeStruct((SLOTS, 32, HEAD), jnp.bfloat16),
             jax.ShapeDtypeStruct((MIGRANTS,), jnp.int32),
         ),
-        in_specs=[SMEM] * 4 + [VMEM] * 2,
+        grid=(1,),
+        in_specs=[SMEM] * 4
+        + [pl.BlockSpec((16, 8, 2, HEAD), lambda i: (7, 0, 0, 0)), pl.BlockSpec((16, 2, 2, HEAD), lambda i: (7, 0, 0, 0))],
         out_specs=(VMEM, SMEM),
         scratch_shapes=[pltpu.SMEM((REPLICAS,), jnp.int32)],
         compiler_params=PARAMS,
@@ -425,7 +429,7 @@
             jax.ShapeDtypeStruct((SLOTS, COPIED, 2, PAGE, HEAD), jnp.bfloat16),
             jax.ShapeDtypeStruct((1,), jnp.int32),
         ),
-        in_specs=[VMEM, HBM, HBM],
+        in_specs=[VMEM, VMEM, HBM],
         out_specs=(VMEM, HBM, SMEM),
         scratch_shapes=attention_scratch(pool)
         + [
@@ -435,7 +439,7 @@
             pltpu.SemaphoreType.DMA,
             pltpu.SemaphoreType.DMA,
         ],
-        compiler_params=PARAMS,
+        compiler_params=ROOMY,
         cost_estimate=pl.CostEstimate(flops=6 * 10**9, bytes_accessed=8 * 2**20, transcendentals=0),
         name="serve_requests",
     )(got, after, pool)
@@ -516,8 +520,8 @@
     got = lax.all_to_all(
         payload.reshape(REPLICAS, CAP, 32, HEAD), "replica", split_axis=0, concat_axis=0, tiled=True
     ).reshape(SLOTS, 32, HEAD)
-    first = stay(table, lengths, query, fresh, pool, FIRST)
-    answered, sending, unused = serve(got, first, pool)
+    first, turn = stay(table, lengths, query, fresh, pool, FIRST)
+    answered, sending, unused = serve(got, turn, pool)
     second = attend_second(unused, table, lengths, query, fresh, pool)
     returned = lax.all_to_all(
         answered.reshape(REPLICAS, CAP, 16, HEAD), "replica", split_axis=0, concat_axis=0, tiled=True

time: 124 us -> 121 us (0.976)
  local copies, waits for them, and re-layouts: 2.58 us -> 1.25 us
    unnamed x16, local copies, waits for them, and re-layouts: 1.37 us -> 0.04 us
  transfers between devices with their start and end apart: 13 -> 13, of which waited for: 7 -> 7; matrix products, arithmetic and copies ran while one was open for 1% -> 1% of each run, Pallas kernels for 29% -> 30%
where the time goes in v4:
time: 121 us
  Pallas kernels  43.5 us (36%)
  starting transfers between devices  38.6 us (32%)
  waiting for transfers between devices  34.9 us (29%)
  other arithmetic  1.59 us (1%)
  local copies, waits for them, and re-layouts  1.25 us (1%)
    ppermute x8, waiting for transfers between devices, shift_z(): return lax.ppermute(value, 'tensor', pairs)  24.7 us
    pallas_call x1, Pallas kernels, project(): pl.pallas_call(project_kernel, out_shape=[jax.ShapeDtypeStruct((ROWS, 8,...  15.3 us
    ppermute x8, starting transfers between devices, shift_z(): return lax.ppermute(value, 'tensor', pairs)  14.8 us
    ppermute x2, waiting for transfers between devices, swap_x(): return lax.ppermute(value, 'tensor', [(t, t ^ 1) for t in range(8)])  10.1 us
    pallas_call x1, Pallas kernels, stay(): pl.pallas_call(stay_kernel, out_shape=(jax.ShapeDtypeStruct((count, 8, 2,...  9.27 us
    pallas_call x1, Pallas kernels, attend_second(): pl.pallas_call(second_kernel, out_shape=jax.ShapeDtypeStruct((SECOND, 8,...  7.98 us
    all_to_all x1, starting transfers between devices, body(): lax.all_to_all(sending.reshape(REPLICAS, CAP, COPIED, 2, PAGE, HEAD), 're...  7.37 us
    all_to_all x1, starting transfers between devices, body(): lax.all_to_all(answered.reshape(REPLICAS, CAP, 16, HEAD), 'replica', spli...  6.94 us
  transfers between devices with their start and end apart: 13, of which 7 were waited for; matrix products, arithmetic and copies ran while one was open for 1% of the time, Pallas kernels for 30%

profile of v4, /device:TPU:10, one launch (start us, length us, event | category | flops | bytes accessed | tf_op | source)
XLA Modules:
  0.0 120.8 jit_solution(6067438482441702954)
XLA Ops:
  0.6 2.0 %pack_requests.1 = (bf16[32,32,128]{2,1,0:T(8,128)(2,1)}, s32[14]{0:T(128)}) custom-call(s32[1,14]{1,0:T(1,128)} %bitcast.62, s32[14,1,16]{2,1,0:T(1,128)} %bitcast.61, s32[16,128]{1,0:T(8,128)} %bitcast.43, s32[1,128]{1,0:T(1,128)} %length_ref.7, bf16[128,8,2,128]{3,2,1,0:T(2,128)(2,1)} %bitcast.56, bf16[128,2,2,128]{3,2,1,0:T(2,128)(2,1)} %bitcast.38), custom_call_target="tpu_custom_call" | custom-call | tf_op jit(solution)/shard_map/pack_requests/pallas_call | solution.py:366
  2.6 6.5 %all-to-all-start = ((bf16[16,2,32,128]{3,2,1,0:T(8,128)(2,1)}), bf16[16,2,32,128]{3,2,1,0:T(8,128)(2,1)S(1)}, u32[]{:S(2)}, u32[]{:S(2)}) async-start(bf16[16,2,32,128]{3,2,1,0:T(8,128)(2,1)} %bitcast.60), calls=%async_computation | async-start | bytes 524288 | tf_op jit(solution)/shard_map/all_to_all | solution.py:520
  9.1 9.3 %attend_first.1 = (bf16[48,8,2,128]{3,2,1,0:T(2,128)(2,1)}, f32[8,128]{1,0:T(8,128)S(1)}) custom-call(s32[16,128]{1,0:T(8,128)} %bitcast.44, s32[1,128]{1,0:T(1,128)} %length_ref.7, bf16[128,8,2,128]{3,2,1,0:T(2,128)(2,1)} %bitcast.57, bf16[128,2,2,128]{3,2,1,0:T(2,128)(2,1)} %bitcast.39, bf16[2,128,64,128]{3,2,1,0:T(8,128)(2,1)} %bitcast.47), custom_call_target="tpu_custom_call" | custom-call | flops 8000000000 | bytes 8388608 | tf_op jit(solution)/shard_map/attend_first/pallas_call | solution.py:196
  18.4 0.0 all-to-all-done
  18.4 5.4 %serve_requests.1 = (bf16[32,16,128]{2,1,0:T(8,128)(2,1)}, bf16[32,4,2,64,128]{4,3,2,1,0:T(8,128)(2,1)}, s32[1]{0:T(128)}) custom-call(bf16[32,32,128]{2,1,0:T(8,128)(2,1)S(1)} %bitcast.42, f32[8,128]{1,0:T(8,128)S(1)} %get-tuple-element.28.after_ref, bf16[2,128,64,128]{3,2,1,0:T(8,128)(2,1)} %bitcast.48), custom_call_target="tpu_custom_call" | custom-call | flops 6000000000 | bytes 8388608 | tf_op jit(solution)/shard_map/serve_requests/pallas_call | solution.py:425
  23.8 6.9 %all-to-all-start.1 = ((bf16[16,2,16,128]{3,2,1,0:T(8,128)(2,1)}), bf16[16,2,16,128]{3,2,1,0:T(8,128)(2,1)S(1)}, u32[]{:S(2)}, u32[]{:S(2)}) async-start(bf16[16,2,16,128]{3,2,1,0:T(8,128)(2,1)} %bitcast.12), calls=%async_computation.1 | async-start | bytes 262144 | tf_op jit(solution)/shard_map/all_to_all | solution.py:526
  30.7 8.0 %attend_second.1.second_ref = bf16[32,8,2,128]{3,2,1,0:T(2,128)(2,1)} custom-call(s32[1]{0:T(128)} %get-tuple-element.29.after_ref, s32[16,128]{1,0:T(8,128)} %bitcast.45, s32[1,128]{1,0:T(1,128)} %length_ref.7, bf16[128,8,2,128]{3,2,1,0:T(2,128)(2,1)} %bitcast.58, bf16[128,2,2,128]{3,2,1,0:T(2,128)(2,1)} %bitcast.40, bf16[2,128,64,128]{3,2,1,0:T(8,128)(2,1)} %bitcast.49), custom_call_target="tpu_custom_call" | custom-call | flops 8000000000 | bytes 8388608 | tf_op jit(solution)/shard_map/attend_second/pallas_call | solution.py:223
  38.7 0.0 all-to-all-done.1
  38.7 0.0 copy-start
  38.7 0.0 copy-start.1
  38.8 0.0 copy-start.2
  38.8 0.0 copy-start.3
  38.8 0.0 copy-start.5
  38.8 7.4 %all-to-all-start.2 = ((bf16[16,2,4,2,64,128]{5,4,3,2,1,0:T(8,128)(2,1)}), bf16[16,2,4,2,64,128]{5,4,3,2,1,0:T(8,128)(2,1)}, u32[]{:S(2)}, u32[]{:S(2)}) async-start(bf16[16,2,4,2,64,128]{5,4,3,2,1,0:T(8,128)(2,1)} %bitcast.51), calls=%async_computation.2 | async-start | bytes 8388608 | tf_op jit(solution)/shard_map/all_to_all | solution.py:529
  46.2 0.0 copy-done.1
  46.2 15.3 %attend_third_project.1 = (bf16[128,8,2,128]{3,2,1,0:T(2,128)(2,1)}, bf16[64,4096]{1,0:T(8,128)(2,1)}, bf16[128,2048]{1,0:T(8,128)(2,1)}, bf16[128,2048]{1,0:T(8...) custom-call(s32[14]{0:T(128)S(1)} %copy-done.4, ...), custom_call_target="tpu_custom_call" | custom-call | flops 1000000000 | bytes 1048576 | tf_op jit(solution)/shard_map/attend_third_project/pallas_call | solution.py:292
  61.5 4.1 %collective-permute-start = (bf16[128,2048]{1,0:T(8,128)(2,1)}, bf16[128,2048]{1,0:T(8,128)(2,1)S(1)}, u32[]{:S(2)}, u32[]{:S(2)}) collective-permute-start(bf16[128,2048]{1,0:T(8,128)(2,1)} %get-tuple-element.33), channel_id=1, source_target_pairs={{0,6},{1,7},{2,0},{3,1},{4,2},{5,3},{6,4},{7,5},{8,14},{9,15},{10,... | collective-permute-start | bytes 1572872 | tf_op jit(solution)/shard_map/ppermute | solution.py:482
  65.6 0.0 collective-permute-start.1
  65.6 3.2 %collective-permute-start.5 = (bf16[128,2048]{1,0:T(8,128)(2,1)}, bf16[128,2048]{1,0:T(8,128)(2,1)S(1)}, u32[]{:S(2)}, u32[]{:S(2)}) collective-permute-start(bf16[128,2048]{1,0:T(8,128)(2,1)} %get-tuple-element.40), channel_id=1, source_target_pairs={{0,6},{1,7},{2,0},{3,1},{4,2},{5,3},{6,4},{7,5},{8,14},{9,15},{10,... | collective-permute-start | bytes 1572872 | tf_op jit(solution)/shard_map/ppermute | solution.py:482
  68.9 0.0 collective-permute-start.6
  68.9 9.4 %collective-permute-done = bf16[128,2048]{1,0:T(8,128)(2,1)S(1)} collective-permute-done((bf16[128,2048]{1,0:T(8,128)(2,1)}, bf16[128,2048]{1,0:T(8,128)(2,1)S(1)}, u32[]{:S(2)}, u32[]{:S(2)}) %collective-permute-start) | collective-permute-done | bytes 524320 | tf_op jit(solution)/shard_map/ppermute | solution.py:482
  78.2 0.1 add_convert_fusion.2
  78.3 3.7 %collective-permute-start.3 = (bf16[64,2048]{1,0:T(8,128)(2,1)S(1)}, bf16[64,2048]{1,0:T(8,128)(2,1)S(1)}, u32[]{:S(2)}, u32[]{:S(2)}) collective-permute-start(bf16[64,2048]{1,0:T(8,128)(2,1)S(1)} %add_convert_fusion.2), channel_id=1, source_target_pairs={{0,6},{1,7},{2,0},{3,1},{4,2},{5,3},{6,4},{7,5},{8,14},{9,15},{10,... | collective-permute-start | bytes 786440 | tf_op jit(solution)/shard_map/ppermute | solution.py:482
  81.9 0.0 collective-permute-done.1
  82.0 0.1 add_convert_fusion.3
  82.0 0.1 collective-permute-start.2
  82.1 7.4 %collective-permute-done.5 = bf16[128,2048]{1,0:T(8,128)(2,1)S(1)} collective-permute-done((bf16[128,2048]{1,0:T(8,128)(2,1)}, bf16[128,2048]{1,0:T(8,128)(2,1)S(1)}, u32[]{:S(2)}, u32[]{:S(2)}) %collective-permute-start.5) | collective-permute-done | bytes 524320 | tf_op jit(solution)/shard_map/ppermute | solution.py:482
  89.5 0.1 add_convert_fusion
  89.5 3.7 %collective-permute-start.8 = (bf16[64,2048]{1,0:T(8,128)(2,1)S(1)}, bf16[64,2048]{1,0:T(8,128)(2,1)S(1)}, u32[]{:S(2)}, u32[]{:S(2)}) collective-permute-start(bf16[64,2048]{1,0:T(8,128)(2,1)S(1)} %add_convert_fusion), channel_id=1, source_target_pairs={{0,6},{1,7},{2,0},{3,1},{4,2},{5,3},{6,4},{7,5},{8,14},{9,15},{10,... | collective-permute-start | bytes 786440 | tf_op jit(solution)/shard_map/ppermute | solution.py:482
  93.2 0.0 collective-permute-done.6
  93.2 0.1 add_convert_fusion.1
  93.3 0.1 collective-permute-start.7
  93.3 1.6 %collective-permute-done.3 = bf16[64,2048]{1,0:T(8,128)(2,1)S(1)} collective-permute-done((bf16[64,2048]{1,0:T(8,128)(2,1)S(1)}, bf16[64,2048]{1,0:T(8,128)(2,1)S(1)}, u32[]{:S(2)}, u32[]{:S(2)}) %collective-permute-start.3) | collective-permute-done | bytes 262176 | tf_op jit(solution)/shard_map/ppermute | solution.py:482
  95.0 3.7 %collective-permute-done.2 = bf16[64,2048]{1,0:T(8,128)(2,1)S(1)} collective-permute-done((bf16[64,2048]{1,0:T(8,128)(2,1)S(1)}, bf16[64,2048]{1,0:T(8,128)(2,1)S(1)}, u32[]{:S(2)}, u32[]{:S(2)}) %collective-permute-start.2) | collective-permute-done | bytes 262176 | tf_op jit(solution)/shard_map/ppermute | solution.py:482
  98.7 0.2 convert_add_fusion.3
  98.9 0.1 pad_maximum_fusion
  99.0 1.5 %collective-permute-start.4 = (bf16[32,4096]{1,0:T(8,128)(2,1)S(1)}, bf16[32,4096]{1,0:T(8,128)(2,1)S(1)}, u32[]{:S(2)}, u32[]{:S(2)}) collective-permute-start(bf16[32,4096]{1,0:T(8,128)(2,1)S(1)} %fusion.3), channel_id=1, source_target_pairs={{0,1},{1,0},{2,3},{3,2},{4,5},{5,4},{6,7},{7,6},{8,9},{9,8},{10,11... | collective-permute-start | bytes 786440 | tf_op jit(solution)/shard_map/ppermute | solution.py:486
  100.6 0.0 collective-permute-done.8
  100.6 2.7 %collective-permute-done.7 = bf16[64,2048]{1,0:T(8,128)(2,1)S(1)} collective-permute-done((bf16[64,2048]{1,0:T(8,128)(2,1)S(1)}, bf16[64,2048]{1,0:T(8,128)(2,1)S(1)}, u32[]{:S(2)}, u32[]{:S(2)}) %collective-permute-start.7) | collective-permute-done | bytes 262176 | tf_op jit(solution)/shard_map/ppermute | solution.py:482
  103.2 0.2 convert_add_fusion.1
  103.4 0.1 pad_maximum_fusion.1
  103.5 1.5 %collective-permute-start.9 = (bf16[32,4096]{1,0:T(8,128)(2,1)S(1)}, bf16[32,4096]{1,0:T(8,128)(2,1)S(1)}, u32[]{:S(2)}, u32[]{:S(2)}) collective-permute-start(bf16[32,4096]{1,0:T(8,128)(2,1)S(1)} %fusion.4), channel_id=1, source_target_pairs={{0,1},{1,0},{2,3},{3,2},{4,5},{5,4},{6,7},{7,6},{8,9},{9,8},{10,11... | collective-permute-start | bytes 786440 | tf_op jit(solution)/shard_map/ppermute | solution.py:486
  105.1 8.7 %collective-permute-done.4 = bf16[32,4096]{1,0:T(8,128)(2,1)S(1)} collective-permute-done((bf16[32,4096]{1,0:T(8,128)(2,1)S(1)}, bf16[32,4096]{1,0:T(8,128)(2,1)S(1)}, u32[]{:S(2)}, u32[]{:S(2)}) %collective-permute-start.4) | collective-permute-done | bytes 262176 | tf_op jit(solution)/shard_map/ppermute | solution.py:486
  113.8 0.0 all-to-all-done.2
  113.8 3.6 %pick_pages.1 = (bf16[14,4,2,64,128]{4,3,2,1,0:T(8,128)(2,1)}, f32[1]{0:T(128)}) custom-call(s32[14]{0:T(128)} %get-tuple-element.25.slot_ref, bf16[32,4,2,64,128]{4,3,2,1,0:T(8,128)(2,1)} %bitcast.23.got_ref), custom_call_target="tpu_custom_call" | custom-call | tf_op jit(solution)/shard_map/pick_pages/pallas_call | solution.py:465
  117.4 1.4 %collective-permute-done.9 = bf16[32,4096]{1,0:T(8,128)(2,1)S(1)} collective-permute-done((bf16[32,4096]{1,0:T(8,128)(2,1)S(1)}, bf16[32,4096]{1,0:T(8,128)(2,1)S(1)}, u32[]{:S(2)}, u32[]{:S(2)}) %collective-permute-start.9) | collective-permute-done | bytes 262176 | tf_op jit(solution)/shard_map/ppermute | solution.py:486
  118.9 0.7 fusion.1
  119.6 1.1 broadcast_in_dim_reshape.7
  (15 shorter events, 0.2 us)
Async XLA Ops:
  2.6 15.8 %all-to-all-start = ((bf16[16,2,32,128]{3,2,1,0:T(8,128)(2,1)}), bf16[16,2,32,128]{3,2,1,0:T(8,128)(2,1)S(1)}, u32[]{:S(2)}, u32[]{:S(2)}) async-start(bf16[16,2,32,128]{3,2,1,0:T(8,128)(2,1)} %bitcast.60), calls=%async_computation | async-start | bytes 524288 | tf_op jit(solution)/shard_map/all_to_all | solution.py:520
  23.8 14.9 %all-to-all-start.1 = ((bf16[16,2,16,128]{3,2,1,0:T(8,128)(2,1)}), bf16[16,2,16,128]{3,2,1,0:T(8,128)(2,1)S(1)}, u32[]{:S(2)}, u32[]{:S(2)}) async-start(bf16[16,2,16,128]{3,2,1,0:T(8,128)(2,1)} %bitcast.12), calls=%async_computation.1 | async-start | bytes 262144 | tf_op jit(solution)/shard_map/all_to_all | solution.py:526
  38.7 7.4 %copy-start = (bf16[1,128,2,2,128]{4,3,2,1,0:T(2,128)(2,1)S(1)}, bf16[1,128,2,2,128]{4,3,2,1,0:T(2,128)(2,1)}, u32[]{:S(2)}) copy-start(bf16[1,128,2,2,128]{4,3,2,1,0:T(2,128)(2,1)} %param.9) | copy-start | bytes 393220
  38.7 7.4 %copy-start.1 = (bf16[48,8,2,128]{3,2,1,0:T(2,128)(2,1)S(1)}, bf16[48,8,2,128]{3,2,1,0:T(2,128)(2,1)}, u32[]{:S(2)}) copy-start(bf16[48,8,2,128]{3,2,1,0:T(2,128)(2,1)} %get-tuple-element.26.first_ref) | copy-start | bytes 589828
  38.8 7.4 %copy-start.2 = (bf16[32,8,2,128]{3,2,1,0:T(2,128)(2,1)S(1)}, bf16[32,8,2,128]{3,2,1,0:T(2,128)(2,1)}, u32[]{:S(2)}) copy-start(bf16[32,8,2,128]{3,2,1,0:T(2,128)(2,1)} %attend_second.1.second_ref) | copy-start | bytes 393220
  38.8 7.4 %copy-start.3 = (s32[1,128,16]{1,2,0:T(8,128)S(1)}, s32[1,128,16]{1,2,0:T(8,128)}, u32[]{:S(2)}) copy-start(s32[1,128,16]{1,2,0:T(8,128)} %param.11) | copy-start | bytes 24580
  38.8 7.4 %copy-start.4 = (s32[14]{0:T(128)S(1)}, s32[14]{0:T(128)}, u32[]{:S(2)}) copy-start(s32[14]{0:T(128)} %get-tuple-element.25.slot_ref) | copy-start | bytes 172
  38.8 7.4 %copy-start.5 = (s32[1,128]{1,0:T(1,128)S(1)}, s32[1,128]{1,0:T(1,128)}, u32[]{:S(2)}) copy-start(s32[1,128]{1,0:T(1,128)} %length_ref.7) | copy-start | bytes 1540
  38.8 75.0 %all-to-all-start.2 = ((bf16[16,2,4,2,64,128]{5,4,3,2,1,0:T(8,128)(2,1)}), bf16[16,2,4,2,64,128]{5,4,3,2,1,0:T(8,128)(2,1)}, u32[]{:S(2)}, u32[]{:S(2)}) async-start(bf16[16,2,4,2,64,128]{5,4,3,2,1,0:T(8,128)(2,1)} %bitcast.51), calls=%async_computation.2 | async-start | bytes 8388608 | tf_op jit(solution)/shard_map/all_to_all | solution.py:529
  61.5 16.7 %collective-permute-start = (bf16[128,2048]{1,0:T(8,128)(2,1)}, bf16[128,2048]{1,0:T(8,128)(2,1)S(1)}, u32[]{:S(2)}, u32[]{:S(2)}) collective-permute-start(bf16[128,2048]{1,0:T(8,128)(2,1)} %get-tuple-element.33), channel_id=1, source_target_pairs={{0,6},{1,7},{2,0},{3,1},{4,2},{5,3},{6,4},{7,5},{8,14},{9,15},{10,... | collective-permute-start | bytes 1572872 | tf_op jit(solution)/shard_map/ppermute | solution.py:482
  65.6 16.3 %collective-permute-start.1 = (bf16[128,2048]{1,0:T(8,128)(2,1)}, bf16[128,2048]{1,0:T(8,128)(2,1)S(1)}, u32[]{:S(2)}, u32[]{:S(2)}) collective-permute-start(bf16[128,2048]{1,0:T(8,128)(2,1)} %get-tuple-element.35), channel_id=1, source_target_pairs={{0,2},{1,3},{2,4},{3,5},{4,6},{5,7},{6,0},{7,1},{8,10},{9,11},{10,... | collective-permute-start | bytes 1572872 | tf_op jit(solution)/shard_map/ppermute | solution.py:482
  65.6 33.1 %copy-start.7 = (bf16[64,4096]{1,0:T(8,128)(2,1)S(1)}, bf16[64,4096]{1,0:T(8,128)(2,1)}, u32[]{:S(2)}) copy-start(bf16[64,4096]{1,0:T(8,128)(2,1)} %get-tuple-element.32) | copy-start | bytes 1572868
  65.6 23.8 %collective-permute-start.5 = (bf16[128,2048]{1,0:T(8,128)(2,1)}, bf16[128,2048]{1,0:T(8,128)(2,1)S(1)}, u32[]{:S(2)}, u32[]{:S(2)}) collective-permute-start(bf16[128,2048]{1,0:T(8,128)(2,1)} %get-tuple-element.40), channel_id=1, source_target_pairs={{0,6},{1,7},{2,0},{3,1},{4,2},{5,3},{6,4},{7,5},{8,14},{9,15},{10,... | collective-permute-start | bytes 1572872 | tf_op jit(solution)/shard_map/ppermute | solution.py:482
  68.9 24.3 %collective-permute-start.6 = (bf16[128,2048]{1,0:T(8,128)(2,1)}, bf16[128,2048]{1,0:T(8,128)(2,1)S(1)}, u32[]{:S(2)}, u32[]{:S(2)}) collective-permute-start(bf16[128,2048]{1,0:T(8,128)(2,1)} %get-tuple-element.42), channel_id=1, source_target_pairs={{0,2},{1,3},{2,4},{3,5},{4,6},{5,7},{6,0},{7,1},{8,10},{9,11},{10,... | collective-permute-start | bytes 1572872 | tf_op jit(solution)/shard_map/ppermute | solution.py:482
  78.2 25.0 %copy-start.6 = (bf16[64,4096]{1,0:T(8,128)(2,1)S(1)}, bf16[64,4096]{1,0:T(8,128)(2,1)}, u32[]{:S(2)}) copy-start(bf16[64,4096]{1,0:T(8,128)(2,1)} %get-tuple-element.37) | copy-start | bytes 1572868
  78.3 16.7 %collective-permute-start.3 = (bf16[64,2048]{1,0:T(8,128)(2,1)S(1)}, bf16[64,2048]{1,0:T(8,128)(2,1)S(1)}, u32[]{:S(2)}, u32[]{:S(2)}) collective-permute-start(bf16[64,2048]{1,0:T(8,128)(2,1)S(1)} %add_convert_fusion.2), channel_id=1, source_target_pairs={{0,6},{1,7},{2,0},{3,1},{4,2},{5,3},{6,4},{7,5},{8,14},{9,15},{10,... | collective-permute-start | bytes 786440 | tf_op jit(solution)/shard_map/ppermute | solution.py:482
  82.0 16.7 %collective-permute-start.2 = (bf16[64,2048]{1,0:T(8,128)(2,1)S(1)}, bf16[64,2048]{1,0:T(8,128)(2,1)S(1)}, u32[]{:S(2)}, u32[]{:S(2)}) collective-permute-start(bf16[64,2048]{1,0:T(8,128)(2,1)S(1)} %add_convert_fusion.3), channel_id=1, source_target_pairs={{0,2},{1,3},{2,4},{3,5},{4,6},{5,7},{6,0},{7,1},{8,10},{9,11},{10,... | collective-permute-start | bytes 786440 | tf_op jit(solution)/shard_map/ppermute | solution.py:482
  89.5 11.0 %collective-permute-start.8 = (bf16[64,2048]{1,0:T(8,128)(2,1)S(1)}, bf16[64,2048]{1,0:T(8,128)(2,1)S(1)}, u32[]{:S(2)}, u32[]{:S(2)}) collective-permute-start(bf16[64,2048]{1,0:T(8,128)(2,1)S(1)} %add_convert_fusion), channel_id=1, source_target_pairs={{0,6},{1,7},{2,0},{3,1},{4,2},{5,3},{6,4},{7,5},{8,14},{9,15},{10,... | collective-permute-start | bytes 786440 | tf_op jit(solution)/shard_map/ppermute | solution.py:482
  93.3 10.0 %collective-permute-start.7 = (bf16[64,2048]{1,0:T(8,128)(2,1)S(1)}, bf16[64,2048]{1,0:T(8,128)(2,1)S(1)}, u32[]{:S(2)}, u32[]{:S(2)}) collective-permute-start(bf16[64,2048]{1,0:T(8,128)(2,1)S(1)} %add_convert_fusion.1), channel_id=1, source_target_pairs={{0,2},{1,3},{2,4},{3,5},{4,6},{5,7},{6,0},{7,1},{8,10},{9,11},{10,... | collective-permute-start | bytes 786440 | tf_op jit(solution)/shard_map/ppermute | solution.py:482
  99.0 14.7 %collective-permute-start.4 = (bf16[32,4096]{1,0:T(8,128)(2,1)S(1)}, bf16[32,4096]{1,0:T(8,128)(2,1)S(1)}, u32[]{:S(2)}, u32[]{:S(2)}) collective-permute-start(bf16[32,4096]{1,0:T(8,128)(2,1)S(1)} %fusion.3), channel_id=1, source_target_pairs={{0,1},{1,0},{2,3},{3,2},{4,5},{5,4},{6,7},{7,6},{8,9},{9,8},{10,11... | collective-permute-start | bytes 786440 | tf_op jit(solution)/shard_map/ppermute | solution.py:486
  103.5 15.3 %collective-permute-start.9 = (bf16[32,4096]{1,0:T(8,128)(2,1)S(1)}, bf16[32,4096]{1,0:T(8,128)(2,1)S(1)}, u32[]{:S(2)}, u32[]{:S(2)}) collective-permute-start(bf16[32,4096]{1,0:T(8,128)(2,1)S(1)} %fusion.4), channel_id=1, source_target_pairs={{0,1},{1,0},{2,3},{3,2},{4,5},{5,4},{6,7},{7,6},{8,9},{9,8},{10,11... | collective-permute-start | bytes 786440 | tf_op jit(solution)/shard_map/ppermute | solution.py:486

commit v5 on v4

--- a/solution.py
+++ b/solution.py
@@ -24,9 +24,9 @@
 SCALE = math.log2(math.e) / math.sqrt(HEAD)
 META_ROW = 4
 CHUNK = 256
-FIRST = 48
+FIRST = 40
 SECOND = 32
-THIRD = 40
+THIRD = 48
 WIDTH = 2048
 WEIGHT_TILE = 1024
 WEIGHT_PARTS = 8
@@ -226,7 +226,7 @@
         in_specs=[SMEM, SMEM, SMEM, HBM, HBM, HBM],
         out_specs=VMEM,
         scratch_shapes=stay_scratch(pool, SECOND),
-        compiler_params=PARAMS,
+        compiler_params=ROOMY,
         cost_estimate=pl.CostEstimate(flops=8 * 10**9, bytes_accessed=8 * 2**20, transcendentals=0),
         name="attend_second",
     )(after, table, lengths, query, fresh, pool)

time: 121 us -> 120 us (level)
  transfers between devices with their start and end apart: 13 -> 13, of which waited for: 7 -> 7; matrix products, arithmetic and copies ran while one was open for 1% -> 1% of each run, Pallas kernels for 30% -> 29%
where the time goes in v5:
time: 120 us; the launch traced here: 119 us
  Pallas kernels  42.4 us (35%)
  starting transfers between devices  39 us (32%)
  waiting for transfers between devices  34.3 us (29%)
  other arithmetic  1.59 us (1%)
  local copies, waits for them, and re-layouts  1.25 us (1%)
    ppermute x8, waiting for transfers between devices, shift_z(): return lax.ppermute(value, 'tensor', pairs)  24.9 us
    pallas_call x1, Pallas kernels, project(): pl.pallas_call(project_kernel, out_shape=[jax.ShapeDtypeStruct((ROWS, 8,...  15.9 us
    ppermute x8, starting transfers between devices, shift_z(): return lax.ppermute(value, 'tensor', pairs)  14.8 us
    ppermute x2, waiting for transfers between devices, swap_x(): return lax.ppermute(value, 'tensor', [(t, t ^ 1) for t in range(8)])  9.42 us
    pallas_call x1, Pallas kernels, stay(): pl.pallas_call(stay_kernel, out_shape=(jax.ShapeDtypeStruct((count, 8, 2,...  8.4 us
    all_to_all x1, starting transfers between devices, body(): lax.all_to_all(sending.reshape(REPLICAS, CAP, COPIED, 2, PAGE, HEAD), 're...  7.37 us
    all_to_all x1, starting transfers between devices, body(): lax.all_to_all(answered.reshape(REPLICAS, CAP, 16, HEAD), 'replica', spli...  7.24 us
    pallas_call x1, Pallas kernels, attend_second(): pl.pallas_call(second_kernel, out_shape=jax.ShapeDtypeStruct((SECOND, 8,...  7.17 us
  transfers between devices with their start and end apart: 13, of which 7 were waited for; matrix products, arithmetic and copies ran while one was open for 1% of the time, Pallas kernels for 29%

profile of v5, /device:TPU:10, one launch (start us, length us, event | category | flops | bytes accessed | tf_op | source)
XLA Modules:
  0.0 119.4 jit_solution(8892662858310156065)
XLA Ops:
  0.6 2.0 %pack_requests.1 = (bf16[32,32,128]{2,1,0:T(8,128)(2,1)}, s32[14]{0:T(128)}) custom-call(s32[1,14]{1,0:T(1,128)} %bitcast.62, s32[14,1,16]{2,1,0:T(1,128)} %bitcast.61, s32[16,128]{1,0:T(8,128)} %bitcast.47, s32[1,128]{1,0:T(1,128)} %length_ref.7, bf16[128,8,2,128]{3,2,1,0:T(2,128)(2,1)} %bitcast.37, bf16[128,2,2,128]{3,2,1,0:T(2,128)(2,1)} %bitcast.42), custom_call_target="tpu_custom_call" | custom-call | tf_op jit(solution)/shard_map/pack_requests/pallas_call | solution.py:366
  2.6 6.5 %all-to-all-start = ((bf16[16,2,32,128]{3,2,1,0:T(8,128)(2,1)}), bf16[16,2,32,128]{3,2,1,0:T(8,128)(2,1)S(1)}, u32[]{:S(2)}, u32[]{:S(2)}) async-start(bf16[16,2,32,128]{3,2,1,0:T(8,128)(2,1)} %bitcast.60), calls=%async_computation | async-start | bytes 524288 | tf_op jit(solution)/shard_map/all_to_all | solution.py:520
  9.1 8.4 %attend_first.1 = (bf16[40,8,2,128]{3,2,1,0:T(2,128)(2,1)}, f32[8,128]{1,0:T(8,128)S(1)}) custom-call(s32[16,128]{1,0:T(8,128)} %bitcast.48, s32[1,128]{1,0:T(1,128)} %length_ref.7, bf16[128,8,2,128]{3,2,1,0:T(2,128)(2,1)} %bitcast.38, bf16[128,2,2,128]{3,2,1,0:T(2,128)(2,1)} %bitcast.43, bf16[2,128,64,128]{3,2,1,0:T(8,128)(2,1)} %bitcast.51), custom_call_target="tpu_custom_call" | custom-call | flops 8000000000 | bytes 8388608 | tf_op jit(solution)/shard_map/attend_first/pallas_call | solution.py:196
  17.5 0.0 all-to-all-done
  17.5 0.0 copy-start
  17.6 0.0 copy-start.1
  17.6 0.0 copy-start.3
  17.6 0.0 copy-start.5
  17.6 5.4 %serve_requests.1 = (bf16[32,16,128]{2,1,0:T(8,128)(2,1)}, bf16[32,4,2,64,128]{4,3,2,1,0:T(8,128)(2,1)}, s32[1]{0:T(128)}) custom-call(bf16[32,32,128]{2,1,0:T(8,128)(2,1)S(1)} %bitcast.46, f32[8,128]{1,0:T(8,128)S(1)} %get-tuple-element.28.after_ref, bf16[2,128,64,128]{3,2,1,0:T(8,128)(2,1)} %bitcast.52), custom_call_target="tpu_custom_call" | custom-call | flops 6000000000 | bytes 8388608 | tf_op jit(solution)/shard_map/serve_requests/pallas_call | solution.py:425
  23.0 7.2 %all-to-all-start.1 = ((bf16[16,2,16,128]{3,2,1,0:T(8,128)(2,1)}), bf16[16,2,16,128]{3,2,1,0:T(8,128)(2,1)S(1)}, u32[]{:S(2)}, u32[]{:S(2)}) async-start(bf16[16,2,16,128]{3,2,1,0:T(8,128)(2,1)} %bitcast.12), calls=%async_computation.1 | async-start | bytes 262144 | tf_op jit(solution)/shard_map/all_to_all | solution.py:526
  30.2 0.0 copy-done
  30.2 7.2 %attend_second.1.second_ref = bf16[32,8,2,128]{3,2,1,0:T(2,128)(2,1)S(1)} custom-call(s32[1]{0:T(128)} %get-tuple-element.29.after_ref, s32[16,128]{1,0:T(8,128)S(1)} %bitcast.49, s32[1,128]{1,0:T(1,128)S(1)} %copy-done.5, bf16[128,8,2,128]{3,2,1,0:T(2,128)(2,1)S(1)} %bitcast.40, bf16[128,2,2,128]{3,2,1,0:T(2,128)(2,1)S(1)} %bitcast.44, ...), custom_call_target="tpu_custom_call" | custom-call | flops 8000000000 | bytes 8388608 | tf_op jit(solution)/shard_map/attend_second/pallas_call | solution.py:223
  37.4 0.0 all-to-all-done.1
  37.4 0.0 copy-start.2
  37.5 7.4 %all-to-all-start.2 = ((bf16[16,2,4,2,64,128]{5,4,3,2,1,0:T(8,128)(2,1)}), bf16[16,2,4,2,64,128]{5,4,3,2,1,0:T(8,128)(2,1)}, u32[]{:S(2)}, u32[]{:S(2)}) async-start(bf16[16,2,4,2,64,128]{5,4,3,2,1,0:T(8,128)(2,1)} %bitcast.55), calls=%async_computation.2 | async-start | bytes 8388608 | tf_op jit(solution)/shard_map/all_to_all | solution.py:529
  44.8 15.9 %attend_third_project.1 = (bf16[128,8,2,128]{3,2,1,0:T(2,128)(2,1)}, bf16[64,4096]{1,0:T(8,128)(2,1)}, bf16[128,2048]{1,0:T(8,128)(2,1)}, bf16[128,2048]{1,0:T(8...) custom-call(s32[14]{0:T(128)S(1)} %copy-done.4, ...), custom_call_target="tpu_custom_call" | custom-call | flops 1000000000 | bytes 1048576 | tf_op jit(solution)/shard_map/attend_third_project/pallas_call | solution.py:292
  60.7 4.1 %collective-permute-start = (bf16[128,2048]{1,0:T(8,128)(2,1)}, bf16[128,2048]{1,0:T(8,128)(2,1)S(1)}, u32[]{:S(2)}, u32[]{:S(2)}) collective-permute-start(bf16[128,2048]{1,0:T(8,128)(2,1)} %get-tuple-element.33), channel_id=1, source_target_pairs={{0,6},{1,7},{2,0},{3,1},{4,2},{5,3},{6,4},{7,5},{8,14},{9,15},{10,... | collective-permute-start | bytes 1572872 | tf_op jit(solution)/shard_map/ppermute | solution.py:482
  64.8 0.0 collective-permute-start.1
  64.8 3.2 %collective-permute-start.5 = (bf16[128,2048]{1,0:T(8,128)(2,1)}, bf16[128,2048]{1,0:T(8,128)(2,1)S(1)}, u32[]{:S(2)}, u32[]{:S(2)}) collective-permute-start(bf16[128,2048]{1,0:T(8,128)(2,1)} %get-tuple-element.40), channel_id=1, source_target_pairs={{0,6},{1,7},{2,0},{3,1},{4,2},{5,3},{6,4},{7,5},{8,14},{9,15},{10,... | collective-permute-start | bytes 1572872 | tf_op jit(solution)/shard_map/ppermute | solution.py:482
  68.1 0.0 collective-permute-start.6
  68.1 9.3 %collective-permute-done = bf16[128,2048]{1,0:T(8,128)(2,1)S(1)} collective-permute-done((bf16[128,2048]{1,0:T(8,128)(2,1)}, bf16[128,2048]{1,0:T(8,128)(2,1)S(1)}, u32[]{:S(2)}, u32[]{:S(2)}) %collective-permute-start) | collective-permute-done | bytes 524320 | tf_op jit(solution)/shard_map/ppermute | solution.py:482
  77.4 0.1 add_convert_fusion.2
  77.5 3.7 %collective-permute-start.3 = (bf16[64,2048]{1,0:T(8,128)(2,1)S(1)}, bf16[64,2048]{1,0:T(8,128)(2,1)S(1)}, u32[]{:S(2)}, u32[]{:S(2)}) collective-permute-start(bf16[64,2048]{1,0:T(8,128)(2,1)S(1)} %add_convert_fusion.2), channel_id=1, source_target_pairs={{0,6},{1,7},{2,0},{3,1},{4,2},{5,3},{6,4},{7,5},{8,14},{9,15},{10,... | collective-permute-start | bytes 786440 | tf_op jit(solution)/shard_map/ppermute | solution.py:482
  81.1 0.0 collective-permute-done.1
  81.1 0.1 add_convert_fusion.3
  81.2 0.1 collective-permute-start.2
  81.3 7.4 %collective-permute-done.5 = bf16[128,2048]{1,0:T(8,128)(2,1)S(1)} collective-permute-done((bf16[128,2048]{1,0:T(8,128)(2,1)}, bf16[128,2048]{1,0:T(8,128)(2,1)S(1)}, u32[]{:S(2)}, u32[]{:S(2)}) %collective-permute-start.5) | collective-permute-done | bytes 524320 | tf_op jit(solution)/shard_map/ppermute | solution.py:482
  88.6 0.1 add_convert_fusion
  88.7 3.7 %collective-permute-start.8 = (bf16[64,2048]{1,0:T(8,128)(2,1)S(1)}, bf16[64,2048]{1,0:T(8,128)(2,1)S(1)}, u32[]{:S(2)}, u32[]{:S(2)}) collective-permute-start(bf16[64,2048]{1,0:T(8,128)(2,1)S(1)} %add_convert_fusion), channel_id=1, source_target_pairs={{0,6},{1,7},{2,0},{3,1},{4,2},{5,3},{6,4},{7,5},{8,14},{9,15},{10,... | collective-permute-start | bytes 786440 | tf_op jit(solution)/shard_map/ppermute | solution.py:482
  92.4 0.0 collective-permute-done.6
  92.4 0.1 add_convert_fusion.1
  92.4 0.1 collective-permute-start.7
  92.5 1.6 %collective-permute-done.3 = bf16[64,2048]{1,0:T(8,128)(2,1)S(1)} collective-permute-done((bf16[64,2048]{1,0:T(8,128)(2,1)S(1)}, bf16[64,2048]{1,0:T(8,128)(2,1)S(1)}, u32[]{:S(2)}, u32[]{:S(2)}) %collective-permute-start.3) | collective-permute-done | bytes 262176 | tf_op jit(solution)/shard_map/ppermute | solution.py:482
  94.1 3.7 %collective-permute-done.2 = bf16[64,2048]{1,0:T(8,128)(2,1)S(1)} collective-permute-done((bf16[64,2048]{1,0:T(8,128)(2,1)S(1)}, bf16[64,2048]{1,0:T(8,128)(2,1)S(1)}, u32[]{:S(2)}, u32[]{:S(2)}) %collective-permute-start.2) | collective-permute-done | bytes 262176 | tf_op jit(solution)/shard_map/ppermute | solution.py:482
  97.9 0.2 convert_add_fusion.3
  98.1 0.1 pad_maximum_fusion
  98.2 1.5 %collective-permute-start.4 = (bf16[32,4096]{1,0:T(8,128)(2,1)S(1)}, bf16[32,4096]{1,0:T(8,128)(2,1)S(1)}, u32[]{:S(2)}, u32[]{:S(2)}) collective-permute-start(bf16[32,4096]{1,0:T(8,128)(2,1)S(1)} %fusion.3), channel_id=1, source_target_pairs={{0,1},{1,0},{2,3},{3,2},{4,5},{5,4},{6,7},{7,6},{8,9},{9,8},{10,11... | collective-permute-start | bytes 786440 | tf_op jit(solution)/shard_map/ppermute | solution.py:486
  99.7 0.0 collective-permute-done.8
  99.7 2.8 %collective-permute-done.7 = bf16[64,2048]{1,0:T(8,128)(2,1)S(1)} collective-permute-done((bf16[64,2048]{1,0:T(8,128)(2,1)S(1)}, bf16[64,2048]{1,0:T(8,128)(2,1)S(1)}, u32[]{:S(2)}, u32[]{:S(2)}) %collective-permute-start.7) | collective-permute-done | bytes 262176 | tf_op jit(solution)/shard_map/ppermute | solution.py:482
  102.5 0.2 convert_add_fusion.1
  102.8 0.1 pad_maximum_fusion.1
  102.9 1.5 %collective-permute-start.9 = (bf16[32,4096]{1,0:T(8,128)(2,1)S(1)}, bf16[32,4096]{1,0:T(8,128)(2,1)S(1)}, u32[]{:S(2)}, u32[]{:S(2)}) collective-permute-start(bf16[32,4096]{1,0:T(8,128)(2,1)S(1)} %fusion.4), channel_id=1, source_target_pairs={{0,1},{1,0},{2,3},{3,2},{4,5},{5,4},{6,7},{7,6},{8,9},{9,8},{10,11... | collective-permute-start | bytes 786440 | tf_op jit(solution)/shard_map/ppermute | solution.py:486
  104.4 8.0 %collective-permute-done.4 = bf16[32,4096]{1,0:T(8,128)(2,1)S(1)} collective-permute-done((bf16[32,4096]{1,0:T(8,128)(2,1)S(1)}, bf16[32,4096]{1,0:T(8,128)(2,1)S(1)}, u32[]{:S(2)}, u32[]{:S(2)}) %collective-permute-start.4) | collective-permute-done | bytes 262176 | tf_op jit(solution)/shard_map/ppermute | solution.py:486
  112.4 0.0 all-to-all-done.2
  112.4 3.6 %pick_pages.1 = (bf16[14,4,2,64,128]{4,3,2,1,0:T(8,128)(2,1)}, f32[1]{0:T(128)}) custom-call(s32[14]{0:T(128)} %get-tuple-element.25.slot_ref, bf16[32,4,2,64,128]{4,3,2,1,0:T(8,128)(2,1)} %bitcast.23.got_ref), custom_call_target="tpu_custom_call" | custom-call | tf_op jit(solution)/shard_map/pick_pages/pallas_call | solution.py:465
  116.1 1.4 %collective-permute-done.9 = bf16[32,4096]{1,0:T(8,128)(2,1)S(1)} collective-permute-done((bf16[32,4096]{1,0:T(8,128)(2,1)S(1)}, bf16[32,4096]{1,0:T(8,128)(2,1)S(1)}, u32[]{:S(2)}, u32[]{:S(2)}) %collective-permute-start.9) | collective-permute-done | bytes 262176 | tf_op jit(solution)/shard_map/ppermute | solution.py:486
  117.5 0.7 fusion.1
  118.3 1.1 broadcast_in_dim_reshape.7
  (15 shorter events, 0.2 us)
Async XLA Ops:
  2.6 14.9 %all-to-all-start = ((bf16[16,2,32,128]{3,2,1,0:T(8,128)(2,1)}), bf16[16,2,32,128]{3,2,1,0:T(8,128)(2,1)S(1)}, u32[]{:S(2)}, u32[]{:S(2)}) async-start(bf16[16,2,32,128]{3,2,1,0:T(8,128)(2,1)} %bitcast.60), calls=%async_computation | async-start | bytes 524288 | tf_op jit(solution)/shard_map/all_to_all | solution.py:520
  17.5 12.7 %copy-start = (bf16[1,128,2,1024]{3,2,1,0:T(2,128)(2,1)S(1)}, bf16[1,128,2,1024]{3,2,1,0:T(2,128)(2,1)}, u32[]{:S(2)}) copy-start(bf16[1,128,2,1024]{3,2,1,0:T(2,128)(2,1)} %param.8) | copy-start | bytes 1572868
  17.6 12.7 %copy-start.1 = (bf16[1,128,2,2,128]{4,3,2,1,0:T(2,128)(2,1)S(1)}, bf16[1,128,2,2,128]{4,3,2,1,0:T(2,128)(2,1)}, u32[]{:S(2)}) copy-start(bf16[1,128,2,2,128]{4,3,2,1,0:T(2,128)(2,1)} %param.9) | copy-start | bytes 393220
  17.6 12.7 %copy-start.3 = (s32[1,128,16]{1,2,0:T(8,128)S(1)}, s32[1,128,16]{1,2,0:T(8,128)}, u32[]{:S(2)}) copy-start(s32[1,128,16]{1,2,0:T(8,128)} %param.11) | copy-start | bytes 24580
  17.6 12.7 %copy-start.5 = (s32[1,128]{1,0:T(1,128)S(1)}, s32[1,128]{1,0:T(1,128)}, u32[]{:S(2)}) copy-start(s32[1,128]{1,0:T(1,128)} %length_ref.7) | copy-start | bytes 1540
  23.0 14.5 %all-to-all-start.1 = ((bf16[16,2,16,128]{3,2,1,0:T(8,128)(2,1)}), bf16[16,2,16,128]{3,2,1,0:T(8,128)(2,1)S(1)}, u32[]{:S(2)}, u32[]{:S(2)}) async-start(bf16[16,2,16,128]{3,2,1,0:T(8,128)(2,1)} %bitcast.12), calls=%async_computation.1 | async-start | bytes 262144 | tf_op jit(solution)/shard_map/all_to_all | solution.py:526
  37.4 7.4 %copy-start.2 = (bf16[40,8,2,128]{3,2,1,0:T(2,128)(2,1)S(1)}, bf16[40,8,2,128]{3,2,1,0:T(2,128)(2,1)}, u32[]{:S(2)}) copy-start(bf16[40,8,2,128]{3,2,1,0:T(2,128)(2,1)} %get-tuple-element.26.first_ref) | copy-start | bytes 491524
  37.4 7.4 %copy-start.4 = (s32[14]{0:T(128)S(1)}, s32[14]{0:T(128)}, u32[]{:S(2)}) copy-start(s32[14]{0:T(128)} %get-tuple-element.25.slot_ref) | copy-start | bytes 172
  37.5 75.0 %all-to-all-start.2 = ((bf16[16,2,4,2,64,128]{5,4,3,2,1,0:T(8,128)(2,1)}), bf16[16,2,4,2,64,128]{5,4,3,2,1,0:T(8,128)(2,1)}, u32[]{:S(2)}, u32[]{:S(2)}) async-start(bf16[16,2,4,2,64,128]{5,4,3,2,1,0:T(8,128)(2,1)} %bitcast.55), calls=%async_computation.2 | async-start | bytes 8388608 | tf_op jit(solution)/shard_map/all_to_all | solution.py:529
  60.7 16.7 %collective-permute-start = (bf16[128,2048]{1,0:T(8,128)(2,1)}, bf16[128,2048]{1,0:T(8,128)(2,1)S(1)}, u32[]{:S(2)}, u32[]{:S(2)}) collective-permute-start(bf16[128,2048]{1,0:T(8,128)(2,1)} %get-tuple-element.33), channel_id=1, source_target_pairs={{0,6},{1,7},{2,0},{3,1},{4,2},{5,3},{6,4},{7,5},{8,14},{9,15},{10,... | collective-permute-start | bytes 1572872 | tf_op jit(solution)/shard_map/ppermute | solution.py:482
  64.8 16.3 %collective-permute-start.1 = (bf16[128,2048]{1,0:T(8,128)(2,1)}, bf16[128,2048]{1,0:T(8,128)(2,1)S(1)}, u32[]{:S(2)}, u32[]{:S(2)}) collective-permute-start(bf16[128,2048]{1,0:T(8,128)(2,1)} %get-tuple-element.35), channel_id=1, source_target_pairs={{0,2},{1,3},{2,4},{3,5},{4,6},{5,7},{6,0},{7,1},{8,10},{9,11},{10,... | collective-permute-start | bytes 1572872 | tf_op jit(solution)/shard_map/ppermute | solution.py:482
  64.8 33.1 %copy-start.7 = (bf16[64,4096]{1,0:T(8,128)(2,1)S(1)}, bf16[64,4096]{1,0:T(8,128)(2,1)}, u32[]{:S(2)}) copy-start(bf16[64,4096]{1,0:T(8,128)(2,1)} %get-tuple-element.32) | copy-start | bytes 1572868
  64.8 23.8 %collective-permute-start.5 = (bf16[128,2048]{1,0:T(8,128)(2,1)}, bf16[128,2048]{1,0:T(8,128)(2,1)S(1)}, u32[]{:S(2)}, u32[]{:S(2)}) collective-permute-start(bf16[128,2048]{1,0:T(8,128)(2,1)} %get-tuple-element.40), channel_id=1, source_target_pairs={{0,6},{1,7},{2,0},{3,1},{4,2},{5,3},{6,4},{7,5},{8,14},{9,15},{10,... | collective-permute-start | bytes 1572872 | tf_op jit(solution)/shard_map/ppermute | solution.py:482
  68.1 24.3 %collective-permute-start.6 = (bf16[128,2048]{1,0:T(8,128)(2,1)}, bf16[128,2048]{1,0:T(8,128)(2,1)S(1)}, u32[]{:S(2)}, u32[]{:S(2)}) collective-permute-start(bf16[128,2048]{1,0:T(8,128)(2,1)} %get-tuple-element.42), channel_id=1, source_target_pairs={{0,2},{1,3},{2,4},{3,5},{4,6},{5,7},{6,0},{7,1},{8,10},{9,11},{10,... | collective-permute-start | bytes 1572872 | tf_op jit(solution)/shard_map/ppermute | solution.py:482
  77.4 25.2 %copy-start.6 = (bf16[64,4096]{1,0:T(8,128)(2,1)S(1)}, bf16[64,4096]{1,0:T(8,128)(2,1)}, u32[]{:S(2)}) copy-start(bf16[64,4096]{1,0:T(8,128)(2,1)} %get-tuple-element.37) | copy-start | bytes 1572868
  77.5 16.7 %collective-permute-start.3 = (bf16[64,2048]{1,0:T(8,128)(2,1)S(1)}, bf16[64,2048]{1,0:T(8,128)(2,1)S(1)}, u32[]{:S(2)}, u32[]{:S(2)}) collective-permute-start(bf16[64,2048]{1,0:T(8,128)(2,1)S(1)} %add_convert_fusion.2), channel_id=1, source_target_pairs={{0,6},{1,7},{2,0},{3,1},{4,2},{5,3},{6,4},{7,5},{8,14},{9,15},{10,... | collective-permute-start | bytes 786440 | tf_op jit(solution)/shard_map/ppermute | solution.py:482
  81.2 16.7 %collective-permute-start.2 = (bf16[64,2048]{1,0:T(8,128)(2,1)S(1)}, bf16[64,2048]{1,0:T(8,128)(2,1)S(1)}, u32[]{:S(2)}, u32[]{:S(2)}) collective-permute-start(bf16[64,2048]{1,0:T(8,128)(2,1)S(1)} %add_convert_fusion.3), channel_id=1, source_target_pairs={{0,2},{1,3},{2,4},{3,5},{4,6},{5,7},{6,0},{7,1},{8,10},{9,11},{10,... | collective-permute-start | bytes 786440 | tf_op jit(solution)/shard_map/ppermute | solution.py:482
  88.7 11.0 %collective-permute-start.8 = (bf16[64,2048]{1,0:T(8,128)(2,1)S(1)}, bf16[64,2048]{1,0:T(8,128)(2,1)S(1)}, u32[]{:S(2)}, u32[]{:S(2)}) collective-permute-start(bf16[64,2048]{1,0:T(8,128)(2,1)S(1)} %add_convert_fusion), channel_id=1, source_target_pairs={{0,6},{1,7},{2,0},{3,1},{4,2},{5,3},{6,4},{7,5},{8,14},{9,15},{10,... | collective-permute-start | bytes 786440 | tf_op jit(solution)/shard_map/ppermute | solution.py:482
  92.4 10.1 %collective-permute-start.7 = (bf16[64,2048]{1,0:T(8,128)(2,1)S(1)}, bf16[64,2048]{1,0:T(8,128)(2,1)S(1)}, u32[]{:S(2)}, u32[]{:S(2)}) collective-permute-start(bf16[64,2048]{1,0:T(8,128)(2,1)S(1)} %add_convert_fusion.1), channel_id=1, source_target_pairs={{0,2},{1,3},{2,4},{3,5},{4,6},{5,7},{6,0},{7,1},{8,10},{9,11},{10,... | collective-permute-start | bytes 786440 | tf_op jit(solution)/shard_map/ppermute | solution.py:482
  98.2 14.2 %collective-permute-start.4 = (bf16[32,4096]{1,0:T(8,128)(2,1)S(1)}, bf16[32,4096]{1,0:T(8,128)(2,1)S(1)}, u32[]{:S(2)}, u32[]{:S(2)}) collective-permute-start(bf16[32,4096]{1,0:T(8,128)(2,1)S(1)} %fusion.3), channel_id=1, source_target_pairs={{0,1},{1,0},{2,3},{3,2},{4,5},{5,4},{6,7},{7,6},{8,9},{9,8},{10,11... | collective-permute-start | bytes 786440 | tf_op jit(solution)/shard_map/ppermute | solution.py:486
  102.9 14.6 %collective-permute-start.9 = (bf16[32,4096]{1,0:T(8,128)(2,1)S(1)}, bf16[32,4096]{1,0:T(8,128)(2,1)S(1)}, u32[]{:S(2)}, u32[]{:S(2)}) collective-permute-start(bf16[32,4096]{1,0:T(8,128)(2,1)S(1)} %fusion.4), channel_id=1, source_target_pairs={{0,1},{1,0},{2,3},{3,2},{4,5},{5,4},{6,7},{7,6},{8,9},{9,8},{10,11... | collective-permute-start | bytes 786440 | tf_op jit(solution)/shard_map/ppermute | solution.py:486
